TPU v7x, 32 devices: a whole 2x2x4 slice. The times are simulated.
32 devices in a mesh: dp: 8 (over z, y), blk: 4 (over x, core).
Axes of the slice: x: 2, y: 2, z: 4, core: 2. Of those that a mesh axis runs over, the one named last changes fastest.
Arguments:
- patches: bfloat16 [4096, 1024], P(('dp', 'blk')), may hold values from -6 to 6
- lengths: int32 [8, 8], P('dp'), may hold values from 1 to 385, 512 in all within a row
- gsd_scale: float32 [8, 8], P('dp'), may hold values from 0.5 to 4
- visible: int32 [8, 512], P('dp'), may hold values from 0 to 1, as said below
- encoder_gain_first: bfloat16 [1024], P('dp'), may hold values from 0.5 to 1.5
- encoder_bias_first: bfloat16 [1024], P('dp'), may hold values from -1 to 1
- encoder_query: bfloat16 [1024, 1024], P('dp'), may hold values from -0.1875 to 0.1875
- encoder_key: bfloat16 [1024, 1024], P('dp'), may hold values from -0.1875 to 0.1875
- encoder_value: bfloat16 [1024, 1024], P('dp'), may hold values from -0.1875 to 0.1875
- encoder_output: bfloat16 [1024, 1024], P('dp'), may hold values from -0.5 to 0.5
- encoder_gain_second: bfloat16 [1024], P('dp'), may hold values from 0.5 to 1.5
- encoder_bias_second: bfloat16 [1024], P('dp'), may hold values from -1 to 1
- encoder_up: bfloat16 [1024, 4096], P('dp'), may hold values from -0.1875 to 0.1875
- encoder_down: bfloat16 [4096, 1024], P('dp'), may hold values from -0.09375 to 0.09375
- embed_proj: bfloat16 [1024, 512], P('dp'), may hold values from -0.1875 to 0.1875
- mask_token: bfloat16 [512], P('dp'), may hold values from -6 to 6
- decoder_gain_first: bfloat16 [512], P('dp'), may hold values from 0.5 to 1.5
- decoder_bias_first: bfloat16 [512], P('dp'), may hold values from -1 to 1
- decoder_query: bfloat16 [512, 512], P('dp'), may hold values from -0.25 to 0.25
- decoder_key: bfloat16 [512, 512], P('dp'), may hold values from -0.25 to 0.25
- decoder_value: bfloat16 [512, 512], P('dp'), may hold values from -0.25 to 0.25
- decoder_output: bfloat16 [512, 512], P('dp'), may hold values from -1 to 1
- decoder_gain_second: bfloat16 [512], P('dp'), may hold values from 0.5 to 1.5
- decoder_bias_second: bfloat16 [512], P('dp'), may hold values from -1 to 1
- decoder_up: bfloat16 [512, 2048], P('dp'), may hold values from -0.25 to 0.25
- decoder_down: bfloat16 [2048, 512], P('dp'), may hold values from -0.125 to 0.125
- cotangent: bfloat16 [4096, 512], P(('dp', 'blk')), may hold values from -6 to 6
Outputs:
- decoded_rows: bfloat16 [4096, 512], P(('dp', 'blk'))
- grad_patches: float32 [4096, 1024], P(('dp', 'blk'))
- grad_encoder_gain_first: float32 [1024], P('dp')
- grad_encoder_bias_first: float32 [1024], P('dp')
- grad_encoder_query: float32 [1024, 1024], P('dp')
- grad_encoder_key: float32 [1024, 1024], P('dp')
- grad_encoder_value: float32 [1024, 1024], P('dp')
- grad_encoder_output: float32 [1024, 1024], P('dp')
- grad_encoder_gain_second: float32 [1024], P('dp')
- grad_encoder_bias_second: float32 [1024], P('dp')
- grad_encoder_up: float32 [1024, 4096], P('dp')
- grad_encoder_down: float32 [4096, 1024], P('dp')
- grad_embed_proj: float32 [1024, 512], P('dp')
- grad_mask_token: float32 [512], P('dp')
- grad_decoder_gain_first: float32 [512], P('dp')
- grad_decoder_bias_first: float32 [512], P('dp')
- grad_decoder_query: float32 [512, 512], P('dp')
- grad_decoder_key: float32 [512, 512], P('dp')
- grad_decoder_value: float32 [512, 512], P('dp')
- grad_decoder_output: float32 [512, 512], P('dp')
- grad_decoder_gain_second: float32 [512], P('dp')
- grad_decoder_bias_second: float32 [512], P('dp')
- grad_decoder_up: float32 [512, 2048], P('dp')
- grad_decoder_down: float32 [2048, 512], P('dp')
Inputs may be any that keep to these rules, and one draw needn't show every extreme that they name: `lengths`: each row lists the patch counts of the 8 images of one group in order; they sum to 512 and the largest is 385. `visible`: each row (one group) has exactly 128 ones, placed anywhere among its 512 patches.
All inputs are finite; a program needn't handle non-finite values.
Results may differ from a plain program's by a relative error of at most 0.023.
Values may be sent and summed in bfloat16 or wider, within the bound.
A program may use at most 384 MiB of HBM per device.

v0:
```python
import math

import jax
import jax.numpy as jnp
from jax import lax
from jax.sharding import PartitionSpec as P

HEADS = 16
DEC_HEADS = 16


EPSILON = 1e-06
MASKED_SCORE = -1e30


def layer_norm(values, gain, shift):
    center = values - jnp.mean(values, axis=-1, keepdims=True)
    spread = jnp.mean(center * center, axis=-1, keepdims=True)
    return center * lax.rsqrt(spread + EPSILON) * gain + shift


def sincos(scaled, width):
    half_width = width // 2
    frequency = jnp.exp(
        jnp.arange(half_width, dtype=jnp.float32) * (-math.log(10000.0) / half_width)
    )
    angles = scaled[:, None] * frequency[None, :]
    return jnp.concatenate([jnp.sin(angles), jnp.cos(angles)], axis=1)


def image_layout(lengths_row, gsd_row, positions):
    image_ends = jnp.cumsum(lengths_row)
    image_starts = image_ends - lengths_row
    image_ids = jnp.sum((positions[:, None] >= image_ends[None, :]).astype(jnp.int32), axis=1)
    onehot = image_ids[:, None] == jnp.arange(lengths_row.shape[0], dtype=jnp.int32)[None, :]
    first_row = jnp.sum(jnp.where(onehot, image_starts[None, :], 0), axis=1)
    gsd_ratio = jnp.sum(jnp.where(onehot, gsd_row[None, :], 0.0), axis=1)
    return (image_ids, (positions - first_row).astype(jnp.float32) * gsd_ratio)


def product(left, right):
    return jnp.dot(left, right, preferred_element_type=jnp.float32)


def trans_product(left, right):
    return lax.dot_general(
        left, right, (((0,), (0,)), ((), ())), preferred_element_type=jnp.float32
    )


def back_product(left, right):
    return lax.dot_general(
        left, right, (((1,), (1,)), ((), ())), preferred_element_type=jnp.float32
    )


def split_heads(matrix, heads):
    row_count = matrix.shape[0]
    return matrix.reshape(row_count, heads // 2, 2, -1).transpose(1, 2, 0, 3)


def merge_heads(blocks):
    row_count = blocks.shape[2]
    return blocks.transpose(2, 0, 1, 3).reshape(row_count, -1)


def attend_forward(queries, key_rows, values, allowed, heads):
    scaling = 1.0 / math.sqrt(queries.shape[1] // heads)

    def per_pair(group_item):
        query_part, key_part, value_part = group_item
        scores = (
            jnp.einsum("hid,hjd->hij", query_part, key_part, preferred_element_type=jnp.float32)
            * scaling
        )
        scores = jnp.where(allowed[None], scores, MASKED_SCORE)
        largest = jnp.max(scores, axis=-1, keepdims=True)
        exponent = jnp.exp(scores - largest)
        totals = jnp.sum(exponent, axis=-1, keepdims=True)
        softmaxed = (exponent / totals).astype(jnp.bfloat16)
        mixture = jnp.einsum(
            "hij,hjd->hid", softmaxed, value_part, preferred_element_type=jnp.float32
        )
        return (mixture.astype(jnp.bfloat16), (largest + jnp.log(totals))[..., 0])

    mixture, log_totals = lax.map(
        per_pair,
        (split_heads(queries, heads), split_heads(key_rows, heads), split_heads(values, heads)),
    )
    return (merge_heads(mixture), log_totals)


def attend_backward(queries, key_rows, values, allowed, heads, log_totals, grad_mixture):
    scaling = 1.0 / math.sqrt(queries.shape[1] // heads)

    def per_pair(group_item):
        query_part, key_part, value_part, total_part, grad_part = group_item
        scores = (
            jnp.einsum("hid,hjd->hij", query_part, key_part, preferred_element_type=jnp.float32)
            * scaling
        )
        softmaxed = jnp.where(allowed[None], jnp.exp(scores - total_part[..., None]), 0.0)
        rounded = softmaxed.astype(jnp.bfloat16)
        grad_values = jnp.einsum(
            "hij,hid->hjd", rounded, grad_part, preferred_element_type=jnp.float32
        )
        grad_probs = jnp.einsum(
            "hid,hjd->hij", grad_part, value_part, preferred_element_type=jnp.float32
        )
        inner_sum = jnp.sum(softmaxed * grad_probs, axis=-1, keepdims=True)
        grad_scores = (softmaxed * (grad_probs - inner_sum)).astype(jnp.bfloat16)
        grad_queries = (
            jnp.einsum("hij,hjd->hid", grad_scores, key_part, preferred_element_type=jnp.float32)
            * scaling
        )
        grad_keys = (
            jnp.einsum("hij,hid->hjd", grad_scores, query_part, preferred_element_type=jnp.float32)
            * scaling
        )
        return (grad_queries, grad_keys, grad_values)

    grad_queries, grad_keys, grad_values = lax.map(
        per_pair,
        (
            split_heads(queries, heads),
            split_heads(key_rows, heads),
            split_heads(values, heads),
            log_totals,
            split_heads(grad_mixture, heads),
        ),
    )
    return (merge_heads(grad_queries), merge_heads(grad_keys), merge_heads(grad_values))


def block_forward(residual, params, heads, allowed, gather_keys):
    (
        gain_first,
        bias_first,
        query_weight,
        key_weight,
        value_weight,
        output_weight,
        gain_second,
        bias_second,
        up_weight,
        down_weight,
    ) = params
    normed = layer_norm(
        residual, gain_first.astype(jnp.float32), bias_first.astype(jnp.float32)
    ).astype(jnp.bfloat16)
    queries = product(normed, query_weight).astype(jnp.bfloat16)
    own_keys = product(normed, key_weight).astype(jnp.bfloat16)
    own_values = product(normed, value_weight).astype(jnp.bfloat16)
    key_rows, values = gather_keys((own_keys, own_values))
    mixture, log_totals = attend_forward(queries, key_rows, values, allowed, heads)
    middle = residual + product(mixture, output_weight)
    lifted = layer_norm(
        middle, gain_second.astype(jnp.float32), bias_second.astype(jnp.float32)
    ).astype(jnp.bfloat16)
    upper = product(lifted, up_weight)
    hidden = jax.nn.gelu(upper, approximate=False).astype(jnp.bfloat16)
    result = middle + product(hidden, down_weight)
    return (
        result,
        (
            residual,
            normed,
            queries,
            key_rows,
            values,
            mixture,
            log_totals,
            middle,
            lifted,
            upper,
            hidden,
        ),
    )


def block_backward(grad_result, params, heads, allowed, saved, scatter_keys):
    (
        gain_first,
        bias_first,
        query_weight,
        key_weight,
        value_weight,
        output_weight,
        gain_second,
        bias_second,
        up_weight,
        down_weight,
    ) = params
    (
        residual,
        normed,
        queries,
        key_rows,
        values,
        mixture,
        log_totals,
        middle,
        lifted,
        upper,
        hidden,
    ) = saved
    grad_branch = grad_result.astype(jnp.bfloat16)
    grad_down = trans_product(hidden, grad_branch)
    grad_hidden = back_product(grad_branch, down_weight)
    unused, gelu_back = jax.vjp(lambda before: jax.nn.gelu(before, approximate=False), upper)
    grad_upper = gelu_back(grad_hidden)[0].astype(jnp.bfloat16)
    grad_up = trans_product(lifted, grad_upper)
    grad_lifted = back_product(grad_upper, up_weight)
    unused, norm_back = jax.vjp(
        layer_norm, middle, gain_second.astype(jnp.float32), bias_second.astype(jnp.float32)
    )
    grad_norm_in, grad_gain_second, grad_bias_second = norm_back(grad_lifted)
    grad_middle = grad_result + grad_norm_in
    grad_attention = grad_middle.astype(jnp.bfloat16)
    grad_output = trans_product(mixture, grad_attention)
    grad_mixture = back_product(grad_attention, output_weight).astype(jnp.bfloat16)
    grad_queries, key_terms, value_terms = attend_backward(
        queries, key_rows, values, allowed, heads, log_totals, grad_mixture
    )
    grad_keys, grad_values = scatter_keys((key_terms, value_terms))
    grad_queries = grad_queries.astype(jnp.bfloat16)
    grad_keys = grad_keys.astype(jnp.bfloat16)
    grad_values = grad_values.astype(jnp.bfloat16)
    grad_query = trans_product(normed, grad_queries)
    grad_key = trans_product(normed, grad_keys)
    grad_value = trans_product(normed, grad_values)
    grad_normed = (
        back_product(grad_queries, query_weight)
        + back_product(grad_keys, key_weight)
        + back_product(grad_values, value_weight)
    )
    unused, norm_back = jax.vjp(
        layer_norm, residual, gain_first.astype(jnp.float32), bias_first.astype(jnp.float32)
    )
    grad_norm_in, grad_gain_first, grad_bias_first = norm_back(grad_normed)
    gradients = (
        grad_gain_first,
        grad_bias_first,
        grad_query,
        grad_key,
        grad_value,
        grad_output,
        grad_gain_second,
        grad_bias_second,
        grad_up,
        grad_down,
    )
    return (grad_middle + grad_norm_in, gradients)


def reduce_gradients(gradients, dp_count, blk_count):
    packed = jnp.concatenate(
        [gradient.reshape(dp_count, blk_count, -1) for gradient in gradients], axis=2
    )
    summed = lax.psum_scatter(packed.reshape(dp_count, -1), "dp", scatter_dimension=0, tiled=True)
    summed = lax.psum(summed.astype(jnp.bfloat16), "blk").astype(jnp.float32).reshape(blk_count, -1)
    pieces = []
    column = 0
    for gradient in gradients:
        columns = gradient.size // (dp_count * blk_count)
        local_shape = (gradient.shape[0] // dp_count,) + gradient.shape[1:]
        pieces.append(summed[:, column : column + columns].reshape(local_shape))
        column = column + columns
    return tuple(pieces)


def local(
    patches,
    lengths,
    gsd_scale,
    visible,
    encoder_gain_first,
    encoder_bias_first,
    encoder_query,
    encoder_key,
    encoder_value,
    encoder_output,
    encoder_gain_second,
    encoder_bias_second,
    encoder_up,
    encoder_down,
    embed_proj,
    mask_token,
    decoder_gain_first,
    decoder_bias_first,
    decoder_query,
    decoder_key,
    decoder_value,
    decoder_output,
    decoder_gain_second,
    decoder_bias_second,
    decoder_up,
    decoder_down,
    cotangent,
):
    row_count = patches.shape[0]
    dp_count = lax.axis_size("dp")
    blk_count = lax.axis_size("blk")
    offset = lax.axis_index("blk") * row_count
    group_rows = jnp.arange(row_count * blk_count, dtype=jnp.int32)
    own_rows = offset + jnp.arange(row_count, dtype=jnp.int32)
    image_ids, scaled = image_layout(lengths[0], gsd_scale[0], group_rows)
    own_images = lax.dynamic_slice_in_dim(image_ids, offset, row_count)
    own_scaled = lax.dynamic_slice_in_dim(scaled, offset, row_count)
    shown_keys = visible[0] > 0
    shown_rows = lax.dynamic_slice_in_dim(visible[0], offset, row_count) > 0
    same_image = own_images[:, None] == image_ids[None, :]
    allowed = same_image & (shown_keys[None, :] | (own_rows[:, None] == group_rows[None, :]))
    encoder_full = (
        lax.all_gather(encoder_gain_first, "dp", axis=0, tiled=True),
        lax.all_gather(encoder_bias_first, "dp", axis=0, tiled=True),
        lax.all_gather(encoder_query, "dp", axis=0, tiled=True),
        lax.all_gather(encoder_key, "dp", axis=0, tiled=True),
        lax.all_gather(encoder_value, "dp", axis=0, tiled=True),
        lax.all_gather(encoder_output, "dp", axis=0, tiled=True),
        lax.all_gather(encoder_gain_second, "dp", axis=0, tiled=True),
        lax.all_gather(encoder_bias_second, "dp", axis=0, tiled=True),
        lax.all_gather(encoder_up, "dp", axis=0, tiled=True),
        lax.all_gather(encoder_down, "dp", axis=0, tiled=True),
    )
    residual = patches.astype(jnp.float32) + sincos(own_scaled, patches.shape[1])
    encoded, encoder_saved = block_forward(
        residual,
        encoder_full,
        HEADS,
        allowed,
        lambda key_value: (
            lax.all_gather(key_value[0], "blk", axis=0, tiled=True),
            lax.all_gather(key_value[1], "blk", axis=0, tiled=True),
        ),
    )
    decoder_full = (
        lax.all_gather(embed_proj, "dp", axis=0, tiled=True),
        lax.all_gather(mask_token, "dp", axis=0, tiled=True),
        lax.all_gather(decoder_gain_first, "dp", axis=0, tiled=True),
        lax.all_gather(decoder_bias_first, "dp", axis=0, tiled=True),
        lax.all_gather(decoder_query, "dp", axis=0, tiled=True),
        lax.all_gather(decoder_key, "dp", axis=0, tiled=True),
        lax.all_gather(decoder_value, "dp", axis=0, tiled=True),
        lax.all_gather(decoder_output, "dp", axis=0, tiled=True),
        lax.all_gather(decoder_gain_second, "dp", axis=0, tiled=True),
        lax.all_gather(decoder_bias_second, "dp", axis=0, tiled=True),
        lax.all_gather(decoder_up, "dp", axis=0, tiled=True),
        lax.all_gather(decoder_down, "dp", axis=0, tiled=True),
    )
    lowered = encoded.astype(jnp.bfloat16)
    embedded = product(lowered, decoder_full[0])
    start = jnp.where(
        shown_rows[:, None], embedded, decoder_full[1].astype(jnp.float32)[None, :]
    ) + sincos(own_scaled, embedded.shape[1])
    decoded, decoder_saved = block_forward(
        start,
        decoder_full[2:],
        DEC_HEADS,
        same_image,
        lambda key_value: (
            lax.all_gather(key_value[0], "blk", axis=0, tiled=True),
            lax.all_gather(key_value[1], "blk", axis=0, tiled=True),
        ),
    )
    decoded_rows = decoded.astype(jnp.bfloat16)
    decoder_back = (
        lax.all_gather(embed_proj, "dp", axis=0, tiled=True),
        lax.all_gather(mask_token, "dp", axis=0, tiled=True),
        lax.all_gather(decoder_gain_first, "dp", axis=0, tiled=True),
        lax.all_gather(decoder_bias_first, "dp", axis=0, tiled=True),
        lax.all_gather(decoder_query, "dp", axis=0, tiled=True),
        lax.all_gather(decoder_key, "dp", axis=0, tiled=True),
        lax.all_gather(decoder_value, "dp", axis=0, tiled=True),
        lax.all_gather(decoder_output, "dp", axis=0, tiled=True),
        lax.all_gather(decoder_gain_second, "dp", axis=0, tiled=True),
        lax.all_gather(decoder_bias_second, "dp", axis=0, tiled=True),
        lax.all_gather(decoder_up, "dp", axis=0, tiled=True),
        lax.all_gather(decoder_down, "dp", axis=0, tiled=True),
    )
    grad_start, decoder_gradients = block_backward(
        cotangent.astype(jnp.float32),
        decoder_back[2:],
        DEC_HEADS,
        same_image,
        decoder_saved,
        lambda key_value: (
            lax.psum_scatter(
                key_value[0].astype(jnp.bfloat16), "blk", scatter_dimension=0, tiled=True
            ).astype(jnp.float32),
            lax.psum_scatter(
                key_value[1].astype(jnp.bfloat16), "blk", scatter_dimension=0, tiled=True
            ).astype(jnp.float32),
        ),
    )
    grad_mask = jnp.sum(jnp.where(shown_rows[:, None], 0.0, grad_start), axis=0)
    grad_embedded = jnp.where(shown_rows[:, None], grad_start, 0.0).astype(jnp.bfloat16)
    grad_embed = trans_product(lowered, grad_embedded)
    grad_encoded = back_product(grad_embedded, decoder_back[0])
    decoder_sums = reduce_gradients(
        (grad_embed, grad_mask) + decoder_gradients, dp_count, blk_count
    )
    encoder_back = (
        lax.all_gather(encoder_gain_first, "dp", axis=0, tiled=True),
        lax.all_gather(encoder_bias_first, "dp", axis=0, tiled=True),
        lax.all_gather(encoder_query, "dp", axis=0, tiled=True),
        lax.all_gather(encoder_key, "dp", axis=0, tiled=True),
        lax.all_gather(encoder_value, "dp", axis=0, tiled=True),
        lax.all_gather(encoder_output, "dp", axis=0, tiled=True),
        lax.all_gather(encoder_gain_second, "dp", axis=0, tiled=True),
        lax.all_gather(encoder_bias_second, "dp", axis=0, tiled=True),
        lax.all_gather(encoder_up, "dp", axis=0, tiled=True),
        lax.all_gather(encoder_down, "dp", axis=0, tiled=True),
    )
    grad_residual, encoder_gradients = block_backward(
        grad_encoded,
        encoder_back,
        HEADS,
        allowed,
        encoder_saved,
        lambda key_value: (
            lax.psum_scatter(
                key_value[0].astype(jnp.bfloat16), "blk", scatter_dimension=0, tiled=True
            ).astype(jnp.float32),
            lax.psum_scatter(
                key_value[1].astype(jnp.bfloat16), "blk", scatter_dimension=0, tiled=True
            ).astype(jnp.float32),
        ),
    )
    encoder_sums = reduce_gradients(encoder_gradients, dp_count, blk_count)
    return (decoded_rows, grad_residual) + encoder_sums + decoder_sums


def solution(mesh):
    in_specs = (
        P(("dp", "blk"), None),
        P("dp", None),
        P("dp", None),
        P("dp", None),
        P("dp"),
        P("dp"),
        P("dp", None),
        P("dp", None),
        P("dp", None),
        P("dp", None),
        P("dp"),
        P("dp"),
        P("dp", None),
        P("dp", None),
        P("dp", None),
        P("dp"),
        P("dp"),
        P("dp"),
        P("dp", None),
        P("dp", None),
        P("dp", None),
        P("dp", None),
        P("dp"),
        P("dp"),
        P("dp", None),
        P("dp", None),
        P(("dp", "blk"), None),
    )
    out_specs = (
        P(("dp", "blk"), None),
        P(("dp", "blk"), None),
        P("dp"),
        P("dp"),
        P("dp", None),
        P("dp", None),
        P("dp", None),
        P("dp", None),
        P("dp"),
        P("dp"),
        P("dp", None),
        P("dp", None),
        P("dp", None),
        P("dp"),
        P("dp"),
        P("dp"),
        P("dp", None),
        P("dp", None),
        P("dp", None),
        P("dp", None),
        P("dp"),
        P("dp"),
        P("dp", None),
        P("dp", None),
    )
    return jax.shard_map(local, mesh=mesh, in_specs=in_specs, out_specs=out_specs, check_vma=False)
```

profile of v0, /device:TPU:0, one launch (start us, length us, event | category | flops | bytes accessed | tf_op | source)
XLA Modules:
  0.0 3988.2 jit_solution(8398304116860409939)
XLA Ops:
  10.3 22.3 all-gather.1
  65.2 47.0 %all-gather.22.cloned.1.call-done = bf16[1024,1024]{1,0:T(8,128)(2,1)} async-done(((bf16[128,1024]{1,0:T(8,128)(2,1)}), bf16[1024,1024]{1,0:T(8,128)(2,1)}) %all-gather.22.cloned.1.call-update) | async-done | bytes 2097168 | tf_op jit(solution)/shard_map/all_gather | solution.py:319
  180.3 33.8 all_gather.111
  214.0 32.6 all_gather.112
  246.6 32.5 all_gather.114
  279.1 34.8 all_gather.116
  321.8 26.0 while.56
  351.1 35.6 all-gather.28.cloned.1.call-done
  392.8 119.2 %all-gather.30.cloned.1.call-done = bf16[4096,1024]{1,0:T(8,128)(2,1)} async-done(((bf16[512,1024]{1,0:T(8,128)(2,1)}), bf16[4096,1024]{1,0:T(8,128)(2,1)}) %all-gather.30.cloned.1.call-update) | async-done | bytes 8388624 | tf_op jit(solution)/shard_map/all_gather | solution.py:324
  521.4 31.1 all-gather.32.cloned.1.call-done
  574.7 26.7 while.57
  608.2 44.4 %all-gather.36.cloned.1.call-done = bf16[2048,512]{1,0:T(8,128)(2,1)} async-done(((bf16[256,512]{1,0:T(8,128)(2,1)}), bf16[2048,512]{1,0:T(8,128)(2,1)}) %all-gather.36.cloned.1.call-update) | async-done | bytes 2097168 | tf_op jit(solution)/shard_map/all_gather | solution.py:349
  663.6 58.0 %while.58 = (s32[]{:T(128)}, bf16[8,2,128,32]{2,3,1,0:T(8,128)(2,1)}, bf16[8,2,512,32]{2,3,1,0:T(8,128)(2,1)}, bf16[8,2,512,32]{2,3,1,0:T(8,128)(2,1)}, bf16[8,2...) while((s32[]{:T(128)}, ...), condition=%wide.region_24.25_spmd.clone, body=%wide.region_22.24_spmd.clone.sunk | while | flops 43228928 | bytes 4633217 | solution.py:122
  802.9 47.1 %while.59 = (s32[]{:T(128)}, bf16[8,2,128,64]{2,3,1,0:T(8,128)(2,1)}, bf16[8,2,512,64]{2,3,1,0:T(8,128)(2,1)S(1)}, bf16[8,2,512,64]{2,3,1,0:T(8,128)(2,1)}, bf16...) while((s32[]{:T(128)}, ...), condition=%wide.region_33.34_spmd.clone, body=%wide.region_31.33_spmd.clone.sunk | while | flops 85409536 | bytes 5191313 | solution.py:122
  985.8 27.6 dynamic-update-slice.15
  1013.4 27.4 dynamic-update-slice.16
  1109.2 27.7 dynamic-update-slice.19
  1136.8 27.6 dynamic-update-slice.20
  1164.5 27.6 dynamic-update-slice.21
  1192.1 27.6 dynamic-update-slice.22
  1252.4 37.6 copy.91
  1290.0 2475.4 %all-reduce.14 = (bf16[8,1573376]{1,0:T(8,128)(2,1)}, bf16[8,459072]{1,0:T(8,128)(2,1)}) all-reduce(f32[8,1573376]{1,0:T(8,128)} %bitcast.327, f32[8,459072]{1,0:T(8,128)} %reshape.522), channel_id=6, replica_groups=mesh['dp'=8,'blk'=4] {'dp'}, use_global_device_ids=true, to_apply=%region_42.43.clone | all-reduce | flops 16259584 | bytes 97557504
  3765.4 62.9 %fusion.96 = bf16[1573376]{0:T(1024)(128)(2,1)} fusion(bf16[8,1573376]{1,0:T(8,128)(2,1)} %get-tuple-element.418, u32[]{:T(128)} %bitcast.93), kind=kLoop, calls=%fused_computation.121 | loop fusion | bytes 6293508 | tf_op jit(solution)/shard_map/convert_element_type | solution.py:261
  3861.0 78.3 %all-reduce.13.cloned.1.call-done = (bf16[4,393344]{1,0:T(4,128)(2,1)}, bf16[4,114768]{1,0:T(4,128)(2,1)}) async-done(((bf16[4,393344]{1,0:T(4,128)(2,1)}, bf16[4,114768]{1,0:T(4,128)(2,1)}), (bf16[4,393344]{1,0:T(4,128)(2,1)}, bf16[4,114768]{1,0:T(4,128)(2,1)})) %all-reduce.13.cloned.1.call-update) | async-done | bytes 4064912 | tf_op jit(solution)/shard_map/psum | solution.py:261
  (669 shorter events, 718.1 us)
Async XLA Ops:
  7.2 55.1 %all-gather.18.cloned.1.call-start = ((), (), s32[]{:S(2)}) async-start(), calls=%async_computation.5 | async-start | bytes 2359296 | tf_op jit(solution)/shard_map/all_gather | solution.py:318
  7.9 104.3 %all-gather.22.cloned.1.call-start = ((), (), s32[]{:S(2)}) async-start(), calls=%async_computation.7 | async-start | bytes 2359296 | tf_op jit(solution)/shard_map/all_gather | solution.py:319
  8.7 306.4 %all-gather.16.cloned.1.call-start = ((), (), s32[]{:S(2)}) async-start(), calls=%async_computation.4 | async-start | bytes 2359296 | tf_op jit(solution)/shard_map/all_gather | solution.py:317
  9.4 307.9 %all-gather.20.cloned.1.call-start = ((), (), s32[]{:S(2)}) async-start(), calls=%async_computation.6 | async-start | bytes 1310720 | tf_op jit(solution)/shard_map/all_gather | solution.py:333
  52.9 295.7 %copy-start = (f32[128,1024]{1,0:T(8,128)}, f32[128,1024]{1,0:T(8,128)S(1)}, u32[]{:S(2)}) copy-start(f32[128,1024]{1,0:T(8,128)S(1)} %get-tuple-element.440) | copy-start | bytes 1572868
  53.1 59.1 %copy-start.95 = (f32[128]{0:T(128)}, f32[128]{0:T(128)S(1)}, u32[]{:S(2)}) copy-start(f32[128]{0:T(128)S(1)} %multiply_reduce_fusion.7) | copy-start | bytes 1540
  65.1 253.8 %all-gather.24.cloned.1.call-start = ((), (), s32[]{:S(2)}) async-start(), calls=%async_computation.8 | async-start | bytes 1310720 | tf_op jit(solution)/shard_map/all_gather | solution.py:334
  115.0 65.2 %copy-start.48 = (bf16[64,512]{1,0:T(8,128)(2,1)S(1)}, bf16[64,512]{1,0:T(8,128)(2,1)}, u32[]{:S(2)}) copy-start(bf16[64,512]{1,0:T(8,128)(2,1)} %param.53) | copy-start | bytes 196612
  115.0 99.0 %copy-start.49 = (bf16[64,512]{1,0:T(8,128)(2,1)S(1)}, bf16[64,512]{1,0:T(8,128)(2,1)}, u32[]{:S(2)}) copy-start(bf16[64,512]{1,0:T(8,128)(2,1)} %param.54) | copy-start | bytes 196612
  115.1 232.8 %all-gather.26.cloned.1.call-start = ((), (), s32[]{:S(2)}) async-start(), calls=%async_computation.9 | async-start | bytes 2359296 | tf_op jit(solution)/shard_map/all_gather | solution.py:320
  115.6 131.0 %copy-start.50 = (bf16[64,512]{1,0:T(8,128)(2,1)S(1)}, bf16[64,512]{1,0:T(8,128)(2,1)}, u32[]{:S(2)}) copy-start(bf16[64,512]{1,0:T(8,128)(2,1)} %param.55) | copy-start | bytes 196612
  115.6 271.1 %all-gather.28.cloned.1.call-start = ((), (), s32[]{:S(2)}) async-start(), calls=%async_computation.10 | async-start | bytes 9437184 | tf_op jit(solution)/shard_map/all_gather | solution.py:323
  116.4 162.7 %copy-start.51 = (bf16[64,512]{1,0:T(8,128)(2,1)S(1)}, bf16[64,512]{1,0:T(8,128)(2,1)}, u32[]{:S(2)}) copy-start(bf16[64,512]{1,0:T(8,128)(2,1)} %param.56) | copy-start | bytes 196612
  116.4 395.6 %all-gather.30.cloned.1.call-start = ((), (), s32[]{:S(2)}) async-start(), calls=%async_computation.11 | async-start | bytes 9437184 | tf_op jit(solution)/shard_map/all_gather | solution.py:324
  117.2 435.4 %all-gather.32.cloned.1.call-start = ((), (), s32[]{:S(2)}) async-start(), calls=%async_computation.12 | async-start | bytes 1179648 | tf_op jit(solution)/shard_map/all_gather | solution.py:338
  117.9 487.2 %all-gather.34.cloned.1.call-start = ((), (), s32[]{:S(2)}) async-start(), calls=%async_computation.13 | async-start | bytes 2359296 | tf_op jit(solution)/shard_map/all_gather | solution.py:348
  118.5 534.1 %all-gather.36.cloned.1.call-start = ((), (), s32[]{:S(2)}) async-start(), calls=%async_computation.14 | async-start | bytes 2359296 | tf_op jit(solution)/shard_map/all_gather | solution.py:349
  119.2 639.9 %reduce-scatter.13.cloned.1.call-start = ((), (), s32[]{:S(2)}) async-start(), calls=%async_computation.15 | async-start | bytes 655360
  246.6 310.9 %copy-start.13 = (bf16[512,512]{1,0:T(8,128)(2,1)}, bf16[512,512]{1,0:T(8,128)(2,1)S(1)}, u32[]{:S(2)}) copy-start(bf16[512,512]{1,0:T(8,128)(2,1)S(1)} %all_gather.112) | copy-start | bytes 1572868
  603.3 134.7 %copy-start.2 = (f32[128,512]{1,0:T(8,128)}, f32[128,512]{1,0:T(8,128)S(1)}, u32[]{:S(2)}) copy-start(f32[128,512]{1,0:T(8,128)S(1)} %get-tuple-element.481) | copy-start | bytes 786436
  723.7 45.2 %reduce-scatter.15.cloned.1.call-start = ((), (), s32[]{:S(2)}) async-start(), calls=%async_computation.16 | async-start | bytes 655360
  737.5 343.6 %reduce-scatter.17.cloned.1.call-start = ((), (), s32[]{:S(2)}) async-start(), calls=%async_computation.17 | async-start | bytes 1310720
  851.3 232.6 %reduce-scatter.19.cloned.1.call-start = ((), (), s32[]{:S(2)}) async-start(), calls=%async_computation.18 | async-start | bytes 1310720
  927.3 3012.0 %all-reduce.13.cloned.1.call-start = ((), (), s32[]{:S(2)}) async-start(), calls=%async_computation.19 | async-start | bytes 8130560 | tf_op jit(solution)/shard_map/psum | solution.py:261
  (98 other events, 962.3 us)
Sparse Core Ops, SparseCore 0:
  10.2 52.1 all-gather.17
  64.5 47.6 all-gather.21
  114.3 47.9 all-gather.15
  164.3 15.2 all-gather.19
  181.5 16.7 all-gather.23
  200.3 57.5 all-gather.25
  259.9 126.7 all-gather.27
  388.8 123.1 all-gather.29
  514.1 38.3 all-gather.31
  554.5 48.0 all-gather.33
  604.8 47.7 all-gather.35
  723.9 20.1 reduce-scatter.12
  747.3 21.6 reduce-scatter.14
  851.4 24.8 reduce-scatter.16
  927.4 25.0 reduce-scatter.18
  3857.0 82.2 all-reduce.12
where the time goes:
time: 4010 us; the launch traced here: 3990 us
  blocking collectives  2720 us (68%)
  local copies, waits for them, and re-layouts  593 us (15%)
  waiting for transfers between devices  379 us (9%)
  matrix products  244 us (6%)
    unnamed x2, blocking collectives  2490 us
    unnamed x249, local copies, waits for them, and re-layouts  296 us
    all_gather x1, waiting for transfers between devices, local(): lax.all_gather(encoder_down, 'dp', axis=0, tiled=True)  119 us
    reshape x22, local copies, waits for them, and re-layouts, reduce_gradients(): gradient.reshape(dp_count, blk_count, -1)  88.2 us
    convert_element_type x2, local copies, waits for them, and re-layouts, reduce_gradients(): summed.astype(jnp.bfloat16)  82.6 us
  transfers between devices with their start and end apart: 16, of which 8 were waited for; matrix products, arithmetic and copies ran while one was open for 9% of the time, Pallas kernels for 0%

commit v1 on v0

v1 whole, which is shorter than its diff:
```python
import math

import jax
import jax.numpy as jnp
from jax import lax
from jax.sharding import PartitionSpec as P

HEADS = 16
EPSILON = 1e-06
MASKED_SCORE = -1e30
F32 = jnp.float32
BF16 = jnp.bfloat16


def dot(left, right):
    return lax.dot_general(left, right, (((1,), (0,)), ((), ())), preferred_element_type=F32)


def dot_t(left, right):
    return lax.dot_general(left, right, (((0,), (0,)), ((), ())), preferred_element_type=F32)


def dot_b(left, right):
    return lax.dot_general(left, right, (((1,), (1,)), ((), ())), preferred_element_type=F32)


def sincos(scaled, width):
    half_width = width // 2
    frequency = jnp.exp(
        jnp.arange(half_width, dtype=F32) * (-math.log(10000.0) / half_width)
    )
    angles = scaled[:, None] * frequency[None, :]
    return jnp.concatenate([jnp.sin(angles), jnp.cos(angles)], axis=1)


def norm_parts(values):
    center = values - jnp.mean(values, axis=-1, keepdims=True)
    spread = jnp.mean(center * center, axis=-1, keepdims=True)
    scale = lax.rsqrt(spread + EPSILON)
    return center * scale, scale


def norm_back(grad, unit, scale, gain):
    grad_gain = jnp.sum(grad * unit, axis=0, keepdims=True)
    grad_bias = jnp.sum(grad, axis=0, keepdims=True)
    inner = grad * gain
    mean_inner = jnp.mean(inner, axis=-1, keepdims=True)
    mean_cross = jnp.mean(inner * unit, axis=-1, keepdims=True)
    return scale * (inner - mean_inner - unit * mean_cross), grad_gain, grad_bias


def gelu_both(upper):
    phi = 0.5 * (1.0 + lax.erf(upper * math.sqrt(0.5)))
    density = jnp.exp(-0.5 * upper * upper) * (1.0 / math.sqrt(2.0 * math.pi))
    return upper * phi, phi + upper * density


def head_forward(queries, key_rows, values, allowed, scaling):
    scores = jnp.where(allowed, dot_b(queries, key_rows) * scaling, MASKED_SCORE)
    largest = jnp.max(scores, axis=-1, keepdims=True)
    exponent = jnp.exp(scores - largest)
    softmaxed = exponent / jnp.sum(exponent, axis=-1, keepdims=True)
    return softmaxed, dot(softmaxed.astype(BF16), values).astype(BF16)


def head_backward(queries, key_rows, values, softmaxed, grad_mixture, scaling):
    grad_values = dot_t(softmaxed.astype(BF16), grad_mixture).astype(BF16)
    grad_probs = dot_b(grad_mixture, values)
    delta = jnp.sum(softmaxed * grad_probs, axis=-1, keepdims=True)
    grad_scores = (softmaxed * (grad_probs - delta)).astype(BF16)
    grad_queries = (dot(grad_scores, key_rows) * scaling).astype(BF16)
    grad_keys = (dot_t(grad_scores, queries) * scaling).astype(BF16)
    return grad_queries, grad_keys, grad_values


def block_forward(residual, params, heads, allowed, total):
    gain_a, bias_a, w_query, w_key, w_value, w_out, gain_b, bias_b, w_up, w_down = params
    unit_a, scale_a = norm_parts(residual)
    normed = (unit_a * gain_a + bias_a).astype(BF16)
    queries = dot(normed, w_query).astype(BF16)
    key_rows = dot(normed, w_key).astype(BF16)
    values = dot(normed, w_value).astype(BF16)
    size = queries.shape[1] // heads
    scaling = 1.0 / math.sqrt(size)
    probs, mixed = [], []
    for head in range(heads):
        part = slice(head * size, (head + 1) * size)
        softmaxed, mixture = head_forward(
            queries[:, part], key_rows[:, part], values[:, part], allowed, scaling
        )
        probs.append(softmaxed)
        mixed.append(mixture)
    mixture = jnp.concatenate(mixed, axis=1)
    middle = residual + total(dot(mixture, w_out))
    unit_b, scale_b = norm_parts(middle)
    lifted = (unit_b * gain_b + bias_b).astype(BF16)
    hidden, slope = gelu_both(dot(lifted, w_up))
    hidden = hidden.astype(BF16)
    result = middle + total(dot(hidden, w_down))
    return result, (
        unit_a, scale_a, normed, queries, key_rows, values, probs, mixture,
        unit_b, scale_b, lifted, slope, hidden,
    )


def block_backward(grad_result, params, heads, saved, total):
    gain_a, bias_a, w_query, w_key, w_value, w_out, gain_b, bias_b, w_up, w_down = params
    (unit_a, scale_a, normed, queries, key_rows, values, probs, mixture,
     unit_b, scale_b, lifted, slope, hidden) = saved
    size = queries.shape[1] // heads
    scaling = 1.0 / math.sqrt(size)
    grad_branch = grad_result.astype(BF16)
    grad_down = dot_t(hidden, grad_branch)
    grad_upper = (dot_b(grad_branch, w_down) * slope).astype(BF16)
    grad_up = dot_t(lifted, grad_upper)
    grad_lifted = total(dot_b(grad_upper, w_up))
    grad_in, grad_gain_b, grad_bias_b = norm_back(grad_lifted, unit_b, scale_b, gain_b)
    grad_middle = grad_result + grad_in
    grad_attention = grad_middle.astype(BF16)
    grad_out = dot_t(mixture, grad_attention)
    grad_mixture = dot_b(grad_attention, w_out).astype(BF16)
    pieces = []
    for head in range(heads):
        part = slice(head * size, (head + 1) * size)
        pieces.append(
            head_backward(
                queries[:, part], key_rows[:, part], values[:, part], probs[head],
                grad_mixture[:, part], scaling,
            )
        )
    grad_queries, grad_keys, grad_values = (
        jnp.concatenate([piece[at] for piece in pieces], axis=1) for at in range(3)
    )
    grad_normed = total(
        dot_b(grad_queries, w_query) + dot_b(grad_keys, w_key) + dot_b(grad_values, w_value)
    )
    grad_in, grad_gain_a, grad_bias_a = norm_back(grad_normed, unit_a, scale_a, gain_a)
    return grad_middle + grad_in, (
        grad_gain_a, grad_bias_a, dot_t(normed, grad_queries), dot_t(normed, grad_keys),
        dot_t(normed, grad_values), grad_out, grad_gain_b, grad_bias_b, grad_up, grad_down,
    )


def layout(lengths_row, gsd_row, visible_row):
    count = visible_row.shape[0]
    positions = jnp.arange(count, dtype=jnp.int32)
    image_ends = jnp.cumsum(lengths_row)
    image_starts = image_ends - lengths_row
    image_ids = jnp.sum((positions[:, None] >= image_ends[None, :]).astype(jnp.int32), axis=1)
    onehot = image_ids[:, None] == jnp.arange(lengths_row.shape[0], dtype=jnp.int32)[None, :]
    first_row = jnp.sum(jnp.where(onehot, image_starts[None, :], 0), axis=1)
    ratio = jnp.sum(jnp.where(onehot, gsd_row[None, :], 0.0), axis=1)
    scaled = (positions - first_row).astype(F32) * ratio
    shown = visible_row > 0
    earlier = (positions[None, :] <= positions[:, None]) & shown[None, :]
    rank = jnp.where(shown, jnp.sum(earlier.astype(jnp.int32), axis=1) - 1, -1)
    return image_ids, scaled, rank


def spread_rows(grad, rank, offset, rows):
    own = lax.dynamic_slice_in_dim(rank, offset, rows)
    place = (own[:, None] == jnp.arange(grad.shape[0], dtype=jnp.int32)[None, :]).astype(BF16)
    high = grad.astype(BF16)
    low = (grad - high.astype(F32)).astype(BF16)
    return dot(place, high) + dot(place, low)


SHOWN = 128


def local(*arguments):
    patches, lengths, gsd_scale, visible = arguments[:4]
    encoder_shards = arguments[4:14]
    embed_shard, mask_shard = arguments[14:16]
    decoder_shards = arguments[16:26]
    cotangent = arguments[26]
    dp_count = lax.axis_size("dp")
    blk_count = lax.axis_size("blk")
    blk = lax.axis_index("blk")
    dp = lax.axis_index("dp")
    rows = patches.shape[0]
    offset = blk * rows
    heads = HEADS // blk_count
    image_ids, scaled, rank = layout(lengths[0], gsd_scale[0], visible[0])
    shown = rank >= 0
    places = rank[None, :] == jnp.arange(SHOWN, dtype=jnp.int32)[:, None]
    packed_ids = jnp.sum(jnp.where(places, image_ids[None, :], 0), axis=1)
    packed_scaled = jnp.sum(jnp.where(places, scaled[None, :], 0.0), axis=1)

    def gather(shard):
        return lax.all_gather(shard, "dp", axis=0, tiled=True)

    def by_columns(shard):
        width = shard.shape[1] // blk_count
        return gather(lax.dynamic_slice_in_dim(shard, blk * width, width, axis=1))

    def by_rows(shard):
        whole = gather(shard)
        height = whole.shape[0] // blk_count
        return lax.dynamic_slice_in_dim(whole, blk * height, height, axis=0)

    def vector(shard):
        return gather(shard).astype(F32)[None, :]

    def load(shards):
        kinds = (vector, vector, by_columns, by_columns, by_columns, by_rows,
                 vector, vector, by_columns, by_rows)
        return tuple(kind(shard) for kind, shard in zip(kinds, shards))

    def total(partial):
        return lax.psum(partial, "blk")

    def sum_columns(grad):
        summed = lax.psum_scatter(grad.astype(BF16), "dp", scatter_dimension=0, tiled=True)
        return lax.all_gather(summed, "blk", axis=1, tiled=True).astype(F32)

    def sum_rows(grad):
        whole = lax.all_gather(grad.astype(BF16), "blk", axis=0, tiled=True)
        return lax.psum_scatter(whole, "dp", scatter_dimension=0, tiled=True).astype(F32)

    def sum_vector(grad):
        return lax.psum_scatter(grad[0], "dp", scatter_dimension=0, tiled=True)

    def reduce(grads):
        kinds = (sum_vector, sum_vector, sum_columns, sum_columns, sum_columns, sum_rows,
                 sum_vector, sum_vector, sum_columns, sum_rows)
        return tuple(kind(grad) for kind, grad in zip(kinds, grads))

    group = lax.all_gather(patches, "blk", axis=0, tiled=True)
    picked = dot(places.astype(BF16), group)
    encoder = load(encoder_shards)
    residual = picked + sincos(packed_scaled, patches.shape[1])
    encoded, encoder_saved = block_forward(
        residual, encoder, heads, packed_ids[:, None] == packed_ids[None, :], total
    )
    embed = gather(embed_shard)
    lowered = encoded.astype(BF16)
    embedded = dot(lowered, embed)
    high = embedded.astype(BF16)
    low = (embedded - high.astype(F32)).astype(BF16)
    places_b = places.astype(BF16)
    start = jnp.where(
        shown[:, None], dot_t(places_b, high) + dot_t(places_b, low), vector(mask_shard)
    ) + sincos(scaled, embed.shape[1])
    decoder = load(decoder_shards)
    decoded, decoder_saved = block_forward(
        start, decoder, heads, image_ids[:, None] == image_ids[None, :], total
    )
    decoded_rows = lax.dynamic_slice_in_dim(decoded, offset, rows).astype(BF16)
    grad_out = lax.all_gather(cotangent, "blk", axis=0, tiled=True).astype(F32)
    grad_start, decoder_grads = block_backward(grad_out, decoder, heads, decoder_saved, total)
    grad_mask = jnp.sum(jnp.where(shown[:, None], 0.0, grad_start), axis=0, keepdims=True)
    grad_embedded = dot(places_b, grad_start.astype(BF16)).astype(BF16)
    width = embed.shape[1] // blk_count
    grad_embed = dot_t(
        lowered, lax.dynamic_slice_in_dim(grad_embedded, blk * width, width, axis=1)
    )
    grad_encoded = dot_b(grad_embedded, embed)
    grad_residual, encoder_grads = block_backward(
        grad_encoded, encoder, heads, encoder_saved, total
    )
    grad_patches = spread_rows(grad_residual, rank, offset, rows)
    return (
        (decoded_rows, grad_patches) + reduce(encoder_grads)
        + (sum_columns(grad_embed), sum_vector(grad_mask)) + reduce(decoder_grads)
    )


def solution(mesh):
    both, vec, mat = P(("dp", "blk"), None), P("dp"), P("dp", None)
    block = (vec, vec, mat, mat, mat, mat, vec, vec, mat, mat)
    in_specs = (both, mat, mat, mat) + block + (mat, vec) + block + (both,)
    out_specs = (both, both) + block + (mat, vec) + block
    return jax.shard_map(local, mesh=mesh, in_specs=in_specs, out_specs=out_specs, check_vma=False)
```

time: 4010 us -> 1900 us (0.47)
  blocking collectives: 2720 us -> 452 us
  waiting for transfers between devices: 379 us -> 1280 us
  local copies, waits for them, and re-layouts: 593 us -> 25.5 us
  matrix products: 244 us -> 68.1 us
    unnamed x2, blocking collectives: 2490 us -> 56.4 us
    reduce_scatter x0 -> x13, waiting for transfers between devices: none -> 810 us  [the longest x9 465 us: sum_columns(): lax.psum_scatter(grad.astype(BF16), 'dp', scatter_dimension=0, tiled=True)]
    unnamed x249 -> x382, local copies, waits for them, and re-layouts: 296 us -> 18.4 us
    dot_general x151 -> x93, matrix products: 244 us -> 68.1 us  [the longest x31 24.7 us: dot_t(): lax.dot_general(left, right, (((0,), (0,)), ((), ())), preferred_element_...]
    all_gather x10 -> x22, blocking collectives: 222 us -> 396 us  [the longest x12 332 us: gather(): return lax.all_gather(shard, 'dp', axis=0, tiled=True)]
    reshape x47 -> x0, local copies, waits for them, and re-layouts: 146 us -> none  [the longest x22 88.2 us: reduce_gradients(): gradient.reshape(dp_count, blk_count, -1)]
    convert_element_type x6 -> x0, local copies, waits for them, and re-layouts: 84.9 us -> none  [the longest x2 82.6 us: reduce_gradients(): summed.astype(jnp.bfloat16)]
    psum x1 -> x7, waiting for transfers between devices: 78.3 us -> 143 us  [total(): return lax.psum(partial, 'blk')]
  transfers between devices with their start and end apart: 16 -> 30, of which waited for: 8 -> 24; matrix products, arithmetic and copies ran while one was open for 9% -> 5% of each run, Pallas kernels for 0% -> 0%
where the time goes in v1:
time: 1900 us; the launch traced here: 1890 us
  waiting for transfers between devices  1280 us (67%)
  blocking collectives  452 us (24%)
  matrix products  68.1 us (4%)
  other arithmetic  49 us (3%)
  local copies, waits for them, and re-layouts  25.5 us (1%)
  between operations  19.4 us (1%)
    reduce_scatter x9, waiting for transfers between devices, sum_columns(): lax.psum_scatter(grad.astype(BF16), 'dp', scatter_dimension=0, tiled=True)  465 us
    reduce_scatter x4, waiting for transfers between devices, sum_rows(): lax.psum_scatter(whole, 'dp', scatter_dimension=0, tiled=True).astype(F32)  344 us
    all_gather x12, blocking collectives, gather(): return lax.all_gather(shard, 'dp', axis=0, tiled=True)  332 us
    all_gather x5, waiting for transfers between devices, gather(): return lax.all_gather(shard, 'dp', axis=0, tiled=True)  204 us
    psum x7, waiting for transfers between devices, total(): return lax.psum(partial, 'blk')  143 us
    all_gather x3, waiting for transfers between devices, sum_rows(): whole = lax.all_gather(grad.astype(BF16), 'blk', axis=0, tiled=True)  107 us
    unnamed x2, blocking collectives  56.4 us
    all_gather x8, blocking collectives, sum_columns(): return lax.all_gather(summed, 'blk', axis=1, tiled=True).astype(F32)  46 us
  transfers between devices with their start and end apart: 30, of which 24 were waited for; matrix products, arithmetic and copies ran while one was open for 5% of the time, Pallas kernels for 0%

profile of v1, /device:TPU:0, one launch (start us, length us, event | category | flops | bytes accessed | tf_op | source)
XLA Modules:
  0.0 1893.7 jit_solution(14634088563756796415)
XLA Ops:
  54.5 33.0 %all_gather.116 = bf16[1024,256]{1,0:T(8,128)(2,1)S(1)} all-gather(bf16[128,256]{1,0:T(8,128)(2,1)S(1)} %constant_dynamic-slice_fusion.5), channel_id=1, replica_groups=mesh['dp'=8,'blk'=4] {'dp'}, dimensions={0}, use_global_device_ids=true | all-gather | bytes 589824 | tf_op jit(solution)/shard_map/all_gather | solution.py:191
  196.3 46.4 %all-gather.19.cloned.1.call-done = bf16[1024,1024]{1,0:T(8,128)(2,1)} async-done(((bf16[128,1024]{1,0:T(8,128)(2,1)}), bf16[1024,1024]{1,0:T(8,128)(2,1)}) %all-gather.19.cloned.1.call-update) | async-done | bytes 2097168 | tf_op jit(solution)/shard_map/all_gather | solution.py:191
  244.9 123.2 %all-gather.21.cloned.1.call-done = bf16[4096,1024]{1,0:T(8,128)(2,1)} async-done(((bf16[512,1024]{1,0:T(8,128)(2,1)}), bf16[4096,1024]{1,0:T(8,128)(2,1)}) %all-gather.21.cloned.1.call-update) | async-done | bytes 8388624 | tf_op jit(solution)/shard_map/all_gather | solution.py:191
  427.3 33.0 %all_gather.127 = bf16[512,128]{1,0:T(8,128)(2,1)} all-gather(bf16[64,128]{1,0:T(8,128)(2,1)S(1)} %constant_dynamic-slice_fusion.2), channel_id=1, replica_groups=mesh['dp'=8,'blk'=4] {'dp'}, dimensions={0}, use_global_device_ids=true | all-gather | bytes 147456 | tf_op jit(solution)/shard_map/all_gather | solution.py:191
  494.3 33.5 %all_gather.129 = bf16[512,512]{1,0:T(8,128)(2,1)} all-gather(bf16[64,512]{1,0:T(8,128)(2,1)S(1)} %copy-done.90), channel_id=1, replica_groups=mesh['dp'=8,'blk'=4] {'dp'}, dimensions={0}, use_global_device_ids=true | all-gather | bytes 589824 | tf_op jit(solution)/shard_map/all_gather | solution.py:191
  557.4 33.4 %all_gather.132 = bf16[512,512]{1,0:T(8,128)(2,1)} all-gather(bf16[64,512]{1,0:T(8,128)(2,1)S(1)} %constant_dynamic-slice_fusion), channel_id=1, replica_groups=mesh['dp'=8,'blk'=4] {'dp'}, dimensions={0}, use_global_device_ids=true | all-gather | bytes 589824 | tf_op jit(solution)/shard_map/all_gather | solution.py:191
  595.3 34.5 %all-gather.25.cloned.1.call-done = bf16[2048,512]{1,0:T(8,128)(2,1)} async-done(((bf16[256,512]{1,0:T(8,128)(2,1)}), bf16[2048,512]{1,0:T(8,128)(2,1)}) %all-gather.25.cloned.1.call-update) | async-done | bytes 2097168 | tf_op jit(solution)/shard_map/all_gather | solution.py:191
  634.7 34.5 %all-reduce.31.cloned.1.call-done = f32[512,512]{0,1:T(8,128)} async-done(((f32[512,512]{0,1:T(8,128)}), f32[512,512]{0,1:T(8,128)}) %all-reduce.31.cloned.1.call-update) | async-done | bytes 1048592 | tf_op jit(solution)/shard_map/psum | solution.py:211
  686.1 36.6 %all-reduce.33.cloned.1.call-done = f32[512,512]{0,1:T(8,128)} async-done(((f32[512,512]{0,1:T(8,128)}), f32[512,512]{0,1:T(8,128)}) %all-reduce.33.cloned.1.call-update) | async-done | bytes 1048592 | tf_op jit(solution)/shard_map/psum | solution.py:211
  803.1 35.4 %reduce-scatter.22.cloned.1.call-done = bf16[128,1024]{1,0:T(8,128)(2,1)} async-done(((bf16[1024,1024]{1,0:T(8,128)(2,1)}), bf16[128,1024]{1,0:T(8,128)(2,1)}) %reduce-scatter.22.cloned.1.call-update) | async-done | bytes 262160 | tf_op jit(solution)/shard_map/reduce_scatter | solution.py:214
  885.7 60.3 %all-gather.31.cloned.1.call-done = bf16[4096,1024]{1,0:T(8,128)(2,1)} async-done(((bf16[1024,1024]{1,0:T(8,128)(2,1)}), bf16[4096,1024]{1,0:T(8,128)(2,1)}) %all-gather.31.cloned.1.call-update) | async-done | bytes 8388624 | tf_op jit(solution)/shard_map/all_gather | solution.py:218
  948.1 62.9 %reduce-scatter.32.cloned.1.call-done = bf16[64,128]{1,0:T(8,128)(2,1)} async-done(((bf16[512,128]{1,0:T(8,128)(2,1)}), bf16[64,128]{1,0:T(8,128)(2,1)}) %reduce-scatter.32.cloned.1.call-update) | async-done | bytes 16400 | tf_op jit(solution)/shard_map/reduce_scatter | solution.py:214
  1017.1 57.9 %reduce-scatter.30.cloned.1.call-done = bf16[64,128]{1,0:T(8,128)(2,1)} async-done(((bf16[512,128]{1,0:T(8,128)(2,1)}), bf16[64,128]{1,0:T(8,128)(2,1)}) %reduce-scatter.30.cloned.1.call-update) | async-done | bytes 16400 | tf_op jit(solution)/shard_map/reduce_scatter | solution.py:214
  1081.2 58.0 %reduce-scatter.28.cloned.1.call-done = bf16[64,128]{1,0:T(8,128)(2,1)} async-done(((bf16[512,128]{1,0:T(8,128)(2,1)}), bf16[64,128]{1,0:T(8,128)(2,1)}) %reduce-scatter.28.cloned.1.call-update) | async-done | bytes 16400 | tf_op jit(solution)/shard_map/reduce_scatter | solution.py:214
  1145.3 58.4 %reduce-scatter.36.cloned.1.call-done = bf16[64,512]{1,0:T(8,128)(2,1)} async-done(((bf16[512,512]{1,0:T(8,128)(2,1)}), bf16[64,512]{1,0:T(8,128)(2,1)}) %reduce-scatter.36.cloned.1.call-update) | async-done | bytes 65552 | tf_op jit(solution)/shard_map/reduce_scatter | solution.py:214
  1210.6 57.3 %reduce-scatter.26.cloned.1.call-done = bf16[128,128]{1,0:T(8,128)(2,1)} async-done(((bf16[1024,128]{1,0:T(8,128)(2,1)}), bf16[128,128]{1,0:T(8,128)(2,1)}) %reduce-scatter.26.cloned.1.call-update) | async-done | bytes 32784 | tf_op jit(solution)/shard_map/reduce_scatter | solution.py:214
  1274.3 57.9 %reduce-scatter.34.cloned.1.call-done = bf16[64,512]{1,0:T(8,128)(2,1)} async-done(((bf16[512,512]{1,0:T(8,128)(2,1)}), bf16[64,512]{1,0:T(8,128)(2,1)}) %reduce-scatter.34.cloned.1.call-update) | async-done | bytes 65552 | tf_op jit(solution)/shard_map/reduce_scatter | solution.py:219
  1333.7 43.8 %all-reduce.37.cloned.1.call-done = (f32[512,512]{0,1:T(8,128)}, f32[128,1024]{1,0:T(8,128)}) async-done(((f32[512,512]{0,1:T(8,128)}, f32[128,1024]{1,0:T(8,128)}), (f32[512,512]{0,1:T(8,128)}, f32[128,1024]{1,0:T(8,128)})) %all-reduce.37.cloned.1.call-update) | async-done | bytes 1572880 | tf_op jit(solution)/shard_map/psum | solution.py:211
  1380.7 37.2 %all-reduce.14 = (f32[1024]{0:T(1024)S(1)}, f32[1024]{0:T(1024)S(1)}, f32[1024]{0:T(1024)S(1)}, f32[1024]{0:T(1024)S(1)}, f32[512]{0:T(512)S(1)}, /*index=5*/f32...) all-reduce(f32[1024]{0:T(1024)S(1)} %get-tuple-element.104, ...), channel_id=2, replica_groups=mesh['dp'=8,'blk'=4] {'dp'}, use_global_device_ids=true, to_apply=%region_56.57.clone | all-reduce | flops 6656 | bytes 53248
  1450.5 58.0 %reduce-scatter.14.cloned.1.call-done = bf16[128,256]{1,0:T(8,128)(2,1)} async-done(((bf16[1024,256]{1,0:T(8,128)(2,1)}), bf16[128,256]{1,0:T(8,128)(2,1)}) %reduce-scatter.14.cloned.1.call-update) | async-done | bytes 65552 | tf_op jit(solution)/shard_map/reduce_scatter | solution.py:214
  1515.3 58.3 %reduce-scatter.16.cloned.1.call-done = bf16[128,256]{1,0:T(8,128)(2,1)} async-done(((bf16[1024,256]{1,0:T(8,128)(2,1)}), bf16[128,256]{1,0:T(8,128)(2,1)}) %reduce-scatter.16.cloned.1.call-update) | async-done | bytes 65552 | tf_op jit(solution)/shard_map/reduce_scatter | solution.py:214
  1593.5 68.5 %reduce-scatter.38.cloned.1.call-done = bf16[256,512]{1,0:T(8,128)(2,1)} async-done(((bf16[2048,512]{1,0:T(8,128)(2,1)}), bf16[256,512]{1,0:T(8,128)(2,1)}) %reduce-scatter.38.cloned.1.call-update) | async-done | bytes 262160 | tf_op jit(solution)/shard_map/reduce_scatter | solution.py:219
  1663.8 68.3 %reduce-scatter.20.cloned.1.call-done = bf16[128,1024]{1,0:T(8,128)(2,1)} async-done(((bf16[1024,1024]{1,0:T(8,128)(2,1)}), bf16[128,1024]{1,0:T(8,128)(2,1)}) %reduce-scatter.20.cloned.1.call-update) | async-done | bytes 262160 | tf_op jit(solution)/shard_map/reduce_scatter | solution.py:219
  1733.9 149.7 %reduce-scatter.24.cloned.1.call-done = bf16[512,1024]{1,0:T(8,128)(2,1)} async-done(((bf16[4096,1024]{1,0:T(8,128)(2,1)}), bf16[512,1024]{1,0:T(8,128)(2,1)}) %reduce-scatter.24.cloned.1.call-update) | async-done | bytes 1048592 | tf_op jit(solution)/shard_map/reduce_scatter | solution.py:219
  (662 shorter events, 534.5 us)
Async XLA Ops:
  7.2 144.5 %all-gather.15.cloned.1.call-start = ((), (), s32[]{:S(2)}) async-start(), calls=%async_computation.13 | async-start | bytes 1310720 | tf_op jit(solution)/shard_map/all_gather | solution.py:229
  7.9 148.8 %all-gather.17.cloned.1.call-start = ((), (), s32[]{:S(2)}) async-start(), calls=%async_computation.14 | async-start | bytes 2359296 | tf_op jit(solution)/shard_map/all_gather | solution.py:191
  8.7 186.1 %all-reduce.25.cloned.1.call-start = ((), (), s32[]{:S(2)}) async-start(), calls=%async_computation.15 | async-start | bytes 1048576 | tf_op jit(solution)/shard_map/psum | solution.py:211
  159.8 208.3 %all-gather.21.cloned.1.call-start = ((), (), s32[]{:S(2)}) async-start(), calls=%async_computation.17 | async-start | bytes 9437184 | tf_op jit(solution)/shard_map/all_gather | solution.py:191
  160.4 370.2 %all-reduce.27.cloned.1.call-start = ((), (), s32[]{:S(2)}) async-start(), calls=%async_computation.18 | async-start | bytes 1048576 | tf_op jit(solution)/shard_map/psum | solution.py:211
  371.0 160.8 %all-gather.23.cloned.1.call-start = ((), (), s32[]{:S(2)}) async-start(), calls=%async_computation.19 | async-start | bytes 1179648 | tf_op jit(solution)/shard_map/all_gather | solution.py:191
  371.7 219.1 %all-reduce.29.cloned.1.call-start = ((), (), s32[]{:S(2)}) async-start(), calls=%async_computation.20 | async-start | bytes 2097152 | tf_op jit(solution)/shard_map/psum | solution.py:211
  735.5 126.0 %all-gather.33.cloned.1.call-start = ((), (), s32[]{:S(2)}) async-start(), calls=%async_computation.40 | async-start | bytes 2621440 | tf_op jit(solution)/shard_map/all_gather | solution.py:218
  738.1 147.6 %all-gather.27.cloned.1.call-start = ((), (), s32[]{:S(2)}) async-start(), calls=%async_computation.28 | async-start | bytes 2621440 | tf_op jit(solution)/shard_map/all_gather | solution.py:218
  771.2 174.9 %all-gather.31.cloned.1.call-start = ((), (), s32[]{:S(2)}) async-start(), calls=%async_computation.32 | async-start | bytes 10485760 | tf_op jit(solution)/shard_map/all_gather | solution.py:218
  773.4 237.6 %reduce-scatter.32.cloned.1.call-start = ((), (), s32[]{:S(2)}) async-start(), calls=%async_computation.37 | async-start | bytes 147456 | tf_op jit(solution)/shard_map/reduce_scatter | solution.py:214
  775.1 300.0 %reduce-scatter.30.cloned.1.call-start = ((), (), s32[]{:S(2)}) async-start(), calls=%async_computation.36 | async-start | bytes 147456 | tf_op jit(solution)/shard_map/reduce_scatter | solution.py:214
  776.1 363.1 %reduce-scatter.28.cloned.1.call-start = ((), (), s32[]{:S(2)}) async-start(), calls=%async_computation.35 | async-start | bytes 147456 | tf_op jit(solution)/shard_map/reduce_scatter | solution.py:214
  777.2 426.6 %reduce-scatter.36.cloned.1.call-start = ((), (), s32[]{:S(2)}) async-start(), calls=%async_computation.39 | async-start | bytes 589824 | tf_op jit(solution)/shard_map/reduce_scatter | solution.py:214
  778.9 489.0 %reduce-scatter.26.cloned.1.call-start = ((), (), s32[]{:S(2)}) async-start(), calls=%async_computation.34 | async-start | bytes 294912 | tf_op jit(solution)/shard_map/reduce_scatter | solution.py:214
  780.9 551.3 %reduce-scatter.34.cloned.1.call-start = ((), (), s32[]{:S(2)}) async-start(), calls=%async_computation.38 | async-start | bytes 589824 | tf_op jit(solution)/shard_map/reduce_scatter | solution.py:219
  792.2 585.3 %all-reduce.37.cloned.1.call-start = ((), (), s32[]{:S(2)}) async-start(), calls=%async_computation.42 | async-start | bytes 3145728 | tf_op jit(solution)/shard_map/psum | solution.py:211
  799.4 644.2 %reduce-scatter.18.cloned.1.call-start = ((), (), s32[]{:S(2)}) async-start(), calls=%async_computation.27 | async-start | bytes 589824 | tf_op jit(solution)/shard_map/reduce_scatter | solution.py:214
  800.6 707.8 %reduce-scatter.14.cloned.1.call-start = ((), (), s32[]{:S(2)}) async-start(), calls=%async_computation.25 | async-start | bytes 589824 | tf_op jit(solution)/shard_map/reduce_scatter | solution.py:214
  801.8 771.8 %reduce-scatter.16.cloned.1.call-start = ((), (), s32[]{:S(2)}) async-start(), calls=%async_computation.26 | async-start | bytes 589824 | tf_op jit(solution)/shard_map/reduce_scatter | solution.py:214
  803.0 787.7 %all-gather.29.cloned.1.call-start = ((), (), s32[]{:S(2)}) async-start(), calls=%async_computation.31 | async-start | bytes 1310720 | tf_op jit(solution)/shard_map/all_gather | solution.py:215
  838.5 823.5 %reduce-scatter.38.cloned.1.call-start = ((), (), s32[]{:S(2)}) async-start(), calls=%async_computation.41 | async-start | bytes 2359296 | tf_op jit(solution)/shard_map/reduce_scatter | solution.py:219
  861.6 870.5 %reduce-scatter.20.cloned.1.call-start = ((), (), s32[]{:S(2)}) async-start(), calls=%async_computation.29 | async-start | bytes 2359296 | tf_op jit(solution)/shard_map/reduce_scatter | solution.py:219
  885.7 997.9 %reduce-scatter.24.cloned.1.call-start = ((), (), s32[]{:S(2)}) async-start(), calls=%async_computation.33 | async-start | bytes 9437184 | tf_op jit(solution)/shard_map/reduce_scatter | solution.py:219
  (186 other events, 6467.5 us)
Sparse Core Ops, SparseCore 0:
  31.2 57.0 all-gather.16
  193.4 49.2 all-gather.18
  244.6 123.4 all-gather.20
  404.6 40.9 all-gather.22
  543.8 34.0 all-reduce.28
  580.2 49.5 all-gather.24
  634.5 34.5 all-reduce.30
  686.2 36.4 all-reduce.32
  732.4 33.5 all-reduce.34
  770.5 67.8 reduce-scatter.21
  887.7 58.2 all-gather.30
  950.1 60.8 reduce-scatter.31
  1015.1 59.8 reduce-scatter.29
  1079.3 59.8 reduce-scatter.27
  1142.7 60.9 reduce-scatter.35
  1207.7 60.1 reduce-scatter.25
  1271.3 60.9 reduce-scatter.33
  1335.5 42.0 all-reduce.36
  1381.7 61.9 reduce-scatter.17
  1447.6 60.8 reduce-scatter.13
  1512.6 60.9 reduce-scatter.15
  1594.2 67.6 reduce-scatter.37
  1665.5 66.5 reduce-scatter.19
  1735.6 147.9 reduce-scatter.23
  (6 shorter events, 142.1 us)

commit v2 on v1

--- a/solution.py
+++ b/solution.py
@@ -1,8 +1,11 @@
+import functools
 import math
 
 import jax
 import jax.numpy as jnp
 from jax import lax
+from jax.experimental import pallas as pl
+from jax.experimental.pallas import tpu as pltpu
 from jax.sharding import PartitionSpec as P
 
 HEADS = 16
@@ -266,9 +269,1155 @@
     )
 
 
+MIB = 2**20
+DECODER_ROWS = 512
+PARTS = 4
+SIDES = 2
+VECTORS = 16
+
+
+class Split:
+    def __init__(self):
+        self.dp = lax.axis_index("dp")
+        self.blk = lax.axis_index("blk")
+        self.z = lax.div(self.dp, 2)
+        self.y = lax.rem(self.dp, 2)
+        self.x = lax.div(self.blk, 2)
+        self.core = lax.rem(self.blk, 2)
+        self.part = lax.rem(3 * self.blk, PARTS)
+        self.y_peer = (self.z * 2 + 1 - self.y, self.blk)
+        self.core_peer = (self.dp, self.x * 2 + 1 - self.core)
+        self.x_peer = (self.dp, (1 - self.x) * 2 + self.core)
+        self.far_peer = (self.dp, (1 - self.x) * 2 + 1 - self.core)
+        self.blk_peers = (self.core_peer, self.x_peer, self.far_peer)
+
+    def ahead(self, step):
+        return lax.rem(self.z + step, PARTS)
+
+    def behind(self, step):
+        return lax.rem(self.z + PARTS - step, PARTS)
+
+    def z_peer(self, step):
+        return (self.ahead(step) * 2 + self.y, self.blk)
+
+
+def remote(source, target, sent, received, device):
+    return pltpu.make_async_remote_copy(
+        src_ref=source, dst_ref=target, send_sem=sent, recv_sem=received,
+        device_id=device, device_id_type=pl.DeviceIdType.MESH,
+    )
+
+
+def span(at, size):
+    return pl.ds(pl.multiple_of(at, size), size)
+
+
+class Columns:
+    def __init__(self, split, whole, rows, local, sems, columns=None):
+        self.split, self.whole, self.rows, self.local = split, whole, rows, local
+        self.columns = columns
+        self.z_sent, self.z_got, self.y_sent, self.y_got = sems
+
+    def block(self, z, y):
+        rows = span((z * 2 + y) * self.rows, self.rows)
+        if self.columns is None:
+            return self.whole.at[rows]
+        return self.whole.at[rows, self.columns]
+
+    def own(self):
+        return self.block(self.split.z, self.split.y)
+
+    def z_copy(self, step):
+        s = self.split
+        return remote(self.own(), self.own(), self.z_sent.at[step - 1],
+                      self.z_got.at[step - 1], s.z_peer(step))
+
+    def z_arrival(self, step):
+        s = self.split
+        block = self.block(s.behind(step), s.y)
+        return remote(block, block, self.z_sent.at[step - 1], self.z_got.at[step - 1],
+                      s.z_peer(step))
+
+    def y_copy(self, step):
+        s = self.split
+        block = self.block(s.behind(step), s.y)
+        return remote(block, block, self.y_sent.at[step], self.y_got.at[step], s.y_peer)
+
+    def y_arrival(self, step):
+        s = self.split
+        block = self.block(s.behind(step), 1 - s.y)
+        return remote(block, block, self.y_sent.at[step], self.y_got.at[step], s.y_peer)
+
+    def fetch(self):
+        for copy in self.local:
+            copy.start()
+
+    def send(self):
+        for copy in self.local:
+            copy.wait()
+        for step in (1, 2, 3):
+            self.z_copy(step).start()
+        self.y_copy(0).start()
+
+    def forward(self):
+        for step in (1, 2, 3):
+            self.z_arrival(step).wait_recv()
+            self.y_copy(step).start()
+
+    def finish(self):
+        for step in range(PARTS):
+            self.y_arrival(step).wait_recv()
+
+    def drain(self):
+        for step in (1, 2, 3):
+            self.z_copy(step).wait_send()
+        for step in range(PARTS):
+            self.y_copy(step).wait_send()
+
+
+class Rows:
+    def __init__(self, split, whole, rows, local, sems):
+        self.split, self.whole, self.rows, self.local = split, whole, rows, local
+        self.z_sent, self.z_got, self.y_sent, self.y_got = sems
+
+    def block(self, y):
+        return self.whole.at[span(y * self.rows, self.rows)]
+
+    def z_copy(self, step):
+        s = self.split
+        return remote(self.block(s.y), self.block(s.y), self.z_sent.at[step - 1],
+                      self.z_got.at[0], s.z_peer(step))
+
+    def y_copy(self):
+        s = self.split
+        return remote(self.block(s.y), self.block(s.y), self.y_sent.at[0],
+                      self.y_got.at[0], s.y_peer)
+
+    def fetch(self):
+        @pl.when(self.split.z == self.split.part)
+        def _():
+            self.local.start()
+
+    def send(self):
+        @pl.when(self.split.z == self.split.part)
+        def _():
+            self.local.wait()
+            for step in (1, 2, 3):
+                self.z_copy(step).start()
+
+    def forward(self):
+        @pl.when(self.split.z != self.split.part)
+        def _():
+            self.z_copy(1).wait_recv()
+        self.y_copy().start()
+
+    def finish(self):
+        s = self.split
+        block = self.block(1 - s.y)
+        remote(block, block, self.y_sent.at[0], self.y_got.at[0], s.y_peer).wait_recv()
+
+    def drain(self):
+        @pl.when(self.split.z == self.split.part)
+        def _():
+            for step in (1, 2, 3):
+                self.z_copy(step).wait_send()
+        self.y_copy().wait_send()
+
+
+def each(count, step, body):
+    @pl.loop(0, count // step)
+    def _(at):
+        body(pl.ds(pl.multiple_of(at * step, step), step))
+
+
+class ColumnSum:
+    def __init__(self, split, grad, met, came, done, sems, step):
+        self.split, self.grad, self.met, self.came, self.done = split, grad, met, came, done
+        self.y_sent, self.y_got, self.z_sent, self.z_got, self.b_sent, self.b_got = sems
+        self.step = step
+
+    def y_copy(self):
+        s = self.split
+        return remote(self.grad.at[:, 1 - s.y], self.met, self.y_sent, self.y_got, s.y_peer)
+
+    def z_copy(self, step):
+        s = self.split
+        return remote(self.met.at[s.ahead(step)], self.came.at[step - 1],
+                      self.z_sent.at[step - 1], self.z_got.at[step - 1], s.z_peer(step))
+
+    def b_copy(self, which):
+        s = self.split
+        block = self.done.at[s.blk]
+        return remote(block, block, self.b_sent.at[which], self.b_got.at[which],
+                      s.blk_peers[which])
+
+    def b_arrival(self, which):
+        s = self.split
+        block = self.done.at[s.blk_peers[which][1]]
+        return remote(block, block, self.b_sent.at[which], self.b_got.at[which],
+                      s.blk_peers[which])
+
+    def start(self):
+        self.y_copy().start()
+
+    def add(self, z):
+        def body(rows):
+            both = self.grad[z, self.split.y, rows].astype(F32) + self.met[z, rows].astype(F32)
+            self.met[z, rows] = both.astype(self.met.dtype)
+        each(self.met.shape[1], self.step, body)
+
+    def middle(self):
+        self.y_copy().wait_recv()
+        for step in (1, 2, 3):
+            self.add(self.split.ahead(step))
+            self.z_copy(step).start()
+
+    def total(self, store):
+        s = self.split
+        for step in (1, 2, 3):
+            self.z_copy(step).wait_recv()
+
+        def body(rows):
+            whole = self.grad[s.z, s.y, rows].astype(F32) + self.met[s.z, rows].astype(F32)
+            for step in range(3):
+                whole = whole + self.came[step, rows].astype(F32)
+            store(rows, whole)
+        each(self.met.shape[1], self.step, body)
+
+    def last(self):
+        def store(rows, whole):
+            self.done[self.split.blk, rows] = whole.astype(self.done.dtype)
+        self.total(store)
+        for which in range(3):
+            self.b_copy(which).start()
+
+    def close(self):
+        for which in range(3):
+            self.b_arrival(which).wait_recv()
+        for which in range(3):
+            self.b_copy(which).wait_send()
+        self.drain()
+
+    def drain(self):
+        self.y_copy().wait_send()
+        for step in (1, 2, 3):
+            self.z_copy(step).wait_send()
+
+
+class RowSum:
+    def __init__(self, split, grad, met, came, done, sems, step):
+        self.split, self.grad, self.met, self.came, self.done = split, grad, met, came, done
+        self.y_sent, self.y_got, self.z_sent, self.z_got, self.b_sent, self.b_got = sems
+        self.step = step
+        s = split
+        self.slot = lax.rem(s.part + PARTS - s.z + 3, PARTS)
+        self.home = (s.part * 2 + s.y, s.blk)
+
+    def y_copy(self):
+        s = self.split
+        return remote(self.grad.at[1 - s.y], self.met, self.y_sent, self.y_got, s.y_peer)
+
+    def z_copy(self):
+        return remote(self.met, self.came.at[self.slot], self.z_sent.at[0],
+                      self.z_got.at[self.slot], self.home)
+
+    def b_copy(self, which):
+        return remote(self.done, self.done, self.b_sent.at[which], self.b_got.at[0],
+                      self.split.blk_peers[which])
+
+    def start(self):
+        self.y_copy().start()
+
+    def middle(self):
+        s = self.split
+        self.y_copy().wait_recv()
+
+        @pl.when(s.z != s.part)
+        def _():
+            def body(rows):
+                both = self.grad[s.y, rows].astype(F32) + self.met[rows].astype(F32)
+                self.met[rows] = both.astype(self.met.dtype)
+            each(self.met.shape[0], self.step, body)
+            self.z_copy().start()
+
+    def last(self):
+        s = self.split
+
+        @pl.when(s.z == s.part)
+        def _():
+            for step in range(3):
+                remote(self.met, self.came.at[step], self.z_sent.at[0],
+                       self.z_got.at[step], s.y_peer).wait_recv()
+
+            def body(rows):
+                whole = self.grad[s.y, rows].astype(F32) + self.met[rows].astype(F32)
+                for step in range(3):
+                    whole = whole + self.came[step, rows].astype(F32)
+                self.done[rows] = whole.astype(self.done.dtype)
+            each(self.met.shape[0], self.step, body)
+            for which in range(3):
+                self.b_copy(which).start()
+
+    def close(self):
+        s = self.split
+        self.y_copy().wait_send()
+
+        @pl.when(s.z == s.part)
+        def _():
+            for which in range(3):
+                self.b_copy(which).wait_send()
+
+        @pl.when(s.z != s.part)
+        def _():
+            self.z_copy().wait_send()
+            self.b_copy(0).wait_recv()
+
+
+class Total:
+    def __init__(self, split, part, met, out, came, whole, sems, slot):
+        self.split, self.part, self.met, self.out = split, part, met, out
+        self.came, self.whole = came.at[slot], whole
+        self.sent, self.got = sems
+
+    def first_copy(self):
+        s = self.split
+        return remote(self.part.at[1 - s.core], self.met, self.sent.at[0], self.got.at[0],
+                      s.core_peer)
+
+    def second_copy(self):
+        return remote(self.out, self.came, self.sent.at[1], self.got.at[1], self.split.x_peer)
+
+    def third_copy(self, half):
+        s = self.split
+        return remote(self.whole.at[half], self.whole.at[half], self.sent.at[2],
+                      self.got.at[2], s.core_peer)
+
+    def start(self):
+        self.first_copy().start()
+
+    def middle(self):
+        s = self.split
+        self.first_copy().wait_recv()
+
+        def body(rows):
+            self.out[rows] = (self.part[s.core, rows] + self.met[rows]).astype(BF16)
+        each(self.out.shape[0], 32, body)
+        self.second_copy().start()
+
+    def end(self):
+        s = self.split
+        self.second_copy().wait_recv()
+
+        def body(rows):
+            self.whole[s.core, rows] = self.out[rows].astype(F32) + self.came[rows].astype(F32)
+        each(self.out.shape[0], 32, body)
+        self.third_copy(s.core).start()
+        self.third_copy(1 - s.core).wait_recv()
+        self.first_copy().wait_send()
+        self.second_copy().wait_send()
+        self.third_copy(s.core).wait_send()
+
+
+def head_mask(width, size, head):
+    lanes = lax.broadcasted_iota(jnp.int32, (1, width), 1)
+    return lax.div(lanes, size) == head
+
+
+def keep(mask, values):
+    return jnp.where(mask, values, jnp.zeros_like(values))
+
+
+class Block:
+    def __init__(self, rows, width, heads, size, names, refs, vectors):
+        self.rows, self.width, self.heads, self.size = rows, width, heads, size
+        self.share = heads * size
+        self.scaling = 1.0 / math.sqrt(size)
+        self.refs = refs
+        self.vectors = vectors
+        self.name = names
+        self.tile = 32 * 1024 // width
+
+    def ref(self, name):
+        return self.refs[self.name + name]
+
+    def row(self, at):
+        return self.refs["gains"][self.vectors + at:self.vectors + at + 1, 0:self.width]
+
+    def norm(self, first):
+        unit, scale = self.ref("unit_a" if first else "unit_b"), self.ref(
+            "scale_a" if first else "scale_b")
+        out = self.ref("normed" if first else "lifted")
+        gain, bias = self.row(0 if first else 2), self.row(1 if first else 3)
+        residual = self.ref("residual")
+
+        def body(rows):
+            one, size = norm_parts(residual[rows])
+            unit[rows] = one
+            scale[rows] = size
+            out[rows] = (one * gain + bias).astype(BF16)
+        each(self.rows, self.tile, body)
+
+    def project(self):
+        normed, mixed, weight = self.ref("normed"), self.ref("qkv"), self.ref("w_qkv")
+
+        def body(rows):
+            mixed[rows] = dot(normed[rows], weight[...]).astype(BF16)
+        each(self.rows, 128, body)
+
+    def parts(self, rows):
+        share, qkv = self.share, self.ref("qkv")
+        return (qkv[rows, 0:share], qkv[rows, share:2 * share], qkv[rows, 2 * share:3 * share])
+
+    def attend(self, ids_column, ids_row):
+        probs, mixture = self.ref("probs"), self.ref("mixture")
+        everything = pl.ds(0, self.rows)
+
+        def body(queries):
+            query = self.parts(queries)[0]
+            unused, key_rows, values = self.parts(everything)
+            allowed = ids_column[...] == ids_row[:, queries]
+
+            def one(head, mixed):
+                mask = head_mask(self.share, self.size, head)
+                scores = jnp.where(
+                    allowed, dot_b(keep(mask, key_rows), query) * self.scaling, MASKED_SCORE
+                )
+                exponent = jnp.exp(scores - jnp.max(scores, axis=0, keepdims=True))
+                softmaxed = exponent * (1.0 / jnp.sum(exponent, axis=0, keepdims=True))
+                probs[head, :, queries] = softmaxed
+                return mixed + dot_t(keep(mask, values), softmaxed.astype(BF16))
+
+            mixed = lax.fori_loop(0, self.heads, one, jnp.zeros((self.share, 128), F32))
+            mixture[queries] = mixed.T.astype(BF16)
+        each(self.rows, 128, body)
+
+    def product(self, left, weight, target, back=False):
+        shape = target.shape
+        half = shape[1]
+
+        def body(rows):
+            made = (dot_b if back else dot)(left[rows], weight[...])
+            at = lax.div(rows.start, half)
+            target[at, pl.ds(pl.multiple_of(lax.rem(rows.start, half), 64), 64)] = made
+        each(self.rows, 64, body)
+
+    def half(self, ref, rows):
+        size = ref.shape[1]
+        start = pl.multiple_of(lax.rem(rows.start, size), rows.size)
+        return ref[lax.div(rows.start, size), pl.ds(start, rows.size)]
+
+    def add_total(self, whole):
+        residual = self.ref("residual")
+
+        def body(rows):
+            residual[rows] = residual[rows] + self.half(whole, rows)
+        each(self.rows, self.tile, body)
+
+    def expand(self):
+        lifted, weight = self.ref("lifted"), self.ref("w_up")
+        hidden, slope = self.ref("hidden"), self.ref("slope")
+
+        def body(rows):
+            def inner(columns):
+                made, gradient = gelu_both(dot(lifted[rows], weight[:, columns]))
+                hidden[rows, columns] = made.astype(BF16)
+                slope[rows, columns] = gradient
+            each(weight.shape[1], 256, inner)
+        each(self.rows, 128, body)
+
+    def back_hidden(self, branch):
+        weight, slope, grad = self.ref("w_down"), self.ref("slope"), self.ref("grad_upper")
+
+        def body(rows):
+            def inner(columns):
+                made = dot_b(branch[rows], weight[columns])
+                grad[rows, columns] = (made * slope[rows, columns]).astype(BF16)
+            each(weight.shape[0], 256, inner)
+        each(self.rows, 128, body)
+
+    def norm_back(self, whole, first, out):
+        unit, scale = self.ref("unit_a" if first else "unit_b"), self.ref(
+            "scale_a" if first else "scale_b")
+        gain, grad = self.row(0 if first else 2), self.ref("grad")
+
+        def body(at, sums):
+            rows = pl.ds(pl.multiple_of(at * self.tile, self.tile), self.tile)
+            moved, gains, biases = norm_back(self.half(whole, rows), unit[rows], scale[rows], gain)
+            new = grad[rows] + moved
+            grad[rows] = new
+            out[rows] = new.astype(BF16)
+            return sums[0] + gains, sums[1] + biases
+        zero = jnp.zeros((1, self.width), F32)
+        return lax.fori_loop(0, self.rows // self.tile, body, (zero, zero))
+
+    def back_mixture(self, branch):
+        weight, grad = self.ref("w_out"), self.ref("grad_mixture")
+
+        def body(rows):
+            grad[rows] = dot_b(branch[rows], weight[...]).astype(BF16)
+        each(self.rows, 128, body)
+
+    def attend_back(self):
+        probs, grad_mixture, grads = self.ref("probs"), self.ref("grad_mixture"), self.ref(
+            "grad_qkv")
+        key_sum, value_sum = self.ref("key_sum"), self.ref("value_sum")
+        share, everything = self.share, pl.ds(0, self.rows)
+        key_sum[...] = jnp.zeros(key_sum.shape, F32)
+        value_sum[...] = jnp.zeros(value_sum.shape, F32)
+
+        def body(queries):
+            query = self.parts(queries)[0]
+            unused, key_rows, values = self.parts(everything)
+            grad_rows = grad_mixture[queries]
+
+            def one(head, total):
+                mask = head_mask(share, self.size, head)
+                softmaxed = probs[head, :, queries]
+                grad_probs = dot_b(keep(mask, values), grad_rows)
+                value_sum[...] += dot(softmaxed.astype(BF16), keep(mask, grad_rows))
+                delta = jnp.sum(softmaxed * grad_probs, axis=0, keepdims=True)
+                grad_scores = (softmaxed * (grad_probs - delta)).astype(BF16)
+                key_sum[...] += dot(grad_scores, keep(mask, query))
+                return total + dot_t(keep(mask, key_rows), grad_scores)
+
+            total = lax.fori_loop(0, self.heads, one, jnp.zeros((share, 128), F32))
+            grads[queries, 0:share] = (total.T * self.scaling).astype(BF16)
+        each(self.rows, 128, body)
+
+        def close(rows):
+            grads[rows, share:2 * share] = (key_sum[rows] * self.scaling).astype(BF16)
+            grads[rows, 2 * share:3 * share] = value_sum[rows].astype(BF16)
+        each(self.rows, 128, close)
+
+
+def weight_grad(left, right, target):
+    if len(target.shape) == 4:
+        parts, sides, rows, width = target.shape
+        if rows >= 128:
+            @pl.loop(0, parts * sides)
+            def _(at):
+                block = dot_t(left[:, span(at * rows, rows)], right[...])
+                target[lax.div(at, sides), lax.rem(at, sides)] = block.astype(BF16)
+        else:
+            @pl.loop(0, parts)
+            def _(at):
+                block = dot_t(left[:, span(at * sides * rows, sides * rows)], right[...])
+                target[at] = block.reshape(sides, rows, width).astype(BF16)
+    else:
+        sides, rows, width = target.shape
+        if rows >= 128:
+            @pl.loop(0, sides)
+            def _(at):
+                block = dot_t(left[:, span(at * rows, rows)], right[...])
+                target[at] = block.astype(BF16)
+        else:
+            block = dot_t(left[...], right[...])
+            target[...] = block.reshape(sides, rows, width).astype(BF16)
+
+
+def vector_store(target, at, row, whole):
+    for owner in range(8):
+        block = owner if whole else owner // 2
+        target[owner // 2, owner % 2, at:at + 1, :] = row[:, 128 * block:128 * block + 128]
+
+
+COLUMN_UNITS = ("e_qkv", "e_up", "e_down", "embed", "d_qkv", "d_up")
+ROW_UNITS = ("e_out", "d_out", "d_down")
+MESSAGES = COLUMN_UNITS + ROW_UNITS
+
+
+def unit_shapes(width, dec_width, hidden, dec_hidden):
+    return {
+        "e_qkv": (width // 8, 3 * width // 4),
+        "e_up": (width // 8, hidden // 4),
+        "e_down": (hidden // 32, width),
+        "embed": (width // 8, dec_width // 4),
+        "d_qkv": (dec_width // 8, 3 * dec_width // 4),
+        "d_up": (dec_width // 8, dec_hidden // 4),
+        "e_out": (width // 8, width),
+        "d_out": (dec_width // 8, dec_width),
+        "d_down": (dec_hidden // 8, dec_width),
+    }
+
+
+def scratch_table(width, dec_width, hidden, dec_hidden, rows, shown):
+    units = unit_shapes(width, dec_width, hidden, dec_hidden)
+    table = {}
+    for name in COLUMN_UNITS:
+        height, columns = units[name]
+        if name != "embed":
+            table["w_" + name] = ((8 * height, columns), BF16)
+        table["g_" + name] = ((PARTS, SIDES, height, columns), BF16)
+        table["m_" + name] = ((PARTS, height, columns), BF16)
+        table["c_" + name] = ((3, height, columns), BF16)
+    table["w_embed"] = ((width, dec_width), BF16)
+    for name in ROW_UNITS:
+        height, columns = units[name]
+        table["w_" + name] = ((2 * height, columns), BF16)
+        table["g_" + name] = ((SIDES, height, columns), BF16)
+        table["m_" + name] = ((height, columns), BF16)
+        table["c_" + name] = ((3, height, columns), BF16)
+    table["w_vector"] = ((8 * VECTORS, 128), BF16)
+    table["g_vector"] = ((PARTS, SIDES, VECTORS, 128), F32)
+    table["m_vector"] = ((PARTS, VECTORS, 128), F32)
+    table["c_vector"] = ((3, VECTORS, 128), F32)
+    table["gains"] = ((VECTORS, width), F32)
+    table["group"] = ((rows, width), BF16)
+    table["cotangents"] = ((rows, dec_width), BF16)
+    for key, count, wide, deep, heads, size in (
+        ("e_", shown, width, hidden // 4, 4, 64), ("d_", rows, dec_width, dec_hidden // 4, 4, 32)
+    ):
+        share = heads * size
+        for name, shape, kind in (
+            ("residual", (count, wide), F32), ("unit_a", (count, wide), F32),
+            ("unit_b", (count, wide), F32), ("scale_a", (count, 1), F32),
+            ("scale_b", (count, 1), F32), ("normed", (count, wide), BF16),
+            ("lifted", (count, wide), BF16), ("qkv", (count, 3 * share), BF16),
+            ("probs", (heads, count, count), F32), ("mixture", (count, share), BF16),
+            ("hidden", (count, deep), BF16), ("slope", (count, deep), F32),
+            ("grad_upper", (count, deep), BF16), ("grad", (count, wide), F32),
+            ("grad_mixture", (count, share), BF16), ("grad_qkv", (count, 3 * share), BF16),
+            ("key_sum", (count, share), F32), ("value_sum", (count, share), F32),
+            ("branch", (count, wide), BF16),
+            ("part", (2, count // 2, wide), F32), ("met", (count // 2, wide), F32),
+            ("out", (count // 2, wide), BF16), ("came", (2, count // 2, wide), BF16),
+            ("whole", (2, count // 2, wide), F32),
+        ):
+            table[key + name] = (shape, kind)
+    table["last_part"] = ((2, 2, rows // 4, dec_width), F32)
+    table["last_met"] = ((2, rows // 4, dec_width), F32)
+    table["last_out"] = ((rows // 4, dec_width), BF16)
+    table["last_came"] = ((rows // 4, dec_width), BF16)
+    table["lowered"] = ((shown, width), BF16)
+    table["picked"] = ((shown, dec_width), BF16)
+    return table
+
+
+INPUTS = (
+    "rank_row", "rank_column", "ids_row", "ids_column", "packed_row", "packed_column",
+    "code", "dec_code", "vector",
+    "patches", "cotangent", "query", "key", "value", "out", "up", "down", "embed",
+    "dec_query", "dec_key", "dec_value", "dec_out", "dec_up", "dec_down",
+)
+RESULTS = ("decoded", "grad_patches", "grad_vector") + MESSAGES
+SEMAPHORES = {
+    "local": (40,),
+    "z_sent": (10, 3), "z_got": (10, 3), "y_sent": (10, 4), "y_got": (10, 4),
+    "gy_sent": (10,), "gy_got": (10,), "gz_sent": (10, 3), "gz_got": (10, 3),
+    "gb_sent": (10, 3), "gb_got": (10, 3),
+    "p_sent": (3,), "p_got": (3,), "c_sent": (3,), "c_got": (3,),
+    "e_sent": (3,), "e_got": (3,), "t_sent": (8, 3), "t_got": (8, 3),
+}
+
+
+def main_kernel(names, *refs):
+    ref = dict(zip(names, refs))
+    s = Split()
+    shown, width = ref["code"].shape
+    rows, dec_width = ref["dec_code"].shape
+    own = ref["patches"].shape[0]
+    sem = {name: ref["s_" + name] for name in SEMAPHORES}
+    counter = [0]
+
+    def local(source, target):
+        at = counter[0]
+        counter[0] = at + 1
+        return pltpu.make_async_copy(source, target, sem["local"].at[at])
+
+    barrier = pltpu.get_barrier_semaphore()
+    peers = [s.z_peer(step) for step in (1, 2, 3)] + [s.y_peer] + list(s.blk_peers)
+    for peer in peers:
+        pl.semaphore_signal(barrier, inc=1, device_id=peer, device_id_type=pl.DeviceIdType.MESH)
+
+    order = ("vector",) + MESSAGES
+    units = {}
+    for at, name in enumerate(order):
+        sems = tuple(sem[kind].at[at] for kind in ("z_sent", "z_got", "y_sent", "y_got"))
+        whole = ref["w_" + name]
+        if name == "vector":
+            copies = [local(ref["vector"], whole.at[span(s.dp * VECTORS, VECTORS)])]
+            units[name] = Columns(s, whole, VECTORS, copies, sems)
+        elif name in ROW_UNITS:
+            source = ref[{"e_out": "out", "d_out": "dec_out", "d_down": "dec_down"}[name]]
+            height = source.shape[0]
+            copy = local(source, whole.at[span(s.y * height, height)])
+            units[name] = Rows(s, whole, height, copy, sems)
+        else:
+            height = ref["g_" + name].shape[2]
+            mine = span(s.dp * height, height)
+            columns = None
+            if name in ("e_qkv", "d_qkv"):
+                kinds = ("query", "key", "value")
+                if name == "d_qkv":
+                    kinds = ("dec_query", "dec_key", "dec_value")
+                size = ref[kinds[0]].shape[1] // PARTS
+                copies = [
+                    local(ref[kind].at[:, span(s.part * size, size)],
+                          whole.at[mine, pl.ds(place * size, size)])
+                    for place, kind in enumerate(kinds)
+                ]
+            elif name == "e_up":
+                size = height
+                copies = [
+                    local(ref["up"].at[:, span((owner * PARTS + s.blk) * size, size)],
+                          whole.at[mine, pl.ds(owner * size, size)])
+                    for owner in range(8)
+                ]
+            elif name == "e_down":
+                copies = [local(ref["down"].at[span(s.blk * height, height)], whole.at[mine])]
+            elif name == "embed":
+                size = dec_width // PARTS
+                columns = span(s.part * size, size)
+                copies = [local(ref["embed"].at[:, columns], whole.at[mine, columns])]
+            else:
+                size = ref["dec_up"].shape[1] // PARTS
+                copies = [local(ref["dec_up"].at[:, span(s.part * size, size)], whole.at[mine])]
+            units[name] = Columns(s, whole, height, copies, sems, columns)
+
+    sums = {}
+    for at, name in enumerate(order):
+        sems = tuple(
+            sem[kind].at[at]
+            for kind in ("gy_sent", "gy_got", "gz_sent", "gz_got", "gb_sent", "gb_got")
+        )
+        kind = RowSum if name in ROW_UNITS else ColumnSum
+        done = None if name == "vector" else ref["o_" + name]
+        wide = ref["g_" + name].shape[-1]
+        sums[name] = kind(s, ref["g_" + name], ref["m_" + name], ref["c_" + name], done, sems,
+                          16 if wide > 512 else 32 if name != "vector" else 8)
+
+    totals = []
+    for at in range(7):
+        key, slot = ("e_", at % 2) if at in (0, 1, 5, 6) else ("d_", at % 2)
+        totals.append(Total(
+            s, *(ref[key + name] for name in ("part", "met", "out", "came", "whole")),
+            (sem["t_sent"].at[at], sem["t_got"].at[at]), slot,
+        ))
+
+    encoder = Block(shown, width, 4, 64, "e_", ref, 0)
+    decoder = Block(rows, dec_width, 4, 32, "d_", ref, 5)
+    for block, key in ((encoder, "e_"), (decoder, "d_")):
+        for short, long in (("w_qkv", "qkv"), ("w_out", "out"), ("w_up", "up"),
+                            ("w_down", "down")):
+            ref[key + short] = ref["w_" + key + long]
+
+    first = ("vector", "e_qkv", "e_out", "embed", "e_up")
+    for name in first:
+        units[name].fetch()
+    mine = span(s.blk * own, own)
+    own_patches = local(ref["patches"], ref["group"].at[mine])
+    own_cotangents = local(ref["cotangent"], ref["cotangents"].at[mine])
+    own_patches.start()
+    own_cotangents.start()
+    for name in ("e_down", "d_qkv", "d_out", "d_up", "d_down"):
+        units[name].fetch()
+
+    pl.semaphore_wait(barrier, len(peers))
+
+    def shares(source, target, kind, which):
+        return remote(source, target.at[mine], sem[kind + "_sent"].at[which],
+                      sem[kind + "_got"].at[which], s.blk_peers[which])
+
+    def shares_arrival(source, target, kind, which):
+        place = span(s.blk_peers[which][1] * own, own)
+        return remote(source, target.at[place], sem[kind + "_sent"].at[which],
+                      sem[kind + "_got"].at[which], s.blk_peers[which])
+
+    for name in ("vector", "e_qkv", "e_out"):
+        units[name].send()
+    for which in range(3):
+        shares(ref["patches"], ref["group"], "p", which).start()
+    for name in ("embed", "e_up"):
+        units[name].send()
+    own_patches.wait()
+    for which in range(3):
+        shares_arrival(ref["patches"], ref["group"], "p", which).wait_recv()
+
+    places = (
+        lax.broadcasted_iota(jnp.int32, (shown, rows), 0) == ref["rank_row"][...]
+    ).astype(BF16)
+    residual = ref["e_residual"]
+
+    def place_patches(columns):
+        residual[:, columns] = dot(places, ref["group"][:, columns]) + ref["code"][:, columns]
+    each(width, 256, place_patches)
+
+    units["vector"].forward()
+    units["vector"].finish()
+    vectors = ref["w_vector"][...].astype(F32)
+    gains = ref["gains"]
+    for at in range(9):
+        for owner in range(8):
+            row = vectors[VECTORS * owner + at:VECTORS * owner + at + 1, :]
+            if at < 4:
+                gains[at:at + 1, 128 * owner:128 * owner + 128] = row
+            elif owner % 2 == 0:
+                pair = VECTORS * (owner + 1) + at
+                gains[at:at + 1, 64 * owner:64 * owner + 128] = row + vectors[pair:pair + 1, :]
+    encoder.norm(True)
+    for name in ("e_qkv", "e_out", "embed"):
+        units[name].forward()
+    units["e_qkv"].finish()
+    encoder.project()
+    encoder.attend(ref["packed_column"], ref["packed_row"])
+    units["e_out"].finish()
+    encoder.product(ref["e_mixture"], ref["w_e_out"], ref["e_part"])
+    totals[0].start()
+    units["e_down"].send()
+    for which in range(3):
+        shares(ref["cotangent"], ref["cotangents"], "c", which).start()
+    totals[0].middle()
+    units["embed"].finish()
+    totals[0].end()
+    encoder.add_total(ref["e_whole"])
+    encoder.norm(False)
+    columns = span(s.part * (dec_width // PARTS), dec_width // PARTS)
+
+    def embed_copy(which):
+        block = ref["w_embed"].at[:, columns]
+        return remote(block, block, sem["e_sent"].at[which], sem["e_got"].at[which],
+                      s.blk_peers[which])
+
+    def embed_arrival(which):
+        size = dec_width // PARTS
+        place = span(lax.rem(3 * s.blk_peers[which][1], PARTS) * size, size)
+        block = ref["w_embed"].at[:, place]
+        return remote(block, block, sem["e_sent"].at[which], sem["e_got"].at[which],
+                      s.blk_peers[which])
+
+    for which in range(3):
+        embed_copy(which).start()
+    units["e_up"].forward()
+    units["d_qkv"].send()
+    units["e_up"].finish()
+    encoder.expand()
+    units["e_down"].forward()
+    for name in ("d_out", "d_up"):
+        units[name].send()
+    units["e_down"].finish()
+    encoder.product(ref["e_hidden"], ref["w_e_down"], ref["e_part"])
+    totals[1].start()
+    units["d_qkv"].forward()
+    totals[1].middle()
+    units["d_down"].send()
+    units["d_out"].forward()
+    for which in range(3):
+        embed_arrival(which).wait_recv()
+    totals[1].end()
+    encoder.add_total(ref["e_whole"])
+
+    lowered = ref["lowered"]
+
+    def lower(part):
+        lowered[part] = residual[part].astype(BF16)
+    each(shown, 32, lower)
+    embedded = dot(lowered[...], ref["w_embed"][...])
+    high = embedded.astype(BF16)
+    low = (embedded - high.astype(F32)).astype(BF16)
+    token = gains[4:5, 0:dec_width]
+    start = ref["d_residual"]
+
+    def place_rows(part):
+        rank = ref["rank_column"][part]
+        here = (lax.broadcasted_iota(jnp.int32, (128, shown), 1) == rank).astype(BF16)
+        made = jnp.where(rank >= 0, dot(here, high) + dot(here, low), token)
+        start[part] = made + ref["dec_code"][part]
+    each(rows, 128, place_rows)
+    decoder.norm(True)
+    units["d_qkv"].finish()
+    decoder.project()
+    decoder.attend(ref["ids_column"], ref["ids_row"])
+    units["d_up"].forward()
+    units["d_out"].finish()
+    decoder.product(ref["d_mixture"], ref["w_d_out"], ref["d_part"])
+    totals[2].start()
+    totals[2].middle()
+    units["d_down"].forward()
+    totals[2].end()
+    decoder.add_total(ref["d_whole"])
+    decoder.norm(False)
+    units["d_up"].finish()
+    decoder.expand()
+    units["d_down"].finish()
+    quarter = rows // 4
+    last_part, last_met = ref["last_part"], ref["last_met"]
+
+    def last_product(part):
+        at = lax.div(part.start, 64)
+        made = dot(ref["d_hidden"][part], ref["w_d_down"][...])
+        per = quarter // 64
+        place = pl.ds(pl.multiple_of(lax.rem(at, per) * 64, 64), 64)
+        block = lax.div(at, per)
+        last_part[lax.div(block, 2), lax.rem(block, 2), place] = made
+    each(rows, 64, last_product)
+    last_sent, last_got = sem["t_sent"].at[7], sem["t_got"].at[7]
+    last_first = remote(last_part.at[:, 1 - s.core], last_met, last_sent.at[0], last_got.at[0],
+                        s.core_peer)
+    last_second = remote(ref["last_out"], ref["last_came"], last_sent.at[1], last_got.at[1],
+                         s.x_peer)
+    last_first.start()
+
+    own_cotangents.wait()
+    for which in range(3):
+        shares_arrival(ref["cotangent"], ref["cotangents"], "c", which).wait_recv()
+    cotangents, grad = ref["cotangents"], ref["d_grad"]
+    decoder.back_hidden(cotangents)
+    decoder.product(ref["d_grad_upper"], ref["w_d_up"], ref["d_part"], back=True)
+    totals[3].start()
+    last_first.wait_recv()
+
+    def last_add(part):
+        made = last_part[1 - s.x, s.core, part] + last_met[1 - s.x, part]
+        ref["last_out"][part] = made.astype(BF16)
+    each(quarter, 64, last_add)
+    totals[3].middle()
+    last_second.start()
+
+    def copy_grad(part):
+        grad[part] = cotangents[part].astype(F32)
+    each(rows, 64, copy_grad)
+    weight_grad(ref["d_hidden"], cotangents, ref["g_d_down"])
+    sums["d_down"].start()
+    weight_grad(ref["d_lifted"], ref["d_grad_upper"], ref["g_d_up"])
+    sums["d_up"].start()
+    totals[3].end()
+    vector_grad = ref["g_vector"]
+    vector_grad[...] = jnp.zeros(vector_grad.shape, F32)
+    gain, bias = decoder.norm_back(ref["d_whole"], False, ref["d_branch"])
+    vector_store(vector_grad, 7, gain, False)
+    vector_store(vector_grad, 8, bias, False)
+    decoder.back_mixture(ref["d_branch"])
+    decoder.attend_back()
+    sums["d_down"].middle()
+    decoder.product(ref["d_grad_qkv"], ref["w_d_qkv"], ref["d_part"], back=True)
+    totals[4].start()
+    sums["d_up"].middle()
+    totals[4].middle()
+    last_second.wait_recv()
+
+    def last_close(part):
+        made = last_part[s.x, s.core, part] + last_met[s.x, part]
+        before = ref["d_residual"][pl.ds(pl.multiple_of(s.blk * own + part.start, 64), 64)]
+        whole = made + ref["last_came"][part].astype(F32) + before
+        ref["decoded"][part] = whole.astype(BF16)
+    each(quarter, 64, last_close)
+    weight_grad(ref["d_mixture"], ref["d_branch"], ref["g_d_out"])
+    sums["d_out"].start()
+    weight_grad(ref["d_normed"], ref["d_grad_qkv"], ref["g_d_qkv"])
+    sums["d_qkv"].start()
+    totals[4].end()
+    gain, bias = decoder.norm_back(ref["d_whole"], True, ref["d_branch"])
+    vector_store(vector_grad, 5, gain, False)
+    vector_store(vector_grad, 6, bias, False)
+
+    def mask_sum(at, total):
+        part = pl.ds(pl.multiple_of(at * 64, 64), 64)
+        hidden_row = ref["rank_column"][part] < 0
+        return total + jnp.sum(jnp.where(hidden_row, grad[part], 0.0), axis=0, keepdims=True)
+    token_grad = lax.fori_loop(0, rows // 64, mask_sum, jnp.zeros((1, dec_width), F32))
+    vector_store(vector_grad, 4, token_grad, False)
+    picked = ref["picked"]
+    picked[...] = dot(places, ref["d_branch"][...]).astype(BF16)
+    grad = ref["e_grad"]
+
+    def back_embed(part):
+        made = dot_b(picked[...], ref["w_embed"][part])
+        grad[:, part] = made
+        ref["e_branch"][:, part] = made.astype(BF16)
+    each(width, 256, back_embed)
+
+    encoder.back_hidden(ref["e_branch"])
+    encoder.product(ref["e_grad_upper"], ref["w_e_up"], ref["e_part"], back=True)
+    totals[5].start()
+    for name in ("d_out", "d_qkv"):
+        sums[name].middle()
+    totals[5].middle()
+    for name in ("d_down", "d_up"):
+        sums[name].last()
+    weight_grad(ref["e_hidden"], ref["e_branch"], ref["g_e_down"])
+    sums["e_down"].start()
+    weight_grad(ref["e_lifted"], ref["e_grad_upper"], ref["g_e_up"])
+    sums["e_up"].start()
+    embed_columns = picked.at[:, columns]
+    weight_grad(lowered, embed_columns, ref["g_embed"])
+    sums["embed"].start()
+    totals[5].end()
+    gain, bias = encoder.norm_back(ref["e_whole"], False, ref["e_branch"])
+    vector_store(vector_grad, 2, gain, True)
+    vector_store(vector_grad, 3, bias, True)
+    encoder.back_mixture(ref["e_branch"])
+    encoder.attend_back()
+    encoder.product(ref["e_grad_qkv"], ref["w_e_qkv"], ref["e_part"], back=True)
+    totals[6].start()
+    weight_grad(ref["e_mixture"], ref["e_branch"], ref["g_e_out"])
+    sums["e_out"].start()
+    totals[6].middle()
+    weight_grad(ref["e_normed"], ref["e_grad_qkv"], ref["g_e_qkv"])
+    sums["e_qkv"].start()
+    totals[6].end()
+    gain, bias = encoder.norm_back(ref["e_whole"], True, ref["e_branch"])
+    vector_store(vector_grad, 0, gain, True)
+    vector_store(vector_grad, 1, bias, True)
+    sums["vector"].start()
+    sums["e_down"].middle()
+    for name in ("d_out", "d_qkv"):
+        sums[name].last()
+    rank = ref["rank_column"][mine]
+    here = (lax.broadcasted_iota(jnp.int32, (own, shown), 1) == rank).astype(BF16)
+
+    def place_grad(part):
+        values = grad[:, part]
+        top = values.astype(BF16)
+        rest = (values - top.astype(F32)).astype(BF16)
+        ref["grad_patches"][:, part] = dot(here, top) + dot(here, rest)
+    each(width, 256, place_grad)
+    for name in ("e_up", "embed", "e_out", "e_qkv", "vector"):
+        sums[name].middle()
+    for name in ("e_down", "e_up", "embed", "e_out", "e_qkv"):
+        sums[name].last()
+
+    def vector_out(part, whole):
+        ref["grad_vector"][part] = whole
+    sums["vector"].total(vector_out)
+    sums["vector"].drain()
+    for name in MESSAGES:
+        sums[name].close()
+    last_first.wait_send()
+    last_second.wait_send()
+    for name in order:
+        units[name].drain()
+    for which in range(3):
+        shares(ref["patches"], ref["group"], "p", which).wait_send()
+        shares(ref["cotangent"], ref["cotangents"], "c", which).wait_send()
+        embed_copy(which).wait_send()
+
+
+def unpack_kernel(names, *refs):
+    ref = dict(zip(names, refs))
+    side = lax.rem(lax.axis_index("dp"), 2)
+    ref["decoded"][...] = ref["i_decoded"][...]
+    ref["grad_patches"][...] = ref["i_grad_patches"][...]
+    vectors = ref["i_grad_vector"][...]
+    for at, name in enumerate(("e_gain_a", "e_bias_a", "e_gain_b", "e_bias_b")):
+        ref[name][...] = vectors[at:at + 1, :]
+    for at, name in enumerate(("mask", "d_gain_a", "d_bias_a", "d_gain_b", "d_bias_b")):
+        row = vectors[at + 4:at + 5, :]
+        ref[name][...] = jnp.where(side == 0, row[:, 0:64], row[:, 64:128])
+    for blk in range(PARTS):
+        part = 3 * blk % PARTS
+        for key in ("e_", "d_"):
+            size = ref[key + "query"].shape[1] // PARTS
+            for place, kind in enumerate(("query", "key", "value")):
+                ref[key + kind][:, part * size:(part + 1) * size] = ref["i_" + key + "qkv"][
+                    blk, :, place * size:(place + 1) * size].astype(F32)
+        size = ref["i_e_up"].shape[1]
+        for owner in range(8):
+            column = (owner * PARTS + blk) * size
+            ref["e_up"][:, column:column + size] = ref["i_e_up"][
+                blk, :, owner * size:(owner + 1) * size].astype(F32)
+        size = ref["i_e_down"].shape[1]
+        ref["e_down"][blk * size:(blk + 1) * size, :] = ref["i_e_down"][blk].astype(F32)
+        for name in ("embed", "d_up"):
+            size = ref["i_" + name].shape[2]
+            ref[name][:, part * size:(part + 1) * size] = ref["i_" + name][blk].astype(F32)
+    for name in ROW_UNITS:
+        ref[name][...] = ref["i_" + name][...].astype(F32)
+
+
+def local_kernel(*arguments):
+    (patches, lengths, gsd_scale, visible,
+     e_gain_a, e_bias_a, e_query, e_key, e_value, e_out, e_gain_b, e_bias_b, e_up, e_down,
+     embed, mask,
+     d_gain_a, d_bias_a, d_query, d_key, d_value, d_out, d_gain_b, d_bias_b, d_up, d_down,
+     cotangent) = arguments
+    width, dec_width = patches.shape[1], cotangent.shape[1]
+    hidden, dec_hidden = e_up.shape[1], d_up.shape[1]
+    rows = visible.shape[1]
+    image_ids, scaled, rank = layout(lengths[0], gsd_scale[0], visible[0])
+    places = rank[None, :] == jnp.arange(SHOWN, dtype=jnp.int32)[:, None]
+    packed_ids = jnp.sum(jnp.where(places, image_ids[None, :], 0), axis=1)
+    packed_scaled = jnp.sum(jnp.where(places, scaled[None, :], 0.0), axis=1)
+    side = lax.rem(lax.axis_index("dp"), 2)
+    zero = jnp.zeros((1, 64), BF16)
+
+    def half(vector):
+        row = vector[None, :]
+        return jnp.where(side == 0, jnp.concatenate([row, zero], 1),
+                         jnp.concatenate([zero, row], 1))
+
+    vector = jnp.concatenate(
+        [e_gain_a[None, :], e_bias_a[None, :], e_gain_b[None, :], e_bias_b[None, :], half(mask),
+         half(d_gain_a), half(d_bias_a), half(d_gain_b), half(d_bias_b),
+         jnp.zeros((VECTORS - 9, 128), BF16)], axis=0)
+    inputs = {
+        "rank_row": rank[None, :], "rank_column": rank[:, None],
+        "ids_row": image_ids[None, :], "ids_column": image_ids[:, None],
+        "packed_row": packed_ids[None, :], "packed_column": packed_ids[:, None],
+        "code": sincos(packed_scaled, width), "dec_code": sincos(scaled, dec_width),
+        "vector": vector, "patches": patches, "cotangent": cotangent,
+        "query": e_query, "key": e_key, "value": e_value, "out": e_out, "up": e_up,
+        "down": e_down, "embed": embed, "dec_query": d_query, "dec_key": d_key,
+        "dec_value": d_value, "dec_out": d_out, "dec_up": d_up, "dec_down": d_down,
+    }
+    units = unit_shapes(width, dec_width, hidden, dec_hidden)
+    shapes = {
+        "decoded": (cotangent.shape, BF16), "grad_patches": (patches.shape, F32),
+        "grad_vector": ((VECTORS, 128), F32),
+    }
+    for name in COLUMN_UNITS:
+        shapes[name] = ((PARTS,) + units[name], BF16)
+    for name in ROW_UNITS:
+        shapes[name] = (units[name], BF16)
+    table = scratch_table(width, dec_width, hidden, dec_hidden, rows, SHOWN)
+    names = INPUTS + tuple("o_" + name if name in MESSAGES else name for name in RESULTS)
+    names = names + tuple(table) + tuple("s_" + name for name in SEMAPHORES)
+    in_vmem = INPUTS[:9]
+    results = pl.pallas_call(
+        functools.partial(main_kernel, names),
+        out_shape=[jax.ShapeDtypeStruct(*shapes[name]) for name in RESULTS],
+        in_specs=[
+            pl.BlockSpec(memory_space=pltpu.VMEM if name in in_vmem else pl.ANY)
+            for name in INPUTS
+        ],
+        out_specs=[pl.BlockSpec(memory_space=pltpu.VMEM) for name in RESULTS],
+        scratch_shapes=[pltpu.VMEM(*entry) for entry in table.values()]
+        + [pltpu.SemaphoreType.DMA(shape) for shape in SEMAPHORES.values()],
+        compiler_params=pltpu.CompilerParams(
+            collective_id=0, has_side_effects=True, vmem_limit_bytes=62 * MIB
+        ),
+    )(*(inputs[name] for name in INPUTS))
+    made = {"i_" + name: result for name, result in zip(RESULTS, results)}
+    finals = {
+        "decoded": (cotangent.shape, BF16), "grad_patches": (patches.shape, F32),
+    }
+    for key, wide, deep in (("e_", width, hidden), ("d_", dec_width, dec_hidden)):
+        small, tall = wide // 8, deep // 8
+        if key == "d_":
+            finals["embed"] = ((width // 8, dec_width), F32)
+            finals["mask"] = ((1, small), F32)
+        for name, shape in (
+            ("gain_a", (1, small)), ("bias_a", (1, small)), ("query", (small, wide)),
+            ("key", (small, wide)), ("value", (small, wide)), ("out", (small, wide)),
+            ("gain_b", (1, small)), ("bias_b", (1, small)), ("up", (small, deep)),
+            ("down", (tall, wide)),
+        ):
+            finals[key + name] = (shape, F32)
+    outputs = pl.pallas_call(
+        functools.partial(unpack_kernel, tuple(made) + tuple(finals)),
+        out_shape=[jax.ShapeDtypeStruct(*entry) for entry in finals.values()],
+        in_specs=[pl.BlockSpec(memory_space=pltpu.VMEM)] * len(made),
+        out_specs=[pl.BlockSpec(memory_space=pltpu.VMEM)] * len(finals),
+        compiler_params=pltpu.CompilerParams(vmem_limit_bytes=40 * MIB),
+    )(*made.values())
+    return tuple(
+        output.reshape(-1) if output.shape[0] == 1 else output for output in outputs
+    )
+
+
 def solution(mesh):
     both, vec, mat = P(("dp", "blk"), None), P("dp"), P("dp", None)
     block = (vec, vec, mat, mat, mat, mat, vec, vec, mat, mat)
     in_specs = (both, mat, mat, mat) + block + (mat, vec) + block + (both,)
     out_specs = (both, both) + block + (mat, vec) + block
-    return jax.shard_map(local, mesh=mesh, in_specs=in_specs, out_specs=out_specs, check_vma=False)
+    body = local_kernel if mesh.shape["dp"] == 8 and mesh.shape["blk"] == 4 else local
+    return jax.shard_map(body, mesh=mesh, in_specs=in_specs, out_specs=out_specs, check_vma=False)

time: 1900 us -> 345 us (0.18)
  waiting for transfers between devices: 1280 us -> 0 us
  blocking collectives: 452 us -> 0 us
  Pallas kernels: 0 us -> 315 us
  matrix products: 68.1 us -> 0 us
  other arithmetic: 49 us -> 12.2 us
    reduce_scatter x13 -> x0, waiting for transfers between devices: 810 us -> none  [the longest x9 465 us: sum_columns(): lax.psum_scatter(grad.astype(BF16), 'dp', scatter_dimension=0, tiled=True)]
    all_gather x22 -> x0, blocking collectives: 396 us -> none  [the longest x12 332 us: gather(): return lax.all_gather(shard, 'dp', axis=0, tiled=True)]
    all_gather x10 -> x0, waiting for transfers between devices: 322 us -> none  [the longest x5 204 us: gather(): return lax.all_gather(shard, 'dp', axis=0, tiled=True)]
    pallas_call x0 -> x2, Pallas kernels: none -> 315 us  [the longest x1 312 us: local_kernel(): pl.pallas_call(functools.partial(main_kernel, names), out_shape=[jax.Shap...]
    psum x7 -> x0, waiting for transfers between devices: 143 us -> none  [total(): return lax.psum(partial, 'blk')]
    dot_general x93 -> x0, matrix products: 68.1 us -> none  [the longest x31 24.7 us: dot_t(): lax.dot_general(left, right, (((0,), (0,)), ((), ())), preferred_element_...]
    unnamed x2 -> x0, blocking collectives: 56.4 us -> none
    convert_element_type x34 -> x0, other arithmetic: 23.5 us -> none  [the longest x9 8.84 us: sum_columns(): return lax.all_gather(summed, 'blk', axis=1, tiled=True).astype(F32)]
  transfers between devices with their start and end apart: 30 -> 0, of which waited for: 24 -> 0; matrix products, arithmetic and copies ran while one was open for 5% -> 0% of each run, Pallas kernels for 0% -> 0%
where the time goes in v2:
time: 345 us; the launch traced here: 344 us
  Pallas kernels  315 us (91%)
  local copies, waits for them, and re-layouts  15.6 us (5%)
  other arithmetic  12.2 us (4%)
    pallas_call x1, Pallas kernels, local_kernel(): pl.pallas_call(functools.partial(main_kernel, names), out_shape=[jax.Shap...  312 us
    unnamed x30, local copies, waits for them, and re-layouts  11.7 us

profile of v2, /device:TPU:0, one launch (start us, length us, event | category | flops | bytes accessed | tf_op | source)
XLA Modules:
  0.0 344.0 jit_solution(2974235049534030328)
XLA Ops:
  0.7 0.8 reduce-window.4
  2.2 0.8 broadcast_select_fusion.6
  3.0 0.8 broadcast_select_fusion.4
  3.8 0.8 broadcast_select_fusion.2
  5.5 1.9 concatenate.51.refs_8_
  9.4 0.7 copy.59.refs_5_
  11.1 0.9 copy.58.refs_3_
  11.9 1.0 multiply_sine_fusion.1
  12.9 0.8 pad_maximum_fusion.1.refs_6_
  13.7 1.9 multiply_sine_fusion
  15.6 1.1 pad_maximum_fusion.refs_7_
  16.8 312.0 %shard_map.442 = (bf16[128,512]{1,0:T(8,128)(2,1)}, f32[128,1024]{1,0:T(8,128)}, f32[16,128]{1,0:T(8,128)}, bf16[4,128,768]{2,1,0:T(8,128)(2,1)}, bf16[4,128,102...) custom-call(s32[1,512]{1,0:T(1,128)} %copy-done.13, ...), custom_call_target="tpu_custom_call" | custom-call | tf_op jit(solution)/shard_map/pallas_call | solution.py:1375
  328.8 1.2 copy-done
  330.0 1.2 copy-done.1
  331.3 1.1 copy-done.2
  332.4 1.0 copy-done.3
  333.4 0.9 copy-done.4
  334.4 0.9 copy-done.5
  335.3 0.9 copy-done.6
  336.3 0.9 copy-done.7
  337.2 0.9 copy-done.8
  338.1 0.9 copy-done.9
  339.0 0.8 copy-done.10
  340.6 3.5 %shard_map.443 = (bf16[128,512]{1,0:T(8,128)(2,1)}, f32[128,1024]{1,0:T(8,128)}, f32[1,128]{1,0:T(1,128)}, f32[1,128]{1,0:T(1,128)}, f32[128,1024]{1,0:T(8,128)}...) custom-call(bf16[128,512]{1,0:T(8,128)(2,1)S(1)} %copy-done.8, ...), custom_call_target="tpu_custom_call" | custom-call | tf_op jit(solution)/shard_map/pallas_call | solution.py:1405
  (36 shorter events, 5.2 us)
Async XLA Ops:
  4.7 12.1 %copy-start.12 = (s32[512]{0:T(512)}, s32[512]{0:T(512)S(1)}, u32[]{:S(2)}) copy-start(s32[512]{0:T(512)S(1)} %convert_reduce_fusion.1) | copy-start | bytes 6148
  9.0 7.8 %copy-start.13 = (s32[1,512]{1,0:T(1,128)}, s32[1,512]{1,0:T(1,128)S(1)}, u32[]{:S(2)}) copy-start(s32[1,512]{1,0:T(1,128)S(1)} %broadcast_select_fusion.1.refs_0_) | copy-start | bytes 6148
  9.1 7.7 %copy-start.14 = (s32[128]{0:T(128)}, s32[128]{0:T(128)S(1)}, u32[]{:S(2)}) copy-start(s32[128]{0:T(128)S(1)} %select_reduce_fusion.1) | copy-start | bytes 1540
  328.8 1.2 copy-start
  330.0 1.2 copy-start.1
  331.3 1.1 copy-start.2
  332.4 1.0 copy-start.3
  333.4 0.9 copy-start.4
  334.4 0.9 copy-start.5
  335.3 0.9 copy-start.6
  336.3 0.9 copy-start.7
  337.2 0.9 copy-start.8
  338.1 0.9 copy-start.9
  339.0 0.8 copy-start.10
  339.9 0.7 copy-start.11

commit v3 on v2

--- a/solution.py
+++ b/solution.py
@@ -300,6 +300,25 @@
     def z_peer(self, step):
         return (self.ahead(step) * 2 + self.y, self.blk)
 
+    def at_z(self, z):
+        return (z * 2 + self.y, self.blk)
+
+    def inward(self, step):
+        high = lax.div(self.z, 2)
+        return lax.rem(self.z + high * (PARTS - step) + (1 - high) * step, PARTS)
+
+    @property
+    def inner(self):
+        return jnp.logical_or(self.z == 1, self.z == 2)
+
+    @property
+    def near_end(self):
+        return jnp.where(self.inner, 3 * self.z - 3, lax.div(self.z, 3) + 1)
+
+    @property
+    def far_end(self):
+        return 6 - 3 * self.z
+
 
 def remote(source, target, sent, received, device):
     return pltpu.make_async_remote_copy(
@@ -324,55 +343,105 @@
             return self.whole.at[rows]
         return self.whole.at[rows, self.columns]
 
-    def own(self):
-        return self.block(self.split.z, self.split.y)
-
-    def z_copy(self, step):
-        s = self.split
-        return remote(self.own(), self.own(), self.z_sent.at[step - 1],
-                      self.z_got.at[step - 1], s.z_peer(step))
-
-    def z_arrival(self, step):
-        s = self.split
-        block = self.block(s.behind(step), s.y)
-        return remote(block, block, self.z_sent.at[step - 1], self.z_got.at[step - 1],
-                      s.z_peer(step))
-
-    def y_copy(self, step):
-        s = self.split
-        block = self.block(s.behind(step), s.y)
-        return remote(block, block, self.y_sent.at[step], self.y_got.at[step], s.y_peer)
-
-    def y_arrival(self, step):
-        s = self.split
-        block = self.block(s.behind(step), 1 - s.y)
-        return remote(block, block, self.y_sent.at[step], self.y_got.at[step], s.y_peer)
+    def z_copy(self, step, y=None):
+        s = self.split
+        block = self.block(s.z, s.y if y is None else y)
+        at = 0 if y is None else 1
+        return remote(block, block, self.z_sent.at[at, step - 1], self.z_got.at[at, s.z],
+                      s.at_z(s.inward(step)))
+
+    def z_arrival(self, z, y=None):
+        s = self.split
+        block = self.block(z, s.y if y is None else y)
+        at = 0 if y is None else 1
+        return remote(block, block, self.z_sent.at[at, 0], self.z_got.at[at, z], s.y_peer)
+
+    def relay(self, y=None):
+        s = self.split
+        block = self.block(s.far_end, s.y if y is None else y)
+        at = 0 if y is None else 1
+        return remote(block, block, self.z_sent.at[at, 3], self.z_got.at[at, s.far_end],
+                      s.at_z(s.near_end))
+
+    def y_copy(self, z, at):
+        s = self.split
+        block = self.block(z, s.y)
+        return remote(block, block, self.y_sent.at[at], self.y_got.at[at], s.y_peer)
+
+    def y_arrival(self, z, at):
+        s = self.split
+        block = self.block(z, 1 - s.y)
+        return remote(block, block, self.y_sent.at[at], self.y_got.at[at], s.y_peer)
 
     def fetch(self):
         for copy in self.local:
             copy.start()
 
+    def spread(self, y=None):
+        self.z_copy(1, y).start()
+        self.z_copy(2, y).start()
+
+        @pl.when(self.split.inner)
+        def _():
+            self.z_copy(3, y).start()
+
+    def collect(self, step, y=None):
+        s = self.split
+        z = s.inward(step)
+        self.z_arrival(z, y).wait_recv()
+        if step == 2:
+            @pl.when(s.inner)
+            def _():
+                self.relay(y).start()
+        return z
+
     def send(self):
         for copy in self.local:
             copy.wait()
-        for step in (1, 2, 3):
-            self.z_copy(step).start()
-        self.y_copy(0).start()
+        self.spread()
+        self.y_copy(self.split.z, 0).start()
 
     def forward(self):
         for step in (1, 2, 3):
-            self.z_arrival(step).wait_recv()
-            self.y_copy(step).start()
+            self.y_copy(self.collect(step), step).start()
 
     def finish(self):
         for step in range(PARTS):
-            self.y_arrival(step).wait_recv()
+            self.y_arrival(self.split.inward(step), step).wait_recv()
+
+    def drain_z(self, y=None):
+        self.z_copy(1, y).wait_send()
+        self.z_copy(2, y).wait_send()
+
+        @pl.when(self.split.inner)
+        def _():
+            self.z_copy(3, y).wait_send()
+            self.relay(y).wait_send()
 
     def drain(self):
+        self.drain_z()
+        for step in range(PARTS):
+            self.y_copy(self.split.inward(step), step).wait_send()
+
+
+class EarlyColumns(Columns):
+    def cross(self):
+        s = self.split
+        self.y_arrival(s.z, 0).wait_recv()
+        self.spread(1 - s.y)
+
+    def forward(self):
         for step in (1, 2, 3):
-            self.z_copy(step).wait_send()
-        for step in range(PARTS):
-            self.y_copy(step).wait_send()
+            self.collect(step)
+
+    def finish(self):
+        for step in (1, 2, 3):
+            self.collect(step, 1 - self.split.y)
+
+    def drain(self):
+        self.drain_z()
+        self.drain_z(1 - self.split.y)
+        self.y_copy(self.split.z, 0).wait_send()
 
 
 class Rows:
@@ -383,10 +452,21 @@
     def block(self, y):
         return self.whole.at[span(y * self.rows, self.rows)]
 
-    def z_copy(self, step):
-        s = self.split
-        return remote(self.block(s.y), self.block(s.y), self.z_sent.at[step - 1],
-                      self.z_got.at[0], s.z_peer(step))
+    def z_copy(self, way):
+        s = self.split
+        return remote(self.block(s.y), self.block(s.y), self.z_sent.at[0, way],
+                      self.z_got.at[0, 0], s.at_z(s.z + 1 - 2 * way))
+
+    def pass_on(self, act):
+        s = self.split
+
+        @pl.when(jnp.logical_and(s.z >= s.part, s.z < PARTS - 1))
+        def _():
+            act(self.z_copy(0))
+
+        @pl.when(jnp.logical_and(s.z <= s.part, s.z > 0))
+        def _():
+            act(self.z_copy(1))
 
     def y_copy(self):
         s = self.split
@@ -402,14 +482,18 @@
         @pl.when(self.split.z == self.split.part)
         def _():
             self.local.wait()
-            for step in (1, 2, 3):
-                self.z_copy(step).start()
+            self.pass_on(lambda copy: copy.start())
+            self.y_copy().start()
 
     def forward(self):
-        @pl.when(self.split.z != self.split.part)
-        def _():
-            self.z_copy(1).wait_recv()
-        self.y_copy().start()
+        s = self.split
+
+        @pl.when(s.z != s.part)
+        def _():
+            remote(self.block(s.y), self.block(s.y), self.z_sent.at[0, 0],
+                   self.z_got.at[0, 0], s.y_peer).wait_recv()
+            self.pass_on(lambda copy: copy.start())
+            self.y_copy().start()
 
     def finish(self):
         s = self.split
@@ -417,17 +501,14 @@
         remote(block, block, self.y_sent.at[0], self.y_got.at[0], s.y_peer).wait_recv()
 
     def drain(self):
-        @pl.when(self.split.z == self.split.part)
-        def _():
-            for step in (1, 2, 3):
-                self.z_copy(step).wait_send()
+        self.pass_on(lambda copy: copy.wait_send())
         self.y_copy().wait_send()
 
 
-def each(count, step, body):
+def each(count, step, body, base=0):
     @pl.loop(0, count // step)
     def _(at):
-        body(pl.ds(pl.multiple_of(at * step, step), step))
+        body(pl.ds(pl.multiple_of(base + at * step, step), step))
 
 
 class ColumnSum:
@@ -442,20 +523,37 @@
 
     def z_copy(self, step):
         s = self.split
-        return remote(self.met.at[s.ahead(step)], self.came.at[step - 1],
-                      self.z_sent.at[step - 1], self.z_got.at[step - 1], s.z_peer(step))
+        target = s.inward(step)
+        return remote(self.met.at[target], self.came.at[s.z], self.z_sent.at[step - 1],
+                      self.z_got.at[s.z], s.at_z(target))
+
+    def z_arrival(self, z):
+        s = self.split
+        return remote(self.met.at[z], self.came.at[z], self.z_sent.at[0], self.z_got.at[z],
+                      s.y_peer)
+
+    def relay(self):
+        s = self.split
+        return remote(self.met.at[3 - s.z], self.came.at[s.near_end], self.z_sent.at[2],
+                      self.z_got.at[s.near_end], s.at_z(s.near_end))
 
     def b_copy(self, which):
         s = self.split
-        block = self.done.at[s.blk]
-        return remote(block, block, self.b_sent.at[which], self.b_got.at[which],
-                      s.blk_peers[which])
+        if which == 2:
+            block = self.done.at[s.x_peer[1]]
+            return remote(block, block, self.b_sent.at[2], self.b_got.at[2], s.core_peer)
+        return remote(self.met.at[s.z], self.done.at[s.blk], self.b_sent.at[which],
+                      self.b_got.at[which], s.blk_peers[which])
 
     def b_arrival(self, which):
         s = self.split
         block = self.done.at[s.blk_peers[which][1]]
         return remote(block, block, self.b_sent.at[which], self.b_got.at[which],
                       s.blk_peers[which])
+
+    def own_copy(self):
+        s = self.split
+        return pltpu.make_async_copy(self.met.at[s.z], self.done.at[s.blk], self.b_sent.at[3])
 
     def start(self):
         self.y_copy().start()
@@ -466,42 +564,142 @@
             self.met[z, rows] = both.astype(self.met.dtype)
         each(self.met.shape[1], self.step, body)
 
+    def arrive(self):
+        self.y_copy().wait_recv()
+
     def middle(self):
-        self.y_copy().wait_recv()
-        for step in (1, 2, 3):
-            self.add(self.split.ahead(step))
-            self.z_copy(step).start()
+        s = self.split
+        self.arrive()
+
+        @pl.when(s.inner)
+        def _():
+            self.add(s.inward(1))
+            self.z_copy(1).start()
+            self.add(s.inward(3))
+            self.z_copy(3).start()
+            self.add(s.inward(2))
+
+        @pl.when(jnp.logical_not(s.inner))
+        def _():
+            self.add(3 - s.z)
+            self.relay().start()
+            self.add(s.inward(2))
+            self.z_copy(2).start()
+            self.add(s.inward(1))
+            self.z_copy(1).start()
+        self.add(s.z)
+
+    def join(self):
+        s = self.split
+
+        @pl.when(s.inner)
+        def _():
+            target = s.inward(2)
+            self.z_arrival(s.z).wait_recv()
+
+            def body(rows):
+                both = self.met[target, rows].astype(F32) + self.came[s.z, rows].astype(F32)
+                self.met[target, rows] = both.astype(self.met.dtype)
+            each(self.met.shape[1], self.step, body)
+            self.z_copy(2).start()
 
     def total(self, store):
         s = self.split
-        for step in (1, 2, 3):
-            self.z_copy(step).wait_recv()
-
-        def body(rows):
-            whole = self.grad[s.z, s.y, rows].astype(F32) + self.met[s.z, rows].astype(F32)
-            for step in range(3):
-                whole = whole + self.came[step, rows].astype(F32)
-            store(rows, whole)
-        each(self.met.shape[1], self.step, body)
+
+        @pl.when(s.inner)
+        def _():
+            sources = (0, 3, 3 - s.z)
+            for z in sources:
+                self.z_arrival(z).wait_recv()
+
+            def body(rows):
+                whole = self.met[s.z, rows].astype(F32)
+                for z in sources:
+                    whole = whole + self.came[z, rows].astype(F32)
+                store(rows, whole)
+            each(self.met.shape[1], self.step, body)
+
+        @pl.when(jnp.logical_not(s.inner))
+        def _():
+            for z in (1, 2):
+                self.z_arrival(z).wait_recv()
+
+            def body(rows):
+                whole = self.met[s.z, rows].astype(F32)
+                for z in (1, 2):
+                    whole = whole + self.came[z, rows].astype(F32)
+                store(rows, whole)
+            each(self.met.shape[1], self.step, body)
 
     def last(self):
+        s = self.split
+
         def store(rows, whole):
-            self.done[self.split.blk, rows] = whole.astype(self.done.dtype)
+            self.met[s.z, rows] = whole.astype(self.met.dtype)
         self.total(store)
-        for which in range(3):
-            self.b_copy(which).start()
+        self.b_copy(1).start()
+        self.b_copy(0).start()
+        self.own_copy().start()
+
+    def pass_on(self):
+        self.b_arrival(1).wait_recv()
+        self.b_copy(2).start()
 
     def close(self):
-        for which in range(3):
-            self.b_arrival(which).wait_recv()
+        self.b_arrival(0).wait_recv()
+        self.b_arrival(2).wait_recv()
         for which in range(3):
             self.b_copy(which).wait_send()
+        self.own_copy().wait()
         self.drain()
 
+    def drain_y(self):
+        self.y_copy().wait_send()
+
     def drain(self):
-        self.y_copy().wait_send()
+        self.drain_y()
         for step in (1, 2, 3):
             self.z_copy(step).wait_send()
+
+
+class ProductSum(ColumnSum):
+    def trade(self, left, right, their_left, their_right, sems):
+        self.left, self.right = left, right
+        self.their_left, self.their_right = their_left, their_right
+        self.t_sent, self.t_got = sems
+        self.width = their_left.shape[2]
+
+    def columns(self, z, y):
+        return self.left.at[:, span((z * 2 + y) * self.width, self.width)]
+
+    def left_copy(self, z):
+        s = self.split
+        return remote(self.columns(z, 1 - s.y), self.their_left.at[z], self.t_sent.at[z],
+                      self.t_got.at[z], s.y_peer)
+
+    def right_copy(self):
+        return remote(self.right, self.their_right, self.t_sent.at[PARTS],
+                      self.t_got.at[PARTS], self.split.y_peer)
+
+    def copies(self):
+        return [self.right_copy()] + [self.left_copy(z) for z in range(PARTS)]
+
+    def start(self):
+        for copy in self.copies():
+            copy.start()
+
+    def add(self, z):
+        both = dot_t(self.columns(z, self.split.y)[...], self.right[...]) + dot_t(
+            self.their_left[z], self.their_right[...])
+        self.met[z] = both.astype(self.met.dtype)
+
+    def arrive(self):
+        for copy in self.copies():
+            copy.wait_recv()
+
+    def drain_y(self):
+        for copy in self.copies():
+            copy.wait_send()
 
 
 class RowSum:
@@ -510,66 +708,119 @@
         self.y_sent, self.y_got, self.z_sent, self.z_got, self.b_sent, self.b_got = sems
         self.step = step
         s = split
-        self.slot = lax.rem(s.part + PARTS - s.z + 3, PARTS)
-        self.home = (s.part * 2 + s.y, s.blk)
+        self.home = lax.rem(3 * s.z, PARTS)
+        self.at_home = s.z == s.part
+        self.below = s.z < s.part
+        self.above = s.z > s.part
+        self.beside = s.x_peer[1] == self.home
 
     def y_copy(self):
         s = self.split
         return remote(self.grad.at[1 - s.y], self.met, self.y_sent, self.y_got, s.y_peer)
 
-    def z_copy(self):
-        return remote(self.met, self.came.at[self.slot], self.z_sent.at[0],
-                      self.z_got.at[self.slot], self.home)
+    def z_copy(self, way):
+        s = self.split
+        return remote(self.met, self.came.at[way], self.z_sent.at[way], self.z_got.at[way],
+                      s.at_z(s.z + 1 - 2 * way))
+
+    def z_arrival(self, way):
+        return remote(self.met, self.came.at[way], self.z_sent.at[way], self.z_got.at[way],
+                      self.split.y_peer)
 
     def b_copy(self, which):
-        return remote(self.done, self.done, self.b_sent.at[which], self.b_got.at[0],
-                      self.split.blk_peers[which])
+        s = self.split
+        source = self.done if which == 2 else self.met
+        device = s.core_peer if which == 2 else s.blk_peers[which]
+        return remote(source, self.done, self.b_sent.at[which], self.b_got.at[0], device)
+
+    def own_copy(self):
+        return pltpu.make_async_copy(self.met, self.done, self.b_sent.at[3])
 
     def start(self):
         self.y_copy().start()
 
+    def send(self, act):
+        @pl.when(self.below)
+        def _():
+            act(self.z_copy(0))
+
+        @pl.when(self.above)
+        def _():
+            act(self.z_copy(1))
+
+    def take(self, way):
+        self.z_arrival(way).wait_recv()
+
+        def body(rows):
+            both = self.met[rows].astype(F32) + self.came[way, rows].astype(F32)
+            self.met[rows] = both.astype(self.met.dtype)
+        each(self.met.shape[0], self.step, body)
+
     def middle(self):
         s = self.split
         self.y_copy().wait_recv()
 
-        @pl.when(s.z != s.part)
-        def _():
-            def body(rows):
-                both = self.grad[s.y, rows].astype(F32) + self.met[rows].astype(F32)
-                self.met[rows] = both.astype(self.met.dtype)
-            each(self.met.shape[0], self.step, body)
-            self.z_copy().start()
+        def body(rows):
+            both = self.grad[s.y, rows].astype(F32) + self.met[rows].astype(F32)
+            self.met[rows] = both.astype(self.met.dtype)
+        each(self.met.shape[0], self.step, body)
+
+        @pl.when(jnp.logical_not(s.inner))
+        def _():
+            self.send(lambda copy: copy.start())
+
+    def join(self):
+        s = self.split
+
+        @pl.when(s.inner)
+        def _():
+            @pl.when(self.below)
+            def _():
+                self.take(0)
+
+            @pl.when(self.above)
+            def _():
+                self.take(1)
+            self.send(lambda copy: copy.start())
 
     def last(self):
         s = self.split
 
-        @pl.when(s.z == s.part)
-        def _():
-            for step in range(3):
-                remote(self.met, self.came.at[step], self.z_sent.at[0],
-                       self.z_got.at[step], s.y_peer).wait_recv()
-
-            def body(rows):
-                whole = self.grad[s.y, rows].astype(F32) + self.met[rows].astype(F32)
-                for step in range(3):
-                    whole = whole + self.came[step, rows].astype(F32)
-                self.done[rows] = whole.astype(self.done.dtype)
-            each(self.met.shape[0], self.step, body)
-            for which in range(3):
-                self.b_copy(which).start()
+        @pl.when(self.at_home)
+        def _():
+            @pl.when(s.z > 0)
+            def _():
+                self.take(0)
+
+            @pl.when(s.z < PARTS - 1)
+            def _():
+                self.take(1)
+            self.b_copy(1).start()
+            self.b_copy(0).start()
+            self.own_copy().start()
+
+    def pass_on(self):
+        @pl.when(self.beside)
+        def _():
+            self.b_copy(0).wait_recv()
+            self.b_copy(2).start()
 
     def close(self):
-        s = self.split
         self.y_copy().wait_send()
-
-        @pl.when(s.z == s.part)
-        def _():
-            for which in range(3):
-                self.b_copy(which).wait_send()
-
-        @pl.when(s.z != s.part)
-        def _():
-            self.z_copy().wait_send()
+        self.send(lambda copy: copy.wait_send())
+
+        @pl.when(self.at_home)
+        def _():
+            self.b_copy(0).wait_send()
+            self.b_copy(1).wait_send()
+            self.own_copy().wait()
+
+        @pl.when(self.beside)
+        def _():
+            self.b_copy(2).wait_send()
+
+        @pl.when(jnp.logical_not(jnp.logical_or(self.at_home, self.beside)))
+        def _():
             self.b_copy(0).wait_recv()
 
 
@@ -578,44 +829,75 @@
         self.split, self.part, self.met, self.out = split, part, met, out
         self.came, self.whole = came.at[slot], whole
         self.sent, self.got = sems
-
-    def first_copy(self):
-        s = self.split
-        return remote(self.part.at[1 - s.core], self.met, self.sent.at[0], self.got.at[0],
-                      s.core_peer)
-
-    def second_copy(self):
-        return remote(self.out, self.came, self.sent.at[1], self.got.at[1], self.split.x_peer)
-
-    def third_copy(self, half):
-        s = self.split
-        return remote(self.whole.at[half], self.whole.at[half], self.sent.at[2],
-                      self.got.at[2], s.core_peer)
-
-    def start(self):
-        self.first_copy().start()
-
-    def middle(self):
-        s = self.split
-        self.first_copy().wait_recv()
+        self.chunks = part.shape[0]
+        self.high = part.shape[2]
+
+    def first_copy(self, at):
+        s = self.split
+        return remote(self.part.at[at, 1 - s.core], self.met.at[at], self.sent.at[at, 0],
+                      self.got.at[at, 0], s.core_peer)
+
+    def second_copy(self, at):
+        return remote(self.out.at[at], self.came.at[at], self.sent.at[at, 1],
+                      self.got.at[at, 1], self.split.x_peer)
+
+    def third_copy(self, at, half):
+        s = self.split
+        return remote(self.whole.at[at, half], self.whole.at[at, half], self.sent.at[at, 2],
+                      self.got.at[at, 2], s.core_peer)
+
+    def start(self, at):
+        self.first_copy(at).start()
+
+    def middle(self, at):
+        s = self.split
+        self.first_copy(at).wait_recv()
 
         def body(rows):
-            self.out[rows] = (self.part[s.core, rows] + self.met[rows]).astype(BF16)
-        each(self.out.shape[0], 32, body)
-        self.second_copy().start()
-
-    def end(self):
-        s = self.split
-        self.second_copy().wait_recv()
+            both = self.part[at, s.core, rows] + self.met[at, rows]
+            self.out[at, rows] = both.astype(BF16)
+        each(self.high, 32, body)
+        self.second_copy(at).start()
+
+    def third(self, at):
+        s = self.split
+        self.second_copy(at).wait_recv()
 
         def body(rows):
-            self.whole[s.core, rows] = self.out[rows].astype(F32) + self.came[rows].astype(F32)
-        each(self.out.shape[0], 32, body)
-        self.third_copy(s.core).start()
-        self.third_copy(1 - s.core).wait_recv()
-        self.first_copy().wait_send()
-        self.second_copy().wait_send()
-        self.third_copy(s.core).wait_send()
+            self.whole[at, s.core, rows] = self.out[at, rows].astype(
+                F32) + self.came[at, rows].astype(F32)
+        each(self.high, 32, body)
+        self.third_copy(at, s.core).start()
+
+    def fourth(self, at):
+        s = self.split
+        self.third_copy(at, 1 - s.core).wait_recv()
+        self.first_copy(at).wait_send()
+        self.second_copy(at).wait_send()
+        self.third_copy(at, s.core).wait_send()
+
+    def begin(self, produce):
+        @pl.loop(0, self.chunks + 1)
+        def _(at):
+            @pl.when(at < self.chunks)
+            def _():
+                produce(at)
+                self.start(at)
+
+            @pl.when(at > 0)
+            def _():
+                self.middle(at - 1)
+
+    def finish(self, consume):
+        self.third(0)
+
+        @pl.loop(0, self.chunks)
+        def _(at):
+            @pl.when(at + 1 < self.chunks)
+            def _():
+                self.third(at + 1)
+            self.fourth(at)
+            consume(at)
 
 
 def head_mask(width, size, head):
@@ -636,6 +918,7 @@
         self.vectors = vectors
         self.name = names
         self.tile = 32 * 1024 // width
+        self.chunk = 2 * refs[names + "part"].shape[2]
 
     def ref(self, name):
         return self.refs[self.name + name]
@@ -643,7 +926,7 @@
     def row(self, at):
         return self.refs["gains"][self.vectors + at:self.vectors + at + 1, 0:self.width]
 
-    def norm(self, first):
+    def norm(self, first, base=0, count=None):
         unit, scale = self.ref("unit_a" if first else "unit_b"), self.ref(
             "scale_a" if first else "scale_b")
         out = self.ref("normed" if first else "lifted")
@@ -655,7 +938,7 @@
             unit[rows] = one
             scale[rows] = size
             out[rows] = (one * gain + bias).astype(BF16)
-        each(self.rows, self.tile, body)
+        each(count or self.rows, self.tile, body, base)
 
     def project(self):
         normed, mixed, weight = self.ref("normed"), self.ref("qkv"), self.ref("w_qkv")
@@ -691,29 +974,30 @@
             mixture[queries] = mixed.T.astype(BF16)
         each(self.rows, 128, body)
 
-    def product(self, left, weight, target, back=False):
-        shape = target.shape
-        half = shape[1]
+    def product(self, left, weight, back=False):
+        target, deep = self.ref("part"), self.chunk
+
+        def produce(at):
+            rows = pl.ds(pl.multiple_of(at * deep, deep), deep)
+            made = (dot_b if back else dot)(left[rows], weight[...])
+            target[at, 0] = made[:deep // 2]
+            target[at, 1] = made[deep // 2:]
+        return produce
+
+    def halves(self, rows):
+        half = self.chunk // 2
+        at = lax.div(rows.start, half)
+        place = pl.ds(pl.multiple_of(lax.rem(rows.start, half), rows.size), rows.size)
+        return self.ref("whole")[lax.div(at, 2), lax.rem(at, 2), place]
+
+    def add_total(self, at):
+        residual = self.ref("residual")
 
         def body(rows):
-            made = (dot_b if back else dot)(left[rows], weight[...])
-            at = lax.div(rows.start, half)
-            target[at, pl.ds(pl.multiple_of(lax.rem(rows.start, half), 64), 64)] = made
-        each(self.rows, 64, body)
-
-    def half(self, ref, rows):
-        size = ref.shape[1]
-        start = pl.multiple_of(lax.rem(rows.start, size), rows.size)
-        return ref[lax.div(rows.start, size), pl.ds(start, rows.size)]
-
-    def add_total(self, whole):
-        residual = self.ref("residual")
-
-        def body(rows):
-            residual[rows] = residual[rows] + self.half(whole, rows)
-        each(self.rows, self.tile, body)
-
-    def expand(self):
+            residual[rows] = residual[rows] + self.halves(rows)
+        each(self.chunk, self.tile, body, at * self.chunk)
+
+    def expand(self, base=0, count=None):
         lifted, weight = self.ref("lifted"), self.ref("w_up")
         hidden, slope = self.ref("hidden"), self.ref("slope")
 
@@ -723,9 +1007,9 @@
                 hidden[rows, columns] = made.astype(BF16)
                 slope[rows, columns] = gradient
             each(weight.shape[1], 256, inner)
-        each(self.rows, 128, body)
-
-    def back_hidden(self, branch):
+        each(count or self.rows, 128, body, base)
+
+    def back_hidden(self, branch, base=0, count=None):
         weight, slope, grad = self.ref("w_down"), self.ref("slope"), self.ref("grad_upper")
 
         def body(rows):
@@ -733,29 +1017,32 @@
                 made = dot_b(branch[rows], weight[columns])
                 grad[rows, columns] = (made * slope[rows, columns]).astype(BF16)
             each(weight.shape[0], 256, inner)
-        each(self.rows, 128, body)
-
-    def norm_back(self, whole, first, out):
+        each(count or self.rows, 128, body, base)
+
+    def clear_sums(self):
+        sums = self.ref("sums")
+        sums[...] = jnp.zeros(sums.shape, F32)
+
+    def norm_back(self, at, first, out):
         unit, scale = self.ref("unit_a" if first else "unit_b"), self.ref(
             "scale_a" if first else "scale_b")
-        gain, grad = self.row(0 if first else 2), self.ref("grad")
-
-        def body(at, sums):
-            rows = pl.ds(pl.multiple_of(at * self.tile, self.tile), self.tile)
-            moved, gains, biases = norm_back(self.half(whole, rows), unit[rows], scale[rows], gain)
+        gain, grad, sums = self.row(0 if first else 2), self.ref("grad"), self.ref("sums")
+
+        def body(rows):
+            moved, gains, biases = norm_back(self.halves(rows), unit[rows], scale[rows], gain)
             new = grad[rows] + moved
             grad[rows] = new
             out[rows] = new.astype(BF16)
-            return sums[0] + gains, sums[1] + biases
-        zero = jnp.zeros((1, self.width), F32)
-        return lax.fori_loop(0, self.rows // self.tile, body, (zero, zero))
-
-    def back_mixture(self, branch):
+            sums[0:1] += gains
+            sums[1:2] += biases
+        each(self.chunk, self.tile, body, at * self.chunk)
+
+    def back_mixture(self, branch, base=0, count=None):
         weight, grad = self.ref("w_out"), self.ref("grad_mixture")
 
         def body(rows):
             grad[rows] = dot_b(branch[rows], weight[...]).astype(BF16)
-        each(self.rows, 128, body)
+        each(count or self.rows, self.chunk, body, base)
 
     def attend_back(self):
         probs, grad_mixture, grads = self.ref("probs"), self.ref("grad_mixture"), self.ref(
@@ -824,6 +1111,8 @@
 COLUMN_UNITS = ("e_qkv", "e_up", "e_down", "embed", "d_qkv", "d_up")
 ROW_UNITS = ("e_out", "d_out", "d_down")
 MESSAGES = COLUMN_UNITS + ROW_UNITS
+TRADED = ("e_qkv", "e_up", "e_down")
+EARLY = ("e_down",)
 
 
 def unit_shapes(width, dec_width, hidden, dec_hidden):
@@ -849,23 +1138,28 @@
             table["w_" + name] = ((8 * height, columns), BF16)
         table["g_" + name] = ((PARTS, SIDES, height, columns), BF16)
         table["m_" + name] = ((PARTS, height, columns), BF16)
-        table["c_" + name] = ((3, height, columns), BF16)
+        table["c_" + name] = ((PARTS, height, columns), BF16)
+        if name in TRADED:
+            del table["g_" + name]
+            table["l_" + name] = ((PARTS, shown, 128), BF16)
+            table["r_" + name] = ((shown, columns), BF16)
     table["w_embed"] = ((width, dec_width), BF16)
     for name in ROW_UNITS:
         height, columns = units[name]
         table["w_" + name] = ((2 * height, columns), BF16)
         table["g_" + name] = ((SIDES, height, columns), BF16)
         table["m_" + name] = ((height, columns), BF16)
-        table["c_" + name] = ((3, height, columns), BF16)
+        table["c_" + name] = ((2, height, columns), BF16)
     table["w_vector"] = ((8 * VECTORS, 128), BF16)
     table["g_vector"] = ((PARTS, SIDES, VECTORS, 128), F32)
     table["m_vector"] = ((PARTS, VECTORS, 128), F32)
-    table["c_vector"] = ((3, VECTORS, 128), F32)
+    table["c_vector"] = ((PARTS, VECTORS, 128), F32)
     table["gains"] = ((VECTORS, width), F32)
     table["group"] = ((rows, width), BF16)
     table["cotangents"] = ((rows, dec_width), BF16)
-    for key, count, wide, deep, heads, size in (
-        ("e_", shown, width, hidden // 4, 4, 64), ("d_", rows, dec_width, dec_hidden // 4, 4, 32)
+    for key, count, wide, deep, heads, size, chunks in (
+        ("e_", shown, width, hidden // 4, 4, 64, 2),
+        ("d_", rows, dec_width, dec_hidden // 4, 4, 32, 4),
     ):
         share = heads * size
         for name, shape, kind in (
@@ -878,36 +1172,106 @@
             ("grad_upper", (count, deep), BF16), ("grad", (count, wide), F32),
             ("grad_mixture", (count, share), BF16), ("grad_qkv", (count, 3 * share), BF16),
             ("key_sum", (count, share), F32), ("value_sum", (count, share), F32),
-            ("branch", (count, wide), BF16),
-            ("part", (2, count // 2, wide), F32), ("met", (count // 2, wide), F32),
-            ("out", (count // 2, wide), BF16), ("came", (2, count // 2, wide), BF16),
-            ("whole", (2, count // 2, wide), F32),
+            ("branch", (count, wide), BF16), ("branch_b", (count, wide), BF16),
+            ("part", (chunks, 2, count // chunks // 2, wide), F32),
+            ("met", (chunks, count // chunks // 2, wide), F32),
+            ("out", (chunks, count // chunks // 2, wide), BF16),
+            ("came", (2, chunks, count // chunks // 2, wide), BF16),
+            ("whole", (chunks, 2, count // chunks // 2, wide), F32),
+            ("sums", (8, wide), F32),
         ):
             table[key + name] = (shape, kind)
     table["last_part"] = ((2, 2, rows // 4, dec_width), F32)
     table["last_met"] = ((2, rows // 4, dec_width), F32)
     table["last_out"] = ((rows // 4, dec_width), BF16)
     table["last_came"] = ((rows // 4, dec_width), BF16)
+    for name, shape, kind in (
+        ("rank_row", (1, rows), jnp.int32), ("rank_column", (rows, 1), jnp.int32),
+        ("ids_row", (1, rows), jnp.int32), ("ids_column", (rows, 1), jnp.int32),
+        ("packed_row", (1, shown), jnp.int32), ("packed_column", (shown, 1), jnp.int32),
+        ("code", (shown, width), F32), ("dec_code", (rows, dec_width), F32),
+        ("staged", (VECTORS, 128), F32),
+    ):
+        table[name] = (shape, kind)
     table["lowered"] = ((shown, width), BF16)
     table["picked"] = ((shown, dec_width), BF16)
     return table
 
 
-INPUTS = (
-    "rank_row", "rank_column", "ids_row", "ids_column", "packed_row", "packed_column",
-    "code", "dec_code", "vector",
+VECTOR_NAMES = (
+    "v_gain_a", "v_bias_a", "v_gain_b", "v_bias_b", "v_mask",
+    "v_dec_gain_a", "v_dec_bias_a", "v_dec_gain_b", "v_dec_bias_b",
+)
+INPUTS = ("lengths", "gsd", "visible") + VECTOR_NAMES + (
     "patches", "cotangent", "query", "key", "value", "out", "up", "down", "embed",
     "dec_query", "dec_key", "dec_value", "dec_out", "dec_up", "dec_down",
 )
 RESULTS = ("decoded", "grad_patches", "grad_vector") + MESSAGES
 SEMAPHORES = {
     "local": (40,),
-    "z_sent": (10, 3), "z_got": (10, 3), "y_sent": (10, 4), "y_got": (10, 4),
-    "gy_sent": (10,), "gy_got": (10,), "gz_sent": (10, 3), "gz_got": (10, 3),
-    "gb_sent": (10, 3), "gb_got": (10, 3),
+    "z_sent": (10, 2, 4), "z_got": (10, 2, 4), "y_sent": (10, 4), "y_got": (10, 4),
+    "gy_sent": (10,), "gy_got": (10,), "gz_sent": (10, 3), "gz_got": (10, 4),
+    "f_sent": (3, 5), "f_got": (3, 5),
+    "gb_sent": (10, 4), "gb_got": (10, 3),
     "p_sent": (3,), "p_got": (3,), "c_sent": (3,), "c_got": (3,),
-    "e_sent": (3,), "e_got": (3,), "t_sent": (8, 3), "t_got": (8, 3),
+    "e_sent": (3,), "e_got": (3,), "t_sent": (8, 4, 3), "t_got": (8, 4, 3),
 }
+
+
+def place_of(ref, positions):
+    ids = jnp.zeros(positions.shape, jnp.int32)
+    first = jnp.zeros(positions.shape, jnp.int32)
+    ratio = jnp.zeros(positions.shape, F32) + ref["gsd"][0, 0]
+    end = jnp.int32(0)
+    count = ref["lengths"].shape[1]
+    for at in range(count - 1):
+        end = end + ref["lengths"][0, at]
+        later = positions >= end
+        ids = ids + later.astype(jnp.int32)
+        first = jnp.where(later, end, first)
+        ratio = jnp.where(later, ref["gsd"][0, at + 1], ratio)
+    return ids, (positions - first).astype(F32) * ratio
+
+
+def lay_out(ref, rows, shown, width, dec_width):
+    ids_row, scaled_row = place_of(ref, lax.broadcasted_iota(jnp.int32, (1, rows), 1))
+    ids_column, scaled_column = place_of(ref, lax.broadcasted_iota(jnp.int32, (rows, 1), 0))
+    ref["ids_row"][...] = ids_row
+    ref["ids_column"][...] = ids_column
+    visible = ref["visible"][...] > 0
+    marks = jnp.broadcast_to(visible.astype(F32), (16, rows)).astype(BF16)
+    down = lax.broadcasted_iota(jnp.int32, (rows, rows), 0)
+    along = lax.broadcasted_iota(jnp.int32, (rows, rows), 1)
+    until = (along <= down).astype(BF16)
+    before = (along < down).astype(BF16)
+    count_row = dot_b(marks, until)[0:1]
+    rank_row = jnp.where(visible, count_row.astype(jnp.int32) - 1, -1)
+    count_column = dot_b(until, marks)[:, 0:1].astype(jnp.int32)
+    others = dot_b(before, marks)[:, 0:1].astype(jnp.int32)
+    rank_column = jnp.where(count_column > others, others, -1)
+    ref["rank_row"][...] = rank_row
+    ref["rank_column"][...] = rank_column
+    here = lax.broadcasted_iota(jnp.int32, (shown, rows), 0) == rank_row
+    packed = jnp.sum(jnp.where(here, ids_row.astype(F32), 0.0), axis=1, keepdims=True)
+    ref["packed_column"][...] = packed.astype(jnp.int32)
+    packed_scaled = jnp.sum(jnp.where(here, scaled_row, 0.0), axis=1, keepdims=True)
+    there = lax.broadcasted_iota(jnp.int32, (rows, shown), 1) == rank_column
+    packed = jnp.sum(jnp.where(there, ids_column.astype(F32), 0.0), axis=0, keepdims=True)
+    ref["packed_row"][...] = packed.astype(jnp.int32)
+    for target, scaled, wide in (
+        (ref["code"], packed_scaled, width), (ref["dec_code"], scaled_column, dec_width)
+    ):
+        half = wide // 2
+        steps = lax.broadcasted_iota(jnp.int32, (1, half), 1).astype(F32)
+        frequency = jnp.exp(steps * (-math.log(10000.0) / half))
+        target[:, 0:1] = scaled
+        tall = 16 * 1024 // half
+
+        def body(part):
+            angles = target[part, 0:1] * frequency
+            made = jnp.concatenate([jnp.sin(angles), jnp.cos(angles)], axis=1)
+            target[part] = made
+        each(target.shape[0], tall, body)
 
 
 def main_kernel(names, *refs):
@@ -929,21 +1293,21 @@
     for peer in peers:
         pl.semaphore_signal(barrier, inc=1, device_id=peer, device_id_type=pl.DeviceIdType.MESH)
 
-    order = ("vector",) + MESSAGES
+    order = ("vector", "e_qkv", "e_out", "e_up", "embed", "e_down", "d_qkv", "d_out", "d_up",
+             "d_down")
     units = {}
     for at, name in enumerate(order):
         sems = tuple(sem[kind].at[at] for kind in ("z_sent", "z_got", "y_sent", "y_got"))
         whole = ref["w_" + name]
         if name == "vector":
-            copies = [local(ref["vector"], whole.at[span(s.dp * VECTORS, VECTORS)])]
-            units[name] = Columns(s, whole, VECTORS, copies, sems)
+            units[name] = Columns(s, whole, VECTORS, [], sems)
         elif name in ROW_UNITS:
             source = ref[{"e_out": "out", "d_out": "dec_out", "d_down": "dec_down"}[name]]
             height = source.shape[0]
             copy = local(source, whole.at[span(s.y * height, height)])
             units[name] = Rows(s, whole, height, copy, sems)
         else:
-            height = ref["g_" + name].shape[2]
+            height = ref["m_" + name].shape[1]
             mine = span(s.dp * height, height)
             columns = None
             if name in ("e_qkv", "d_qkv"):
@@ -972,7 +1336,8 @@
             else:
                 size = ref["dec_up"].shape[1] // PARTS
                 copies = [local(ref["dec_up"].at[:, span(s.part * size, size)], whole.at[mine])]
-            units[name] = Columns(s, whole, height, copies, sems, columns)
+            kind = EarlyColumns if name in EARLY else Columns
+            units[name] = kind(s, whole, height, copies, sems, columns)
 
     sums = {}
     for at, name in enumerate(order):
@@ -980,11 +1345,17 @@
             sem[kind].at[at]
             for kind in ("gy_sent", "gy_got", "gz_sent", "gz_got", "gb_sent", "gb_got")
         )
-        kind = RowSum if name in ROW_UNITS else ColumnSum
+        kind = RowSum if name in ROW_UNITS else ProductSum if name in TRADED else ColumnSum
         done = None if name == "vector" else ref["o_" + name]
-        wide = ref["g_" + name].shape[-1]
-        sums[name] = kind(s, ref["g_" + name], ref["m_" + name], ref["c_" + name], done, sems,
+        wide = ref["m_" + name].shape[-1]
+        sums[name] = kind(s, ref.get("g_" + name), ref["m_" + name], ref["c_" + name], done, sems,
                           16 if wide > 512 else 32 if name != "vector" else 8)
+    for at, (name, left, right) in enumerate((
+        ("e_qkv", "e_normed", "e_grad_qkv"), ("e_up", "e_lifted", "e_grad_upper"),
+        ("e_down", "e_hidden", "e_branch"),
+    )):
+        sums[name].trade(ref[left], ref[right], ref["l_" + name], ref["r_" + name],
+                         (sem["f_sent"].at[at], sem["f_got"].at[at]))
 
     totals = []
     for at in range(7):
@@ -1001,16 +1372,19 @@
                             ("w_down", "down")):
             ref[key + short] = ref["w_" + key + long]
 
-    first = ("vector", "e_qkv", "e_out", "embed", "e_up")
-    for name in first:
+    for name in order:
         units[name].fetch()
     mine = span(s.blk * own, own)
     own_patches = local(ref["patches"], ref["group"].at[mine])
     own_cotangents = local(ref["cotangent"], ref["cotangents"].at[mine])
     own_patches.start()
     own_cotangents.start()
-    for name in ("e_down", "d_qkv", "d_out", "d_up", "d_down"):
-        units[name].fetch()
+    staged = ref["staged"]
+    staged[...] = jnp.zeros(staged.shape, F32)
+    for at, name in enumerate(VECTOR_NAMES):
+        row = ref[name][...].astype(F32)[None, :]
+        staged[at:at + 1, 0:row.shape[1]] = row
+    ref["w_vector"][span(s.dp * VECTORS, VECTORS)] = staged[...].astype(BF16)
 
     pl.semaphore_wait(barrier, len(peers))
 
@@ -1027,8 +1401,11 @@
         units[name].send()
     for which in range(3):
         shares(ref["patches"], ref["group"], "p", which).start()
-    for name in ("embed", "e_up"):
-        units[name].send()
+    for which in range(3):
+        shares(ref["cotangent"], ref["cotangents"], "c", which).start()
+    units["e_up"].send()
+
+    lay_out(ref, rows, shown, width, dec_width)
     own_patches.wait()
     for which in range(3):
         shares_arrival(ref["patches"], ref["group"], "p", which).wait_recv()
@@ -1053,24 +1430,23 @@
                 gains[at:at + 1, 128 * owner:128 * owner + 128] = row
             elif owner % 2 == 0:
                 pair = VECTORS * (owner + 1) + at
-                gains[at:at + 1, 64 * owner:64 * owner + 128] = row + vectors[pair:pair + 1, :]
+                other = pltpu.roll(vectors[pair:pair + 1, :], 64, 1)
+                gains[at:at + 1, 64 * owner:64 * owner + 128] = row + other
     encoder.norm(True)
-    for name in ("e_qkv", "e_out", "embed"):
-        units[name].forward()
+    units["e_qkv"].forward()
+    units["embed"].send()
+    units["e_out"].forward()
     units["e_qkv"].finish()
     encoder.project()
     encoder.attend(ref["packed_column"], ref["packed_row"])
+    units["e_down"].send()
     units["e_out"].finish()
-    encoder.product(ref["e_mixture"], ref["w_e_out"], ref["e_part"])
-    totals[0].start()
-    units["e_down"].send()
-    for which in range(3):
-        shares(ref["cotangent"], ref["cotangents"], "c", which).start()
-    totals[0].middle()
-    units["embed"].finish()
-    totals[0].end()
-    encoder.add_total(ref["e_whole"])
-    encoder.norm(False)
+    totals[0].begin(encoder.product(ref["e_mixture"], ref["w_e_out"]))
+
+    def after_attention(at):
+        encoder.add_total(at)
+        encoder.norm(False, at * encoder.chunk, encoder.chunk)
+    totals[0].finish(after_attention)
     columns = span(s.part * (dec_width // PARTS), dec_width // PARTS)
 
     def embed_copy(which):
@@ -1085,32 +1461,33 @@
         return remote(block, block, sem["e_sent"].at[which], sem["e_got"].at[which],
                       s.blk_peers[which])
 
-    for which in range(3):
-        embed_copy(which).start()
     units["e_up"].forward()
+    units["e_down"].cross()
+    units["embed"].forward()
     units["d_qkv"].send()
     units["e_up"].finish()
     encoder.expand()
-    units["e_down"].forward()
+    units["embed"].finish()
+    for which in range(3):
+        embed_copy(which).start()
     for name in ("d_out", "d_up"):
         units[name].send()
+    units["e_down"].forward()
+    units["d_qkv"].forward()
+    units["d_down"].send()
     units["e_down"].finish()
-    encoder.product(ref["e_hidden"], ref["w_e_down"], ref["e_part"])
-    totals[1].start()
-    units["d_qkv"].forward()
-    totals[1].middle()
-    units["d_down"].send()
+    totals[1].begin(encoder.product(ref["e_hidden"], ref["w_e_down"]))
     units["d_out"].forward()
     for which in range(3):
         embed_arrival(which).wait_recv()
-    totals[1].end()
-    encoder.add_total(ref["e_whole"])
-
     lowered = ref["lowered"]
 
-    def lower(part):
+    def after_hidden(at):
+        encoder.add_total(at)
+        part = pl.ds(pl.multiple_of(at * encoder.chunk, encoder.chunk), encoder.chunk)
         lowered[part] = residual[part].astype(BF16)
-    each(shown, 32, lower)
+    totals[1].finish(after_hidden)
+
     embedded = dot(lowered[...], ref["w_embed"][...])
     high = embedded.astype(BF16)
     low = (embedded - high.astype(F32)).astype(BF16)
@@ -1124,33 +1501,27 @@
         start[part] = made + ref["dec_code"][part]
     each(rows, 128, place_rows)
     decoder.norm(True)
+    units["d_up"].forward()
     units["d_qkv"].finish()
     decoder.project()
     decoder.attend(ref["ids_column"], ref["ids_row"])
-    units["d_up"].forward()
+    units["d_down"].forward()
     units["d_out"].finish()
-    decoder.product(ref["d_mixture"], ref["w_d_out"], ref["d_part"])
-    totals[2].start()
-    totals[2].middle()
-    units["d_down"].forward()
-    totals[2].end()
-    decoder.add_total(ref["d_whole"])
-    decoder.norm(False)
+    totals[2].begin(decoder.product(ref["d_mixture"], ref["w_d_out"]))
     units["d_up"].finish()
-    decoder.expand()
     units["d_down"].finish()
+    last_part, last_met = ref["last_part"], ref["last_met"]
     quarter = rows // 4
-    last_part, last_met = ref["last_part"], ref["last_met"]
-
-    def last_product(part):
-        at = lax.div(part.start, 64)
+
+    def decoder_rest(at):
+        decoder.add_total(at)
+        decoder.norm(False, at * decoder.chunk, decoder.chunk)
+        decoder.expand(at * decoder.chunk, decoder.chunk)
+        part = pl.ds(pl.multiple_of(at * quarter, quarter), quarter)
         made = dot(ref["d_hidden"][part], ref["w_d_down"][...])
-        per = quarter // 64
-        place = pl.ds(pl.multiple_of(lax.rem(at, per) * 64, 64), 64)
-        block = lax.div(at, per)
-        last_part[lax.div(block, 2), lax.rem(block, 2), place] = made
-    each(rows, 64, last_product)
-    last_sent, last_got = sem["t_sent"].at[7], sem["t_got"].at[7]
+        last_part[lax.div(at, 2), lax.rem(at, 2)] = made
+    totals[2].finish(decoder_rest)
+    last_sent, last_got = sem["t_sent"].at[7, 0], sem["t_got"].at[7, 0]
     last_first = remote(last_part.at[:, 1 - s.core], last_met, last_sent.at[0], last_got.at[0],
                         s.core_peer)
     last_second = remote(ref["last_out"], ref["last_came"], last_sent.at[1], last_got.at[1],
@@ -1161,38 +1532,41 @@
     for which in range(3):
         shares_arrival(ref["cotangent"], ref["cotangents"], "c", which).wait_recv()
     cotangents, grad = ref["cotangents"], ref["d_grad"]
-    decoder.back_hidden(cotangents)
-    decoder.product(ref["d_grad_upper"], ref["w_d_up"], ref["d_part"], back=True)
-    totals[3].start()
+    multiply = decoder.product(ref["d_grad_upper"], ref["w_d_up"], back=True)
+
+    def decoder_hidden(at):
+        decoder.back_hidden(cotangents, at * decoder.chunk, decoder.chunk)
+        multiply(at)
+    totals[3].begin(decoder_hidden)
     last_first.wait_recv()
 
     def last_add(part):
         made = last_part[1 - s.x, s.core, part] + last_met[1 - s.x, part]
         ref["last_out"][part] = made.astype(BF16)
     each(quarter, 64, last_add)
-    totals[3].middle()
     last_second.start()
 
     def copy_grad(part):
         grad[part] = cotangents[part].astype(F32)
     each(rows, 64, copy_grad)
+    vector_grad = ref["g_vector"]
+    vector_grad[...] = jnp.zeros(vector_grad.shape, F32)
+    decoder.clear_sums()
     weight_grad(ref["d_hidden"], cotangents, ref["g_d_down"])
     sums["d_down"].start()
     weight_grad(ref["d_lifted"], ref["d_grad_upper"], ref["g_d_up"])
     sums["d_up"].start()
-    totals[3].end()
-    vector_grad = ref["g_vector"]
-    vector_grad[...] = jnp.zeros(vector_grad.shape, F32)
-    gain, bias = decoder.norm_back(ref["d_whole"], False, ref["d_branch"])
-    vector_store(vector_grad, 7, gain, False)
-    vector_store(vector_grad, 8, bias, False)
-    decoder.back_mixture(ref["d_branch"])
+
+    def decoder_middle(at):
+        decoder.norm_back(at, False, ref["d_branch"])
+        decoder.back_mixture(ref["d_branch"], at * decoder.chunk, decoder.chunk)
+    totals[3].finish(decoder_middle)
+    vector_store(vector_grad, 7, ref["d_sums"][0:1], False)
+    vector_store(vector_grad, 8, ref["d_sums"][1:2], False)
     decoder.attend_back()
     sums["d_down"].middle()
-    decoder.product(ref["d_grad_qkv"], ref["w_d_qkv"], ref["d_part"], back=True)
-    totals[4].start()
+    totals[4].begin(decoder.product(ref["d_grad_qkv"], ref["w_d_qkv"], back=True))
     sums["d_up"].middle()
-    totals[4].middle()
     last_second.wait_recv()
 
     def last_close(part):
@@ -1201,14 +1575,56 @@
         whole = made + ref["last_came"][part].astype(F32) + before
         ref["decoded"][part] = whole.astype(BF16)
     each(quarter, 64, last_close)
+    decoder.clear_sums()
+    weight_grad(ref["d_normed"], ref["d_grad_qkv"], ref["g_d_qkv"])
+    sums["d_qkv"].start()
     weight_grad(ref["d_mixture"], ref["d_branch"], ref["g_d_out"])
     sums["d_out"].start()
-    weight_grad(ref["d_normed"], ref["d_grad_qkv"], ref["g_d_qkv"])
-    sums["d_qkv"].start()
-    totals[4].end()
-    gain, bias = decoder.norm_back(ref["d_whole"], True, ref["d_branch"])
-    vector_store(vector_grad, 5, gain, False)
-    vector_store(vector_grad, 6, bias, False)
+
+    def decoder_first(at):
+        decoder.norm_back(at, True, ref["d_branch_b"])
+    totals[4].finish(decoder_first)
+    picked = ref["picked"]
+    picked[...] = dot(places, ref["d_branch_b"][...]).astype(BF16)
+    encoder_grad = ref["e_grad"]
+
+    def back_embed(part):
+        made = dot_b(picked[...], ref["w_embed"][part])
+        encoder_grad[:, part] = made
+        ref["e_branch"][:, part] = made.astype(BF16)
+    each(width, 256, back_embed)
+
+    sums["e_down"].start()
+    encoder.back_hidden(ref["e_branch"])
+    sums["e_up"].start()
+    totals[5].begin(encoder.product(ref["e_grad_upper"], ref["w_e_up"], back=True))
+    sums["d_down"].join()
+    sums["e_down"].middle()
+    encoder.clear_sums()
+
+    def encoder_middle(at):
+        encoder.norm_back(at, False, ref["e_branch_b"])
+        encoder.back_mixture(ref["e_branch_b"], at * encoder.chunk, encoder.chunk)
+    totals[5].finish(encoder_middle)
+    vector_store(vector_grad, 2, ref["e_sums"][0:1], True)
+    vector_store(vector_grad, 3, ref["e_sums"][1:2], True)
+    sums["e_up"].middle()
+    encoder.attend_back()
+    sums["e_qkv"].start()
+    totals[6].begin(encoder.product(ref["e_grad_qkv"], ref["w_e_qkv"], back=True))
+    weight_grad(ref["e_mixture"], ref["e_branch_b"], ref["g_e_out"])
+    sums["e_out"].start()
+    sums["e_down"].join()
+    encoder.clear_sums()
+    sums["e_qkv"].middle()
+
+    def encoder_first(at):
+        encoder.norm_back(at, True, ref["e_branch_b"])
+    totals[6].finish(encoder_first)
+    vector_store(vector_grad, 0, ref["e_sums"][0:1], True)
+    vector_store(vector_grad, 1, ref["e_sums"][1:2], True)
+    vector_store(vector_grad, 5, ref["d_sums"][0:1], False)
+    vector_store(vector_grad, 6, ref["d_sums"][1:2], False)
 
     def mask_sum(at, total):
         part = pl.ds(pl.multiple_of(at * 64, 64), 64)
@@ -1216,70 +1632,48 @@
         return total + jnp.sum(jnp.where(hidden_row, grad[part], 0.0), axis=0, keepdims=True)
     token_grad = lax.fori_loop(0, rows // 64, mask_sum, jnp.zeros((1, dec_width), F32))
     vector_store(vector_grad, 4, token_grad, False)
-    picked = ref["picked"]
-    picked[...] = dot(places, ref["d_branch"][...]).astype(BF16)
-    grad = ref["e_grad"]
-
-    def back_embed(part):
-        made = dot_b(picked[...], ref["w_embed"][part])
-        grad[:, part] = made
-        ref["e_branch"][:, part] = made.astype(BF16)
-    each(width, 256, back_embed)
-
-    encoder.back_hidden(ref["e_branch"])
-    encoder.product(ref["e_grad_upper"], ref["w_e_up"], ref["e_part"], back=True)
-    totals[5].start()
-    for name in ("d_out", "d_qkv"):
-        sums[name].middle()
-    totals[5].middle()
-    for name in ("d_down", "d_up"):
-        sums[name].last()
-    weight_grad(ref["e_hidden"], ref["e_branch"], ref["g_e_down"])
-    sums["e_down"].start()
-    weight_grad(ref["e_lifted"], ref["e_grad_upper"], ref["g_e_up"])
-    sums["e_up"].start()
+    sums["vector"].start()
     embed_columns = picked.at[:, columns]
     weight_grad(lowered, embed_columns, ref["g_embed"])
     sums["embed"].start()
-    totals[5].end()
-    gain, bias = encoder.norm_back(ref["e_whole"], False, ref["e_branch"])
-    vector_store(vector_grad, 2, gain, True)
-    vector_store(vector_grad, 3, bias, True)
-    encoder.back_mixture(ref["e_branch"])
-    encoder.attend_back()
-    encoder.product(ref["e_grad_qkv"], ref["w_e_qkv"], ref["e_part"], back=True)
-    totals[6].start()
-    weight_grad(ref["e_mixture"], ref["e_branch"], ref["g_e_out"])
-    sums["e_out"].start()
-    totals[6].middle()
-    weight_grad(ref["e_normed"], ref["e_grad_qkv"], ref["g_e_qkv"])
-    sums["e_qkv"].start()
-    totals[6].end()
-    gain, bias = encoder.norm_back(ref["e_whole"], True, ref["e_branch"])
-    vector_store(vector_grad, 0, gain, True)
-    vector_store(vector_grad, 1, bias, True)
-    sums["vector"].start()
-    sums["e_down"].middle()
-    for name in ("d_out", "d_qkv"):
-        sums[name].last()
+    sums["e_out"].middle()
+    for name in ("d_qkv", "d_out"):
+        sums[name].middle()
+    sums["d_up"].join()
+    sums["e_up"].join()
+    sums["d_down"].last()
+    sums["d_up"].last()
+    sums["embed"].middle()
+    sums["vector"].middle()
+    sums["e_down"].last()
+
     rank = ref["rank_column"][mine]
     here = (lax.broadcasted_iota(jnp.int32, (own, shown), 1) == rank).astype(BF16)
 
     def place_grad(part):
-        values = grad[:, part]
+        values = encoder_grad[:, part]
         top = values.astype(BF16)
         rest = (values - top.astype(F32)).astype(BF16)
         ref["grad_patches"][:, part] = dot(here, top) + dot(here, rest)
     each(width, 256, place_grad)
-    for name in ("e_up", "embed", "e_out", "e_qkv", "vector"):
-        sums[name].middle()
-    for name in ("e_down", "e_up", "embed", "e_out", "e_qkv"):
+    sums["e_qkv"].join()
+    sums["d_down"].pass_on()
+    sums["d_up"].pass_on()
+    sums["e_up"].last()
+    sums["e_down"].pass_on()
+    for name in ("e_out", "d_qkv", "d_out", "embed", "vector"):
+        sums[name].join()
+    sums["e_qkv"].last()
+    sums["e_up"].pass_on()
+    for name in ("e_out", "d_qkv", "d_out", "embed"):
         sums[name].last()
 
     def vector_out(part, whole):
         ref["grad_vector"][part] = whole
     sums["vector"].total(vector_out)
     sums["vector"].drain()
+    for name in ("e_qkv", "e_out", "d_qkv", "d_out", "embed"):
+        sums[name].pass_on()
     for name in MESSAGES:
         sums[name].close()
     last_first.wait_send()
@@ -1333,32 +1727,15 @@
     width, dec_width = patches.shape[1], cotangent.shape[1]
     hidden, dec_hidden = e_up.shape[1], d_up.shape[1]
     rows = visible.shape[1]
-    image_ids, scaled, rank = layout(lengths[0], gsd_scale[0], visible[0])
-    places = rank[None, :] == jnp.arange(SHOWN, dtype=jnp.int32)[:, None]
-    packed_ids = jnp.sum(jnp.where(places, image_ids[None, :], 0), axis=1)
-    packed_scaled = jnp.sum(jnp.where(places, scaled[None, :], 0.0), axis=1)
-    side = lax.rem(lax.axis_index("dp"), 2)
-    zero = jnp.zeros((1, 64), BF16)
-
-    def half(vector):
-        row = vector[None, :]
-        return jnp.where(side == 0, jnp.concatenate([row, zero], 1),
-                         jnp.concatenate([zero, row], 1))
-
-    vector = jnp.concatenate(
-        [e_gain_a[None, :], e_bias_a[None, :], e_gain_b[None, :], e_bias_b[None, :], half(mask),
-         half(d_gain_a), half(d_bias_a), half(d_gain_b), half(d_bias_b),
-         jnp.zeros((VECTORS - 9, 128), BF16)], axis=0)
     inputs = {
-        "rank_row": rank[None, :], "rank_column": rank[:, None],
-        "ids_row": image_ids[None, :], "ids_column": image_ids[:, None],
-        "packed_row": packed_ids[None, :], "packed_column": packed_ids[:, None],
-        "code": sincos(packed_scaled, width), "dec_code": sincos(scaled, dec_width),
-        "vector": vector, "patches": patches, "cotangent": cotangent,
+        "lengths": lengths, "gsd": gsd_scale, "visible": visible,
+        "patches": patches, "cotangent": cotangent,
         "query": e_query, "key": e_key, "value": e_value, "out": e_out, "up": e_up,
         "down": e_down, "embed": embed, "dec_query": d_query, "dec_key": d_key,
         "dec_value": d_value, "dec_out": d_out, "dec_up": d_up, "dec_down": d_down,
     }
+    inputs.update(zip(VECTOR_NAMES, (
+        e_gain_a, e_bias_a, e_gain_b, e_bias_b, mask, d_gain_a, d_bias_a, d_gain_b, d_bias_b)))
     units = unit_shapes(width, dec_width, hidden, dec_hidden)
     shapes = {
         "decoded": (cotangent.shape, BF16), "grad_patches": (patches.shape, F32),
@@ -1371,15 +1748,16 @@
     table = scratch_table(width, dec_width, hidden, dec_hidden, rows, SHOWN)
     names = INPUTS + tuple("o_" + name if name in MESSAGES else name for name in RESULTS)
     names = names + tuple(table) + tuple("s_" + name for name in SEMAPHORES)
-    in_vmem = INPUTS[:9]
+    spaces = {"lengths": pltpu.SMEM, "gsd": pltpu.SMEM, "visible": pltpu.VMEM}
+    spaces.update({name: pltpu.VMEM for name in VECTOR_NAMES})
     results = pl.pallas_call(
         functools.partial(main_kernel, names),
         out_shape=[jax.ShapeDtypeStruct(*shapes[name]) for name in RESULTS],
-        in_specs=[
-            pl.BlockSpec(memory_space=pltpu.VMEM if name in in_vmem else pl.ANY)
-            for name in INPUTS
+        in_specs=[pl.BlockSpec(memory_space=spaces.get(name, pl.ANY)) for name in INPUTS],
+        out_specs=[
+            pl.BlockSpec(memory_space=pl.ANY if name in MESSAGES else pltpu.VMEM)
+            for name in RESULTS
         ],
-        out_specs=[pl.BlockSpec(memory_space=pltpu.VMEM) for name in RESULTS],
         scratch_shapes=[pltpu.VMEM(*entry) for entry in table.values()]
         + [pltpu.SemaphoreType.DMA(shape) for shape in SEMAPHORES.values()],
         compiler_params=pltpu.CompilerParams(
@@ -1407,7 +1785,7 @@
         out_shape=[jax.ShapeDtypeStruct(*entry) for entry in finals.values()],
         in_specs=[pl.BlockSpec(memory_space=pltpu.VMEM)] * len(made),
         out_specs=[pl.BlockSpec(memory_space=pltpu.VMEM)] * len(finals),
-        compiler_params=pltpu.CompilerParams(vmem_limit_bytes=40 * MIB),
+        compiler_params=pltpu.CompilerParams(vmem_limit_bytes=62 * MIB),
     )(*made.values())
     return tuple(
         output.reshape(-1) if output.shape[0] == 1 else output for output in outputs

time: 345 us -> 258 us (0.75)
  Pallas kernels: 315 us -> 255 us
  local copies, waits for them, and re-layouts: 15.6 us -> 0 us
  other arithmetic: 12.2 us -> 0 us
    pallas_call x1, Pallas kernels: 312 us -> 249 us  [local_kernel(): pl.pallas_call(functools.partial(main_kernel, names), out_shape=[jax.Shap...]
    unnamed x30 -> x0, local copies, waits for them, and re-layouts: 11.7 us -> none
    select_n x5 -> x0, other arithmetic: 3.86 us -> none  [the longest x3 2.43 us: half(): jnp.where(side == 0, jnp.concatenate([row, zero], 1), jnp.concatenate([ze...]
where the time goes in v3:
time: 258 us; the launch traced here: 256 us
  Pallas kernels  255 us (99%)
    pallas_call x1, Pallas kernels, local_kernel(): pl.pallas_call(functools.partial(main_kernel, names), out_shape=[jax.Shap...  249 us
    pallas_call x1, Pallas kernels, local_kernel(): pl.pallas_call(functools.partial(unpack_kernel, tuple(made) + tuple(final...  5.84 us

profile of v3, /device:TPU:0, one launch (start us, length us, event | category | flops | bytes accessed | tf_op | source)
XLA Modules:
  0.0 256.0 jit_solution(16480596230834046130)
XLA Ops:
  0.7 249.3 %shard_map.442 = (bf16[128,512]{1,0:T(8,128)(2,1)}, f32[128,1024]{1,0:T(8,128)}, f32[16,128]{1,0:T(8,128)}, bf16[4,128,768]{2,1,0:T(8,128)(2,1)}, bf16[4,128,102...) custom-call(s32[1,8]{1,0:T(1,128)} %refs_0_.1, ...), custom_call_target="tpu_custom_call" | custom-call | tf_op jit(solution)/shard_map/pallas_call | solution.py:1753
  250.0 5.8 %shard_map.443 = (bf16[128,512]{1,0:T(8,128)(2,1)}, f32[128,1024]{1,0:T(8,128)}, f32[1,128]{1,0:T(1,128)}, f32[1,128]{1,0:T(1,128)}, f32[128,1024]{1,0:T(8,128)}...) custom-call(bf16[128,512]{1,0:T(8,128)(2,1)} %get-tuple-element.60.r, ...), custom_call_target="tpu_custom_call" | custom-call | tf_op jit(solution)/shard_map/pallas_call | solution.py:1783

commit v4 on v3

--- a/solution.py
+++ b/solution.py
@@ -335,127 +335,175 @@
     def __init__(self, split, whole, rows, local, sems, columns=None):
         self.split, self.whole, self.rows, self.local = split, whole, rows, local
         self.columns = columns
-        self.z_sent, self.z_got, self.y_sent, self.y_got = sems
-
-    def block(self, z, y):
-        rows = span((z * 2 + y) * self.rows, self.rows)
+        self.z_sent, self.z_got, self.y_sent, self.y_got = sems[:4]
+        self.cross_sent, self.cross_got = sems[4:]
+
+    def view(self, rows):
         if self.columns is None:
             return self.whole.at[rows]
         return self.whole.at[rows, self.columns]
 
-    def z_copy(self, step, y=None):
-        s = self.split
-        block = self.block(s.z, s.y if y is None else y)
-        at = 0 if y is None else 1
-        return remote(block, block, self.z_sent.at[at, step - 1], self.z_got.at[at, s.z],
-                      s.at_z(s.inward(step)))
-
-    def z_arrival(self, z, y=None):
-        s = self.split
-        block = self.block(z, s.y if y is None else y)
-        at = 0 if y is None else 1
-        return remote(block, block, self.z_sent.at[at, 0], self.z_got.at[at, z], s.y_peer)
-
-    def relay(self, y=None):
-        s = self.split
-        block = self.block(s.far_end, s.y if y is None else y)
-        at = 0 if y is None else 1
-        return remote(block, block, self.z_sent.at[at, 3], self.z_got.at[at, s.far_end],
-                      s.at_z(s.near_end))
+    def block(self, z, y):
+        return self.view(span((z * 2 + y) * self.rows, self.rows))
+
+    def lane(self, crossed):
+        s = self.split
+        if crossed:
+            return 1 - s.y, self.cross_sent, self.cross_got
+        return s.y, self.z_sent, self.z_got
+
+    def z_copy(self, step, crossed=False):
+        s = self.split
+        y, sent, got = self.lane(crossed)
+        block = self.block(s.z, y)
+        return remote(block, block, sent, got.at[s.z], s.at_z(s.inward(step)))
+
+    def z_arrival(self, z, crossed=False):
+        y, sent, got = self.lane(crossed)
+        block = self.block(z, y)
+        return remote(block, block, sent, got.at[z], self.split.y_peer)
+
+    def relay(self, crossed=False):
+        s = self.split
+        y, sent, got = self.lane(crossed)
+        block = self.block(s.far_end, y)
+        return remote(block, block, sent, got.at[s.far_end], s.at_z(s.near_end))
 
     def y_copy(self, z, at):
         s = self.split
         block = self.block(z, s.y)
-        return remote(block, block, self.y_sent.at[at], self.y_got.at[at], s.y_peer)
+        return remote(block, block, self.y_sent, self.y_got.at[at], s.y_peer)
 
     def y_arrival(self, z, at):
         s = self.split
         block = self.block(z, 1 - s.y)
-        return remote(block, block, self.y_sent.at[at], self.y_got.at[at], s.y_peer)
+        return remote(block, block, self.y_sent, self.y_got.at[at], s.y_peer)
+
+    def sent(self, sem, count):
+        blocks = self.view(pl.ds(0, count * self.rows))
+        remote(blocks, blocks, sem, self.y_got.at[0], self.split.y_peer).wait_send()
 
     def fetch(self):
         for copy in self.local:
             copy.start()
 
-    def spread(self, y=None):
-        self.z_copy(1, y).start()
-        self.z_copy(2, y).start()
+    def spread(self, crossed=False):
+        self.z_copy(1, crossed).start()
+        self.z_copy(2, crossed).start()
 
         @pl.when(self.split.inner)
         def _():
-            self.z_copy(3, y).start()
-
-    def collect(self, step, y=None):
+            self.z_copy(3, crossed).start()
+
+    def collect(self, step, crossed=False):
         s = self.split
         z = s.inward(step)
-        self.z_arrival(z, y).wait_recv()
+        self.z_arrival(z, crossed).wait_recv()
         if step == 2:
             @pl.when(s.inner)
             def _():
-                self.relay(y).start()
+                self.relay(crossed).start()
         return z
 
-    def send(self):
+    def send(self, y_too=True):
         for copy in self.local:
             copy.wait()
         self.spread()
+        if y_too:
+            self.send_y()
+
+    def send_y(self):
         self.y_copy(self.split.z, 0).start()
 
-    def forward(self):
-        for step in (1, 2, 3):
+    def forward(self, steps=(1, 2, 3)):
+        for step in steps:
             self.y_copy(self.collect(step), step).start()
 
     def finish(self):
         for step in range(PARTS):
             self.y_arrival(self.split.inward(step), step).wait_recv()
 
-    def drain_z(self, y=None):
-        self.z_copy(1, y).wait_send()
-        self.z_copy(2, y).wait_send()
-
+    def drain_z(self, sem):
         @pl.when(self.split.inner)
         def _():
-            self.z_copy(3, y).wait_send()
-            self.relay(y).wait_send()
+            self.sent(sem, 4)
+
+        @pl.when(jnp.logical_not(self.split.inner))
+        def _():
+            self.sent(sem, 2)
 
     def drain(self):
-        self.drain_z()
-        for step in range(PARTS):
-            self.y_copy(self.split.inward(step), step).wait_send()
+        self.drain_z(self.z_sent)
+        self.sent(self.y_sent, PARTS)
 
 
 class EarlyColumns(Columns):
     def cross(self):
         s = self.split
         self.y_arrival(s.z, 0).wait_recv()
-        self.spread(1 - s.y)
-
-    def forward(self):
-        for step in (1, 2, 3):
+        self.spread(True)
+
+    def forward(self, steps=(1, 2, 3)):
+        for step in steps:
             self.collect(step)
 
+    def finish(self, steps=(1, 2, 3)):
+        for step in steps:
+            self.collect(step, True)
+
+    def drain(self):
+        self.drain_z(self.z_sent)
+        self.drain_z(self.cross_sent)
+        self.sent(self.y_sent, 1)
+
+
+class Shared:
+    def __init__(self, split, source, block, sems):
+        self.split, self.source, self.block = split, source, block
+        self.sents, self.gots = sems
+
+    def copy(self, which):
+        s = self.split
+        if which == 2:
+            block = self.block(s.x_peer[1])
+            return remote(block, block, self.sents.at[2], self.gots.at[2], s.core_peer)
+        return remote(self.source, self.block(s.blk), self.sents.at[which],
+                      self.gots.at[which], s.blk_peers[which])
+
+    def arrival(self, which):
+        s = self.split
+        block = self.block(s.blk_peers[which][1])
+        return remote(block, block, self.sents.at[which], self.gots.at[which], s.core_peer)
+
+    def start(self):
+        self.copy(1).start()
+        self.copy(0).start()
+
+    def pass_on(self):
+        self.arrival(1).wait_recv()
+        self.copy(2).start()
+
     def finish(self):
-        for step in (1, 2, 3):
-            self.collect(step, 1 - self.split.y)
+        self.arrival(0).wait_recv()
+        self.arrival(2).wait_recv()
 
     def drain(self):
-        self.drain_z()
-        self.drain_z(1 - self.split.y)
-        self.y_copy(self.split.z, 0).wait_send()
+        for which in range(3):
+            self.copy(which).wait_send()
 
 
 class Rows:
     def __init__(self, split, whole, rows, local, sems):
         self.split, self.whole, self.rows, self.local = split, whole, rows, local
-        self.z_sent, self.z_got, self.y_sent, self.y_got = sems
+        self.z_sent, self.z_got, self.y_sent, self.y_got = sems[:4]
 
     def block(self, y):
         return self.whole.at[span(y * self.rows, self.rows)]
 
     def z_copy(self, way):
         s = self.split
-        return remote(self.block(s.y), self.block(s.y), self.z_sent.at[0, way],
-                      self.z_got.at[0, 0], s.at_z(s.z + 1 - 2 * way))
+        return remote(self.block(s.y), self.block(s.y), self.z_got.at[1 + way],
+                      self.z_got.at[0], s.at_z(s.z + 1 - 2 * way))
 
     def pass_on(self, act):
         s = self.split
@@ -470,7 +518,7 @@
 
     def y_copy(self):
         s = self.split
-        return remote(self.block(s.y), self.block(s.y), self.y_sent.at[0],
+        return remote(self.block(s.y), self.block(s.y), self.y_sent,
                       self.y_got.at[0], s.y_peer)
 
     def fetch(self):
@@ -490,15 +538,15 @@
 
         @pl.when(s.z != s.part)
         def _():
-            remote(self.block(s.y), self.block(s.y), self.z_sent.at[0, 0],
-                   self.z_got.at[0, 0], s.y_peer).wait_recv()
+            remote(self.block(s.y), self.block(s.y), self.z_sent,
+                   self.z_got.at[0], s.y_peer).wait_recv()
             self.pass_on(lambda copy: copy.start())
             self.y_copy().start()
 
     def finish(self):
         s = self.split
         block = self.block(1 - s.y)
-        remote(block, block, self.y_sent.at[0], self.y_got.at[0], s.y_peer).wait_recv()
+        remote(block, block, self.y_sent, self.y_got.at[0], s.y_peer).wait_recv()
 
     def drain(self):
         self.pass_on(lambda copy: copy.wait_send())
@@ -663,9 +711,13 @@
 
 
 class ProductSum(ColumnSum):
-    def trade(self, left, right, their_left, their_right, sems):
+    def trade(self, left, right, their_left, their_right, sems, told=None, heard=None, after=None):
         self.left, self.right = left, right
         self.their_left, self.their_right = their_left, their_right
+        self.told = right if told is None else told
+        self.heard = their_right if heard is None else heard
+        self.tells = told is not False
+        self.after = after
         self.t_sent, self.t_got = sems
         self.width = their_left.shape[2]
 
@@ -674,19 +726,23 @@
 
     def left_copy(self, z):
         s = self.split
-        return remote(self.columns(z, 1 - s.y), self.their_left.at[z], self.t_sent.at[z],
-                      self.t_got.at[z], s.y_peer)
+        return remote(self.columns(z, 1 - s.y), self.their_left.at[z], self.t_sent.at[0],
+                      self.t_got.at[0], s.y_peer)
+
+    def left_copies(self):
+        return remote(self.their_left, self.their_left, self.t_sent.at[0], self.t_got.at[0],
+                      self.split.y_peer)
 
     def right_copy(self):
-        return remote(self.right, self.their_right, self.t_sent.at[PARTS],
-                      self.t_got.at[PARTS], self.split.y_peer)
-
-    def copies(self):
-        return [self.right_copy()] + [self.left_copy(z) for z in range(PARTS)]
+        return remote(self.told, self.heard, self.t_sent.at[1], self.t_got.at[1],
+                      self.split.y_peer)
+
+    def start_left(self):
+        for z in range(PARTS):
+            self.left_copy(z).start()
 
     def start(self):
-        for copy in self.copies():
-            copy.start()
+        self.right_copy().start()
 
     def add(self, z):
         both = dot_t(self.columns(z, self.split.y)[...], self.right[...]) + dot_t(
@@ -694,12 +750,16 @@
         self.met[z] = both.astype(self.met.dtype)
 
     def arrive(self):
-        for copy in self.copies():
-            copy.wait_recv()
+        self.left_copies().wait_recv()
+        if self.tells:
+            self.right_copy().wait_recv()
+        if self.after is not None:
+            self.after()
 
     def drain_y(self):
-        for copy in self.copies():
-            copy.wait_send()
+        self.left_copies().wait_send()
+        if self.tells:
+            self.right_copy().wait_send()
 
 
 class RowSum:
@@ -1032,7 +1092,8 @@
             moved, gains, biases = norm_back(self.halves(rows), unit[rows], scale[rows], gain)
             new = grad[rows] + moved
             grad[rows] = new
-            out[rows] = new.astype(BF16)
+            if out is not None:
+                out[rows] = new.astype(BF16)
             sums[0:1] += gains
             sums[1:2] += biases
         each(self.chunk, self.tile, body, at * self.chunk)
@@ -1110,9 +1171,10 @@
 
 COLUMN_UNITS = ("e_qkv", "e_up", "e_down", "embed", "d_qkv", "d_up")
 ROW_UNITS = ("e_out", "d_out", "d_down")
+ROW_SUMS = ("d_out", "d_down")
 MESSAGES = COLUMN_UNITS + ROW_UNITS
-TRADED = ("e_qkv", "e_up", "e_down")
-EARLY = ("e_down",)
+TRADED = ("e_qkv", "e_up", "e_down", "e_out", "embed")
+EARLY = ()
 
 
 def unit_shapes(width, dec_width, hidden, dec_hidden):
@@ -1142,11 +1204,20 @@
         if name in TRADED:
             del table["g_" + name]
             table["l_" + name] = ((PARTS, shown, 128), BF16)
-            table["r_" + name] = ((shown, columns), BF16)
+            if name != "embed":
+                table["r_" + name] = ((shown, columns), BF16)
     table["w_embed"] = ((width, dec_width), BF16)
     for name in ROW_UNITS:
         height, columns = units[name]
         table["w_" + name] = ((2 * height, columns), BF16)
+        if name == "e_out":
+            narrow = columns // PARTS
+            table["m_e_out"] = ((PARTS, height, narrow), BF16)
+            table["c_e_out"] = ((PARTS, height, narrow), BF16)
+            table["l_e_out"] = ((PARTS, shown, 128), BF16)
+            table["r_e_out"] = ((shown, narrow), BF16)
+            table["mixture_all"] = ((shown, width), BF16)
+            continue
         table["g_" + name] = ((SIDES, height, columns), BF16)
         table["m_" + name] = ((height, columns), BF16)
         table["c_" + name] = ((2, height, columns), BF16)
@@ -1194,6 +1265,7 @@
     ):
         table[name] = (shape, kind)
     table["lowered"] = ((shown, width), BF16)
+    table["their_picked"] = ((shown, dec_width), BF16)
     table["picked"] = ((shown, dec_width), BF16)
     return table
 
@@ -1208,13 +1280,14 @@
 )
 RESULTS = ("decoded", "grad_patches", "grad_vector") + MESSAGES
 SEMAPHORES = {
-    "local": (40,),
-    "z_sent": (10, 2, 4), "z_got": (10, 2, 4), "y_sent": (10, 4), "y_got": (10, 4),
-    "gy_sent": (10,), "gy_got": (10,), "gz_sent": (10, 3), "gz_got": (10, 4),
-    "f_sent": (3, 5), "f_got": (3, 5),
-    "gb_sent": (10, 4), "gb_got": (10, 3),
+    "local": (24,),
+    "z_sent": (11,), "z_got": (11, 4), "y_sent": (11,), "y_got": (11, 4),
+    "cross_sent": (1,), "cross_got": (1, 4),
+    "gy_sent": (11,), "gy_got": (11,), "gz_sent": (11, 3), "gz_got": (11, 4),
+    "f_sent": (5, 2), "f_got": (5, 2), "m_sent": (3,), "m_got": (3,), "gb_sent": (11, 4), "gb_got": (11, 3),
     "p_sent": (3,), "p_got": (3,), "c_sent": (3,), "c_got": (3,),
-    "e_sent": (3,), "e_got": (3,), "t_sent": (8, 4, 3), "t_got": (8, 4, 3),
+    "e_sent": (3,), "e_got": (3,), "l_sent": (2,), "l_got": (2,),
+    "e_t_sent": (2, 2, 3), "e_t_got": (2, 2, 3), "d_t_sent": (2, 4, 3), "d_t_got": (2, 4, 3),
 }
 
 
@@ -1293,12 +1366,13 @@
     for peer in peers:
         pl.semaphore_signal(barrier, inc=1, device_id=peer, device_id_type=pl.DeviceIdType.MESH)
 
-    order = ("vector", "e_qkv", "e_out", "e_up", "embed", "e_down", "d_qkv", "d_out", "d_up",
-             "d_down")
+    order = ("vector", "e_qkv", "e_out", "e_up", "embed", "e_down", "e_down_b", "d_qkv", "d_out",
+             "d_up", "d_down")
     units = {}
     for at, name in enumerate(order):
         sems = tuple(sem[kind].at[at] for kind in ("z_sent", "z_got", "y_sent", "y_got"))
-        whole = ref["w_" + name]
+        sems = sems + (sem["cross_sent"].at[0], sem["cross_got"].at[0])
+        whole = ref["w_e_down" if name == "e_down_b" else "w_" + name]
         if name == "vector":
             units[name] = Columns(s, whole, VECTORS, [], sems)
         elif name in ROW_UNITS:
@@ -1307,7 +1381,7 @@
             copy = local(source, whole.at[span(s.y * height, height)])
             units[name] = Rows(s, whole, height, copy, sems)
         else:
-            height = ref["m_" + name].shape[1]
+            height = ref["m_e_down" if name == "e_down_b" else "m_" + name].shape[1]
             mine = span(s.dp * height, height)
             columns = None
             if name in ("e_qkv", "d_qkv"):
@@ -1327,8 +1401,11 @@
                           whole.at[mine, pl.ds(owner * size, size)])
                     for owner in range(8)
                 ]
-            elif name == "e_down":
-                copies = [local(ref["down"].at[span(s.blk * height, height)], whole.at[mine])]
+            elif name in ("e_down", "e_down_b"):
+                size = width // 2
+                columns = pl.ds(size if name == "e_down_b" else 0, size)
+                copies = [local(ref["down"].at[span(s.blk * height, height), columns],
+                                whole.at[mine, columns])]
             elif name == "embed":
                 size = dec_width // PARTS
                 columns = span(s.part * size, size)
@@ -1341,28 +1418,44 @@
 
     sums = {}
     for at, name in enumerate(order):
+        if name == "e_down_b":
+            continue
         sems = tuple(
             sem[kind].at[at]
             for kind in ("gy_sent", "gy_got", "gz_sent", "gz_got", "gb_sent", "gb_got")
         )
-        kind = RowSum if name in ROW_UNITS else ProductSum if name in TRADED else ColumnSum
+        kind = RowSum if name in ROW_SUMS else ProductSum if name in TRADED else ColumnSum
         done = None if name == "vector" else ref["o_" + name]
         wide = ref["m_" + name].shape[-1]
         sums[name] = kind(s, ref.get("g_" + name), ref["m_" + name], ref["c_" + name], done, sems,
                           16 if wide > 512 else 32 if name != "vector" else 8)
-    for at, (name, left, right) in enumerate((
-        ("e_qkv", "e_normed", "e_grad_qkv"), ("e_up", "e_lifted", "e_grad_upper"),
-        ("e_down", "e_hidden", "e_branch"),
+    def their_embed():
+        def body(part):
+            made = dot_b(ref["their_picked"][...], ref["w_embed"][part])
+            ref["r_e_down"][:, part] = made.astype(BF16)
+        each(width, 256, body)
+
+    picked, their_picked = ref["picked"], ref["their_picked"]
+    embed_columns = span(s.part * (dec_width // PARTS), dec_width // PARTS)
+    out_columns = span(s.part * (width // PARTS), width // PARTS)
+    for at, (name, left, right, their_right, more) in enumerate((
+        ("e_qkv", "e_normed", ref["e_grad_qkv"], ref["r_e_qkv"], ()),
+        ("e_up", "e_lifted", ref["e_grad_upper"], ref["r_e_up"], ()),
+        ("e_down", "e_hidden", ref["e_branch"], ref["r_e_down"],
+         (picked, their_picked, their_embed)),
+        ("e_out", "mixture_all", ref["e_branch_b"].at[:, out_columns], ref["r_e_out"], ()),
+        ("embed", "lowered", picked.at[:, embed_columns], their_picked.at[:, embed_columns],
+         (False,)),
     )):
-        sums[name].trade(ref[left], ref[right], ref["l_" + name], ref["r_" + name],
-                         (sem["f_sent"].at[at], sem["f_got"].at[at]))
+        sums[name].trade(ref[left], right, ref["l_" + name], their_right,
+                         (sem["f_sent"].at[at], sem["f_got"].at[at]), *more)
 
     totals = []
     for at in range(7):
         key, slot = ("e_", at % 2) if at in (0, 1, 5, 6) else ("d_", at % 2)
         totals.append(Total(
             s, *(ref[key + name] for name in ("part", "met", "out", "came", "whole")),
-            (sem["t_sent"].at[at], sem["t_got"].at[at]), slot,
+            (sem[key + "t_sent"].at[slot], sem[key + "t_got"].at[slot]), slot,
         ))
 
     encoder = Block(shown, width, 4, 64, "e_", ref, 0)
@@ -1388,27 +1481,35 @@
 
     pl.semaphore_wait(barrier, len(peers))
 
-    def shares(source, target, kind, which):
-        return remote(source, target.at[mine], sem[kind + "_sent"].at[which],
-                      sem[kind + "_got"].at[which], s.blk_peers[which])
-
-    def shares_arrival(source, target, kind, which):
-        place = span(s.blk_peers[which][1] * own, own)
-        return remote(source, target.at[place], sem[kind + "_sent"].at[which],
-                      sem[kind + "_got"].at[which], s.blk_peers[which])
-
+    def place_in(name):
+        return lambda blk: ref[name].at[span(blk * own, own)]
+
+    def embed_block(blk):
+        size = dec_width // PARTS
+        return ref["w_embed"].at[:, span(lax.rem(3 * blk, PARTS) * size, size)]
+
+    def mixture_block(blk):
+        size = width // PARTS
+        return ref["mixture_all"].at[:, span(lax.rem(3 * blk, PARTS) * size, size)]
+
+    shared = {
+        "p": Shared(s, ref["patches"], place_in("group"), (sem["p_sent"], sem["p_got"])),
+        "c": Shared(s, ref["cotangent"], place_in("cotangents"), (sem["c_sent"], sem["c_got"])),
+        "e": Shared(s, embed_block(s.blk), embed_block, (sem["e_sent"], sem["e_got"])),
+        "m": Shared(s, ref["e_mixture"], mixture_block, (sem["m_sent"], sem["m_got"])),
+    }
     for name in ("vector", "e_qkv", "e_out"):
         units[name].send()
-    for which in range(3):
-        shares(ref["patches"], ref["group"], "p", which).start()
-    for which in range(3):
-        shares(ref["cotangent"], ref["cotangents"], "c", which).start()
+    shared["p"].start()
     units["e_up"].send()
 
     lay_out(ref, rows, shown, width, dec_width)
+    units["vector"].forward()
+    units["e_qkv"].forward()
+    shared["p"].pass_on()
     own_patches.wait()
-    for which in range(3):
-        shares_arrival(ref["patches"], ref["group"], "p", which).wait_recv()
+    units["e_out"].forward()
+    shared["p"].finish()
 
     places = (
         lax.broadcasted_iota(jnp.int32, (shown, rows), 0) == ref["rank_row"][...]
@@ -1419,7 +1520,7 @@
         residual[:, columns] = dot(places, ref["group"][:, columns]) + ref["code"][:, columns]
     each(width, 256, place_patches)
 
-    units["vector"].forward()
+    units["e_up"].forward((1,))
     units["vector"].finish()
     vectors = ref["w_vector"][...].astype(F32)
     gains = ref["gains"]
@@ -1433,53 +1534,45 @@
                 other = pltpu.roll(vectors[pair:pair + 1, :], 64, 1)
                 gains[at:at + 1, 64 * owner:64 * owner + 128] = row + other
     encoder.norm(True)
-    units["e_qkv"].forward()
+    units["e_up"].forward((2,))
     units["embed"].send()
-    units["e_out"].forward()
+    units["e_down"].send()
     units["e_qkv"].finish()
     encoder.project()
+    units["e_up"].forward((3,))
     encoder.attend(ref["packed_column"], ref["packed_row"])
-    units["e_down"].send()
+    ref["mixture_all"][:, out_columns] = ref["e_mixture"][...]
     units["e_out"].finish()
     totals[0].begin(encoder.product(ref["e_mixture"], ref["w_e_out"]))
+    units["embed"].forward()
 
     def after_attention(at):
         encoder.add_total(at)
         encoder.norm(False, at * encoder.chunk, encoder.chunk)
     totals[0].finish(after_attention)
-    columns = span(s.part * (dec_width // PARTS), dec_width // PARTS)
-
-    def embed_copy(which):
-        block = ref["w_embed"].at[:, columns]
-        return remote(block, block, sem["e_sent"].at[which], sem["e_got"].at[which],
-                      s.blk_peers[which])
-
-    def embed_arrival(which):
-        size = dec_width // PARTS
-        place = span(lax.rem(3 * s.blk_peers[which][1], PARTS) * size, size)
-        block = ref["w_embed"].at[:, place]
-        return remote(block, block, sem["e_sent"].at[which], sem["e_got"].at[which],
-                      s.blk_peers[which])
-
-    units["e_up"].forward()
-    units["e_down"].cross()
-    units["embed"].forward()
-    units["d_qkv"].send()
+    shared["c"].start()
+    shared["m"].start()
+    units["e_down"].forward()
+    units["e_down_b"].send()
     units["e_up"].finish()
     encoder.expand()
+    units["d_qkv"].send()
+    units["d_out"].send()
     units["embed"].finish()
-    for which in range(3):
-        embed_copy(which).start()
-    for name in ("d_out", "d_up"):
-        units[name].send()
-    units["e_down"].forward()
+    shared["e"].start()
+    shared["c"].pass_on()
+    shared["m"].pass_on()
+    units["e_down_b"].forward()
+    units["d_up"].send()
+    units["d_down"].send()
     units["d_qkv"].forward()
-    units["d_down"].send()
+    shared["e"].pass_on()
     units["e_down"].finish()
+    units["e_down_b"].finish()
     totals[1].begin(encoder.product(ref["e_hidden"], ref["w_e_down"]))
     units["d_out"].forward()
-    for which in range(3):
-        embed_arrival(which).wait_recv()
+    units["d_up"].forward()
+    shared["e"].finish()
     lowered = ref["lowered"]
 
     def after_hidden(at):
@@ -1501,11 +1594,10 @@
         start[part] = made + ref["dec_code"][part]
     each(rows, 128, place_rows)
     decoder.norm(True)
-    units["d_up"].forward()
+    units["d_down"].forward()
     units["d_qkv"].finish()
     decoder.project()
     decoder.attend(ref["ids_column"], ref["ids_row"])
-    units["d_down"].forward()
     units["d_out"].finish()
     totals[2].begin(decoder.product(ref["d_mixture"], ref["w_d_out"]))
     units["d_up"].finish()
@@ -1521,7 +1613,7 @@
         made = dot(ref["d_hidden"][part], ref["w_d_down"][...])
         last_part[lax.div(at, 2), lax.rem(at, 2)] = made
     totals[2].finish(decoder_rest)
-    last_sent, last_got = sem["t_sent"].at[7, 0], sem["t_got"].at[7, 0]
+    last_sent, last_got = sem["l_sent"], sem["l_got"]
     last_first = remote(last_part.at[:, 1 - s.core], last_met, last_sent.at[0], last_got.at[0],
                         s.core_peer)
     last_second = remote(ref["last_out"], ref["last_came"], last_sent.at[1], last_got.at[1],
@@ -1529,8 +1621,10 @@
     last_first.start()
 
     own_cotangents.wait()
-    for which in range(3):
-        shares_arrival(ref["cotangent"], ref["cotangents"], "c", which).wait_recv()
+    shared["c"].finish()
+    shared["m"].finish()
+    for name in ("e_down", "embed", "e_up", "e_out", "e_qkv"):
+        sums[name].start_left()
     cotangents, grad = ref["cotangents"], ref["d_grad"]
     multiply = decoder.product(ref["d_grad_upper"], ref["w_d_up"], back=True)
 
@@ -1584,8 +1678,8 @@
     def decoder_first(at):
         decoder.norm_back(at, True, ref["d_branch_b"])
     totals[4].finish(decoder_first)
-    picked = ref["picked"]
     picked[...] = dot(places, ref["d_branch_b"][...]).astype(BF16)
+    sums["e_down"].start()
     encoder_grad = ref["e_grad"]
 
     def back_embed(part):
@@ -1593,12 +1687,13 @@
         encoder_grad[:, part] = made
         ref["e_branch"][:, part] = made.astype(BF16)
     each(width, 256, back_embed)
-
-    sums["e_down"].start()
+    sums["d_down"].join()
+
     encoder.back_hidden(ref["e_branch"])
     sums["e_up"].start()
     totals[5].begin(encoder.product(ref["e_grad_upper"], ref["w_e_up"], back=True))
-    sums["d_down"].join()
+    sums["d_qkv"].middle()
+    sums["d_out"].middle()
     sums["e_down"].middle()
     encoder.clear_sums()
 
@@ -1606,21 +1701,32 @@
         encoder.norm_back(at, False, ref["e_branch_b"])
         encoder.back_mixture(ref["e_branch_b"], at * encoder.chunk, encoder.chunk)
     totals[5].finish(encoder_middle)
-    vector_store(vector_grad, 2, ref["e_sums"][0:1], True)
-    vector_store(vector_grad, 3, ref["e_sums"][1:2], True)
+    sums["e_out"].start()
+    sums["d_up"].join()
     sums["e_up"].middle()
     encoder.attend_back()
     sums["e_qkv"].start()
     totals[6].begin(encoder.product(ref["e_grad_qkv"], ref["w_e_qkv"], back=True))
-    weight_grad(ref["e_mixture"], ref["e_branch_b"], ref["g_e_out"])
-    sums["e_out"].start()
+    sums["d_down"].last()
+    sums["d_qkv"].join()
+    sums["d_out"].join()
+    sums["d_up"].last()
+    sums["e_out"].middle()
+    sums["embed"].middle()
+    vector_store(vector_grad, 2, ref["e_sums"][0:1], True)
+    vector_store(vector_grad, 3, ref["e_sums"][1:2], True)
+    encoder.clear_sums()
     sums["e_down"].join()
-    encoder.clear_sums()
     sums["e_qkv"].middle()
 
     def encoder_first(at):
-        encoder.norm_back(at, True, ref["e_branch_b"])
+        encoder.norm_back(at, True, None)
     totals[6].finish(encoder_first)
+    sums["e_up"].join()
+    sums["d_down"].pass_on()
+    sums["d_up"].pass_on()
+    sums["d_qkv"].last()
+    sums["d_out"].last()
     vector_store(vector_grad, 0, ref["e_sums"][0:1], True)
     vector_store(vector_grad, 1, ref["e_sums"][1:2], True)
     vector_store(vector_grad, 5, ref["d_sums"][0:1], False)
@@ -1633,20 +1739,6 @@
     token_grad = lax.fori_loop(0, rows // 64, mask_sum, jnp.zeros((1, dec_width), F32))
     vector_store(vector_grad, 4, token_grad, False)
     sums["vector"].start()
-    embed_columns = picked.at[:, columns]
-    weight_grad(lowered, embed_columns, ref["g_embed"])
-    sums["embed"].start()
-    sums["e_out"].middle()
-    for name in ("d_qkv", "d_out"):
-        sums[name].middle()
-    sums["d_up"].join()
-    sums["e_up"].join()
-    sums["d_down"].last()
-    sums["d_up"].last()
-    sums["embed"].middle()
-    sums["vector"].middle()
-    sums["e_down"].last()
-
     rank = ref["rank_column"][mine]
     here = (lax.broadcasted_iota(jnp.int32, (own, shown), 1) == rank).astype(BF16)
 
@@ -1656,34 +1748,36 @@
         rest = (values - top.astype(F32)).astype(BF16)
         ref["grad_patches"][:, part] = dot(here, top) + dot(here, rest)
     each(width, 256, place_grad)
+    sums["e_out"].join()
+    sums["embed"].join()
+    sums["d_qkv"].pass_on()
+    sums["d_out"].pass_on()
+    sums["vector"].middle()
+    sums["e_down"].last()
     sums["e_qkv"].join()
-    sums["d_down"].pass_on()
-    sums["d_up"].pass_on()
+    sums["vector"].join()
+    sums["e_down"].pass_on()
     sums["e_up"].last()
-    sums["e_down"].pass_on()
-    for name in ("e_out", "d_qkv", "d_out", "embed", "vector"):
-        sums[name].join()
+    sums["e_out"].last()
+    sums["embed"].last()
+    sums["e_up"].pass_on()
     sums["e_qkv"].last()
-    sums["e_up"].pass_on()
-    for name in ("e_out", "d_qkv", "d_out", "embed"):
-        sums[name].last()
+    sums["e_out"].pass_on()
+    sums["embed"].pass_on()
 
     def vector_out(part, whole):
         ref["grad_vector"][part] = whole
     sums["vector"].total(vector_out)
     sums["vector"].drain()
-    for name in ("e_qkv", "e_out", "d_qkv", "d_out", "embed"):
-        sums[name].pass_on()
+    sums["e_qkv"].pass_on()
     for name in MESSAGES:
         sums[name].close()
     last_first.wait_send()
     last_second.wait_send()
     for name in order:
         units[name].drain()
-    for which in range(3):
-        shares(ref["patches"], ref["group"], "p", which).wait_send()
-        shares(ref["cotangent"], ref["cotangents"], "c", which).wait_send()
-        embed_copy(which).wait_send()
+    for gathered in shared.values():
+        gathered.drain()
 
 
 def unpack_kernel(names, *refs):
@@ -1711,10 +1805,10 @@
                 blk, :, owner * size:(owner + 1) * size].astype(F32)
         size = ref["i_e_down"].shape[1]
         ref["e_down"][blk * size:(blk + 1) * size, :] = ref["i_e_down"][blk].astype(F32)
-        for name in ("embed", "d_up"):
+        for name in ("embed", "d_up", "e_out"):
             size = ref["i_" + name].shape[2]
             ref[name][:, part * size:(part + 1) * size] = ref["i_" + name][blk].astype(F32)
-    for name in ROW_UNITS:
+    for name in ROW_SUMS:
         ref[name][...] = ref["i_" + name][...].astype(F32)
 
 
@@ -1743,8 +1837,9 @@
     }
     for name in COLUMN_UNITS:
         shapes[name] = ((PARTS,) + units[name], BF16)
-    for name in ROW_UNITS:
+    for name in ROW_SUMS:
         shapes[name] = (units[name], BF16)
+    shapes["e_out"] = ((PARTS, width // 8, width // PARTS), BF16)
     table = scratch_table(width, dec_width, hidden, dec_hidden, rows, SHOWN)
     names = INPUTS + tuple("o_" + name if name in MESSAGES else name for name in RESULTS)
     names = names + tuple(table) + tuple("s_" + name for name in SEMAPHORES)

time: 258 us -> 246 us (0.953)
  the two profiles are of different devices: /device:TPU:0 before, /device:TPU:21 now
where the time goes in v4:
time: 246 us; the launch traced here: 245 us
  Pallas kernels  245 us (100%)
    pallas_call x1, Pallas kernels, local_kernel(): pl.pallas_call(functools.partial(main_kernel, names), out_shape=[jax.Shap...  239 us
    pallas_call x1, Pallas kernels, local_kernel(): pl.pallas_call(functools.partial(unpack_kernel, tuple(made) + tuple(final...  5.84 us

profile of v4, /device:TPU:21, one launch (start us, length us, event | category | flops | bytes accessed | tf_op | source)
XLA Modules:
  0.0 245.3 jit_solution(12925347996947110363)
XLA Ops:
  0.7 238.7 %shard_map.442 = (bf16[128,512]{1,0:T(8,128)(2,1)}, f32[128,1024]{1,0:T(8,128)}, f32[16,128]{1,0:T(8,128)}, bf16[4,128,768]{2,1,0:T(8,128)(2,1)}, bf16[4,128,102...) custom-call(s32[1,8]{1,0:T(1,128)} %refs_0_.1, ...), custom_call_target="tpu_custom_call" | custom-call | tf_op jit(solution)/shard_map/pallas_call | solution.py:1848
  239.3 5.8 %shard_map.443 = (bf16[128,512]{1,0:T(8,128)(2,1)}, f32[128,1024]{1,0:T(8,128)}, f32[1,128]{1,0:T(1,128)}, f32[1,128]{1,0:T(1,128)}, f32[128,1024]{1,0:T(8,128)}...) custom-call(bf16[128,512]{1,0:T(8,128)(2,1)} %get-tuple-element.60.r, ...), custom_call_target="tpu_custom_call" | custom-call | tf_op jit(solution)/shard_map/pallas_call | solution.py:1878

commit v5 on v4

--- a/solution.py
+++ b/solution.py
@@ -762,6 +762,47 @@
             self.right_copy().wait_send()
 
 
+class GatheredSum(ColumnSum):
+    def gather(self, left, lefts, sems, right):
+        self.left, self.lefts, self.right = left, lefts, right
+        self.l_sent, self.l_got = sems
+        self.count, self.width = lefts.shape[0], lefts.shape[2]
+
+    def columns(self, owner):
+        return self.left.at[:, span(owner * self.width, self.width)]
+
+    def left_copy(self, step):
+        s = self.split
+        owner = lax.rem(s.dp + step, self.count)
+        return remote(self.columns(owner), self.lefts.at[s.dp], self.l_sent, self.l_got,
+                      (owner, s.blk))
+
+    def left_copies(self):
+        blocks = self.lefts.at[pl.ds(0, self.count - 1)]
+        return remote(blocks, blocks, self.l_sent, self.l_got, self.split.y_peer)
+
+    def start_left(self):
+        for step in range(1, self.count):
+            self.left_copy(step).start()
+        self.lefts[self.split.dp] = self.columns(self.split.dp)[...]
+
+    def last(self):
+        s = self.split
+        self.left_copies().wait_recv()
+        zero = jnp.zeros(self.met.shape[1:], F32)
+
+        def one(group, whole):
+            return whole + dot_t(self.lefts[group], self.right(group))
+        whole = lax.fori_loop(0, self.count, one, zero)
+        self.met[s.z] = whole.astype(self.met.dtype)
+        self.b_copy(1).start()
+        self.b_copy(0).start()
+        self.own_copy().start()
+
+    def drain(self):
+        self.left_copies().wait_send()
+
+
 class RowSum:
     def __init__(self, split, grad, met, came, done, sems, step):
         self.split, self.grad, self.met, self.came, self.done = split, grad, met, came, done
@@ -1173,7 +1214,8 @@
 ROW_UNITS = ("e_out", "d_out", "d_down")
 ROW_SUMS = ("d_out", "d_down")
 MESSAGES = COLUMN_UNITS + ROW_UNITS
-TRADED = ("e_qkv", "e_up", "e_down", "e_out", "embed")
+TRADED = ("e_qkv", "e_up", "e_out")
+GATHERED = ("e_down", "embed")
 EARLY = ()
 
 
@@ -1204,8 +1246,11 @@
         if name in TRADED:
             del table["g_" + name]
             table["l_" + name] = ((PARTS, shown, 128), BF16)
-            if name != "embed":
-                table["r_" + name] = ((shown, columns), BF16)
+            table["r_" + name] = ((shown, columns), BF16)
+        if name in GATHERED:
+            del table["g_" + name]
+            del table["c_" + name]
+            table["l_" + name] = ((8, shown, 128), BF16)
     table["w_embed"] = ((width, dec_width), BF16)
     for name in ROW_UNITS:
         height, columns = units[name]
@@ -1265,8 +1310,8 @@
     ):
         table[name] = (shape, kind)
     table["lowered"] = ((shown, width), BF16)
-    table["their_picked"] = ((shown, dec_width), BF16)
-    table["picked"] = ((shown, dec_width), BF16)
+    table["w_picked"] = ((8 * shown, dec_width), BF16)
+    table["right"] = ((shown, width), BF16)
     return table
 
 
@@ -1281,7 +1326,7 @@
 RESULTS = ("decoded", "grad_patches", "grad_vector") + MESSAGES
 SEMAPHORES = {
     "local": (24,),
-    "z_sent": (11,), "z_got": (11, 4), "y_sent": (11,), "y_got": (11, 4),
+    "z_sent": (12,), "z_got": (12, 4), "y_sent": (12,), "y_got": (12, 4),
     "cross_sent": (1,), "cross_got": (1, 4),
     "gy_sent": (11,), "gy_got": (11,), "gz_sent": (11, 3), "gz_got": (11, 4),
     "f_sent": (5, 2), "f_got": (5, 2), "m_sent": (3,), "m_got": (3,), "gb_sent": (11, 4), "gb_got": (11, 3),
@@ -1362,7 +1407,7 @@
         return pltpu.make_async_copy(source, target, sem["local"].at[at])
 
     barrier = pltpu.get_barrier_semaphore()
-    peers = [s.z_peer(step) for step in (1, 2, 3)] + [s.y_peer] + list(s.blk_peers)
+    peers = [(lax.rem(s.dp + step, 8), s.blk) for step in range(1, 8)] + list(s.blk_peers)
     for peer in peers:
         pl.semaphore_signal(barrier, inc=1, device_id=peer, device_id_type=pl.DeviceIdType.MESH)
 
@@ -1424,31 +1469,45 @@
             sem[kind].at[at]
             for kind in ("gy_sent", "gy_got", "gz_sent", "gz_got", "gb_sent", "gb_got")
         )
-        kind = RowSum if name in ROW_SUMS else ProductSum if name in TRADED else ColumnSum
+        kind = ColumnSum
+        for names, other in ((ROW_SUMS, RowSum), (TRADED, ProductSum), (GATHERED, GatheredSum)):
+            if name in names:
+                kind = other
         done = None if name == "vector" else ref["o_" + name]
         wide = ref["m_" + name].shape[-1]
-        sums[name] = kind(s, ref.get("g_" + name), ref["m_" + name], ref["c_" + name], done, sems,
+        sums[name] = kind(s, ref.get("g_" + name), ref["m_" + name], ref.get("c_" + name), done, sems,
                           16 if wide > 512 else 32 if name != "vector" else 8)
-    def their_embed():
-        def body(part):
-            made = dot_b(ref["their_picked"][...], ref["w_embed"][part])
-            ref["r_e_down"][:, part] = made.astype(BF16)
-        each(width, 256, body)
-
-    picked, their_picked = ref["picked"], ref["their_picked"]
+    all_picked = ref["w_picked"]
     embed_columns = span(s.part * (dec_width // PARTS), dec_width // PARTS)
     out_columns = span(s.part * (width // PARTS), width // PARTS)
-    for at, (name, left, right, their_right, more) in enumerate((
-        ("e_qkv", "e_normed", ref["e_grad_qkv"], ref["r_e_qkv"], ()),
-        ("e_up", "e_lifted", ref["e_grad_upper"], ref["r_e_up"], ()),
-        ("e_down", "e_hidden", ref["e_branch"], ref["r_e_down"],
-         (picked, their_picked, their_embed)),
-        ("e_out", "mixture_all", ref["e_branch_b"].at[:, out_columns], ref["r_e_out"], ()),
-        ("embed", "lowered", picked.at[:, embed_columns], their_picked.at[:, embed_columns],
-         (False,)),
+    for at, (name, left, right, their_right) in enumerate((
+        ("e_qkv", "e_normed", ref["e_grad_qkv"], ref["r_e_qkv"]),
+        ("e_up", "e_lifted", ref["e_grad_upper"], ref["r_e_up"]),
+        ("e_out", "mixture_all", ref["e_branch_b"].at[:, out_columns], ref["r_e_out"]),
     )):
         sums[name].trade(ref[left], right, ref["l_" + name], their_right,
-                         (sem["f_sent"].at[at], sem["f_got"].at[at]), *more)
+                         (sem["f_sent"].at[at], sem["f_got"].at[at]))
+
+    def of_group(group):
+        return pl.ds(pl.multiple_of(group * shown, shown), shown)
+
+    def embed_right(group):
+        return all_picked[of_group(group), embed_columns]
+
+    def down_right(group):
+        def body(part):
+            made = dot_b(all_picked[of_group(group)], ref["w_embed"][part])
+            ref["right"][:, part] = made.astype(BF16)
+        each(width, 256, body)
+        return ref["right"][...]
+
+    for at, (name, left, right) in enumerate((
+        ("e_down", "e_hidden", down_right), ("embed", "lowered", embed_right),
+    )):
+        sums[name].gather(ref[left], ref["l_" + name],
+                          (sem["f_sent"].at[3 + at, 0], sem["f_got"].at[3 + at, 0]), right)
+    sems = tuple(sem[kind].at[11] for kind in ("z_sent", "z_got", "y_sent", "y_got"))
+    picked_unit = Columns(s, all_picked, shown, [], sems + (None, None))
 
     totals = []
     for at in range(7):
@@ -1661,14 +1720,12 @@
     sums["d_down"].middle()
     totals[4].begin(decoder.product(ref["d_grad_qkv"], ref["w_d_qkv"], back=True))
     sums["d_up"].middle()
-    last_second.wait_recv()
 
     def last_close(part):
         made = last_part[s.x, s.core, part] + last_met[s.x, part]
         before = ref["d_residual"][pl.ds(pl.multiple_of(s.blk * own + part.start, 64), 64)]
         whole = made + ref["last_came"][part].astype(F32) + before
         ref["decoded"][part] = whole.astype(BF16)
-    each(quarter, 64, last_close)
     decoder.clear_sums()
     weight_grad(ref["d_normed"], ref["d_grad_qkv"], ref["g_d_qkv"])
     sums["d_qkv"].start()
@@ -1678,8 +1735,9 @@
     def decoder_first(at):
         decoder.norm_back(at, True, ref["d_branch_b"])
     totals[4].finish(decoder_first)
+    picked = all_picked.at[of_group(s.dp)]
     picked[...] = dot(places, ref["d_branch_b"][...]).astype(BF16)
-    sums["e_down"].start()
+    picked_unit.send()
     encoder_grad = ref["e_grad"]
 
     def back_embed(part):
@@ -1692,41 +1750,41 @@
     encoder.back_hidden(ref["e_branch"])
     sums["e_up"].start()
     totals[5].begin(encoder.product(ref["e_grad_upper"], ref["w_e_up"], back=True))
-    sums["d_qkv"].middle()
-    sums["d_out"].middle()
-    sums["e_down"].middle()
+    picked_unit.forward((1, 2))
     encoder.clear_sums()
+    sums["e_up"].middle()
 
     def encoder_middle(at):
         encoder.norm_back(at, False, ref["e_branch_b"])
         encoder.back_mixture(ref["e_branch_b"], at * encoder.chunk, encoder.chunk)
     totals[5].finish(encoder_middle)
     sums["e_out"].start()
+    picked_unit.forward((3,))
     sums["d_up"].join()
-    sums["e_up"].middle()
     encoder.attend_back()
     sums["e_qkv"].start()
     totals[6].begin(encoder.product(ref["e_grad_qkv"], ref["w_e_qkv"], back=True))
     sums["d_down"].last()
-    sums["d_qkv"].join()
-    sums["d_out"].join()
     sums["d_up"].last()
     sums["e_out"].middle()
-    sums["embed"].middle()
+    sums["d_qkv"].middle()
+    sums["d_out"].middle()
     vector_store(vector_grad, 2, ref["e_sums"][0:1], True)
     vector_store(vector_grad, 3, ref["e_sums"][1:2], True)
     encoder.clear_sums()
-    sums["e_down"].join()
     sums["e_qkv"].middle()
 
     def encoder_first(at):
         encoder.norm_back(at, True, None)
     totals[6].finish(encoder_first)
     sums["e_up"].join()
+    picked_unit.finish()
+    sums["embed"].last()
+    sums["e_down"].last()
     sums["d_down"].pass_on()
     sums["d_up"].pass_on()
-    sums["d_qkv"].last()
-    sums["d_out"].last()
+    sums["d_qkv"].join()
+    sums["d_out"].join()
     vector_store(vector_grad, 0, ref["e_sums"][0:1], True)
     vector_store(vector_grad, 1, ref["e_sums"][1:2], True)
     vector_store(vector_grad, 5, ref["d_sums"][0:1], False)
@@ -1748,18 +1806,19 @@
         rest = (values - top.astype(F32)).astype(BF16)
         ref["grad_patches"][:, part] = dot(here, top) + dot(here, rest)
     each(width, 256, place_grad)
+    last_second.wait_recv()
+    each(quarter, 64, last_close)
     sums["e_out"].join()
-    sums["embed"].join()
-    sums["d_qkv"].pass_on()
-    sums["d_out"].pass_on()
+    sums["d_qkv"].last()
+    sums["d_out"].last()
     sums["vector"].middle()
-    sums["e_down"].last()
     sums["e_qkv"].join()
     sums["vector"].join()
     sums["e_down"].pass_on()
     sums["e_up"].last()
     sums["e_out"].last()
-    sums["embed"].last()
+    sums["d_qkv"].pass_on()
+    sums["d_out"].pass_on()
     sums["e_up"].pass_on()
     sums["e_qkv"].last()
     sums["e_out"].pass_on()
@@ -1776,6 +1835,7 @@
     last_second.wait_send()
     for name in order:
         units[name].drain()
+    picked_unit.drain()
     for gathered in shared.values():
         gathered.drain()
 

time: 246 us -> 234 us (0.951)
  the two profiles are of different devices: /device:TPU:21 before, /device:TPU:0 now
where the time goes in v5:
time: 234 us
  Pallas kernels  233 us (100%)
    pallas_call x1, Pallas kernels, local_kernel(): pl.pallas_call(functools.partial(main_kernel, names), out_shape=[jax.Shap...  227 us
    pallas_call x1, Pallas kernels, local_kernel(): pl.pallas_call(functools.partial(unpack_kernel, tuple(made) + tuple(final...  5.84 us

profile of v5, /device:TPU:0, one launch (start us, length us, event | category | flops | bytes accessed | tf_op | source)
XLA Modules:
  0.0 233.5 jit_solution(16728384997288667800)
XLA Ops:
  0.7 226.8 %shard_map.442 = (bf16[128,512]{1,0:T(8,128)(2,1)}, f32[128,1024]{1,0:T(8,128)}, f32[16,128]{1,0:T(8,128)}, bf16[4,128,768]{2,1,0:T(8,128)(2,1)}, bf16[4,128,102...) custom-call(s32[1,8]{1,0:T(1,128)} %refs_0_.1, ...), custom_call_target="tpu_custom_call" | custom-call | tf_op jit(solution)/shard_map/pallas_call | solution.py:1908
  227.5 5.8 %shard_map.443 = (bf16[128,512]{1,0:T(8,128)(2,1)}, f32[128,1024]{1,0:T(8,128)}, f32[1,128]{1,0:T(1,128)}, f32[1,128]{1,0:T(1,128)}, f32[128,1024]{1,0:T(8,128)}...) custom-call(bf16[128,512]{1,0:T(8,128)(2,1)} %get-tuple-element.60.r, ...), custom_call_target="tpu_custom_call" | custom-call | tf_op jit(solution)/shard_map/pallas_call | solution.py:1938

commit v6 on v5

--- a/solution.py
+++ b/solution.py
@@ -1274,7 +1274,7 @@
     table["group"] = ((rows, width), BF16)
     table["cotangents"] = ((rows, dec_width), BF16)
     for key, count, wide, deep, heads, size, chunks in (
-        ("e_", shown, width, hidden // 4, 4, 64, 2),
+        ("e_", shown, width, hidden // 4, 4, 64, 1),
         ("d_", rows, dec_width, dec_hidden // 4, 4, 32, 4),
     ):
         share = heads * size
@@ -1332,7 +1332,7 @@
     "f_sent": (5, 2), "f_got": (5, 2), "m_sent": (3,), "m_got": (3,), "gb_sent": (11, 4), "gb_got": (11, 3),
     "p_sent": (3,), "p_got": (3,), "c_sent": (3,), "c_got": (3,),
     "e_sent": (3,), "e_got": (3,), "l_sent": (2,), "l_got": (2,),
-    "e_t_sent": (2, 2, 3), "e_t_got": (2, 2, 3), "d_t_sent": (2, 4, 3), "d_t_got": (2, 4, 3),
+    "e_t_sent": (2, 1, 3), "e_t_got": (2, 1, 3), "d_t_sent": (2, 4, 3), "d_t_got": (2, 4, 3),
 }
 
 
@@ -1746,6 +1746,7 @@
         ref["e_branch"][:, part] = made.astype(BF16)
     each(width, 256, back_embed)
     sums["d_down"].join()
+    sums["d_up"].join()
 
     encoder.back_hidden(ref["e_branch"])
     sums["e_up"].start()
@@ -1760,7 +1761,6 @@
     totals[5].finish(encoder_middle)
     sums["e_out"].start()
     picked_unit.forward((3,))
-    sums["d_up"].join()
     encoder.attend_back()
     sums["e_qkv"].start()
     totals[6].begin(encoder.product(ref["e_grad_qkv"], ref["w_e_qkv"], back=True))

time: 234 us -> 234 us (level)
  no operation moved by 1% of the time
where the time goes in v6:
time: 234 us; the launch traced here: 233 us
  Pallas kernels  233 us (100%)
    pallas_call x1, Pallas kernels, local_kernel(): pl.pallas_call(functools.partial(main_kernel, names), out_shape=[jax.Shap...  227 us
    pallas_call x1, Pallas kernels, local_kernel(): pl.pallas_call(functools.partial(unpack_kernel, tuple(made) + tuple(final...  5.84 us

profile of v6, /device:TPU:0, one launch (start us, length us, event | category | flops | bytes accessed | tf_op | source)
XLA Modules:
  0.0 233.5 jit_solution(278283490465600707)
XLA Ops:
  0.7 226.8 %shard_map.442 = (bf16[128,512]{1,0:T(8,128)(2,1)}, f32[128,1024]{1,0:T(8,128)}, f32[16,128]{1,0:T(8,128)}, bf16[4,128,768]{2,1,0:T(8,128)(2,1)}, bf16[4,128,102...) custom-call(s32[1,8]{1,0:T(1,128)} %refs_0_.1, ...), custom_call_target="tpu_custom_call" | custom-call | tf_op jit(solution)/shard_map/pallas_call | solution.py:1908
  227.5 5.8 %shard_map.443 = (bf16[128,512]{1,0:T(8,128)(2,1)}, f32[128,1024]{1,0:T(8,128)}, f32[1,128]{1,0:T(1,128)}, f32[1,128]{1,0:T(1,128)}, f32[128,1024]{1,0:T(8,128)}...) custom-call(bf16[128,512]{1,0:T(8,128)(2,1)} %get-tuple-element.60.r, ...), custom_call_target="tpu_custom_call" | custom-call | tf_op jit(solution)/shard_map/pallas_call | solution.py:1938
